TPU v7x, 32 devices: a whole 2x2x4 slice. The times are simulated.
32 devices in a mesh: seq: 16 (over z, y, core), tp: 2 (over x).
Axes of the slice: x: 2, y: 2, z: 4, core: 2. Of those that a mesh axis runs over, the one named last changes fastest.
Arguments:
- q_pre: bfloat16 [4096, 7168], P('seq', 'tp')
- k_cache: bfloat16 [4096, 1024], P('seq', 'tp')
- v_cache: bfloat16 [4096, 1024], P('seq', 'tp'), may hold values from -6 to 6
- prompt_lengths: int32 [3], replicated, may hold values from 1 to 3072, 4096 in all
- q_dec: bfloat16 [64, 4, 7168], P(None, None, 'tp')
- k_new: bfloat16 [64, 4, 1024], P(None, None, 'tp')
- v_new: bfloat16 [64, 4, 1024], P(None, None, 'tp'), may hold values from -6 to 6
- block_table: int32 [64, 32], replicated, may hold values from 0 to 63, as said below
- w_out: bfloat16 [7168, 7168], P('tp', 'seq'), may hold values from -0.0625 to 0.0625
Outputs:
- pre_out: bfloat16 [4096, 7168], P('seq', 'tp')
- dec_out: bfloat16 [64, 4, 7168], P('tp', None, 'seq')
Inputs may be any that keep to these rules, and one draw needn't show every extreme that they name: `block_table`: each row names 32 different cache blocks.
All inputs are finite; a program needn't handle non-finite values.
Results may differ from a plain program's by a relative error of at most 0.022.
Values may be sent and summed in bfloat16 or wider, within the bound.
No kernel may reach another device: no remote copies, remote signals or barrier semaphores. Data moves between devices by JAX's collectives and lax.ppermute only.
A program may use at most 128 MiB of HBM per device.

v0:
```python
import functools
import math

import jax
import jax.numpy as jnp
from jax import lax
from jax.experimental import pallas as pl
from jax.experimental.pallas import tpu as pltpu
from jax.sharding import PartitionSpec as P

H = 56
KVH = 8
HD = 128
BLK = 64
SPAN = 512
PAIR = 2
NEG = -1e30
LEAST, MOST = 2.0**-60, 2.0**100
FACTOR = math.log2(math.e) / math.sqrt(HD)
ROOM = 16 * 1024 * 1024
LITTLE = 4 * 1024 * 1024
CORE, CHIP, ACROSS, PARTS, LEVELS = 0, 1, 2, 3, 11
BRIEF = pl.CostEstimate(flops=1024, bytes_accessed=1024, transcendentals=0)
HBM = pl.BlockSpec(memory_space=pltpu.HBM)
VMEM = pl.BlockSpec(memory_space=pltpu.VMEM)
SMEM = pl.BlockSpec(memory_space=pltpu.SMEM)


def dot_nt(a, b):
    return lax.dot_general(a, b, (((1,), (1,)), ((), ())), preferred_element_type=jnp.float32)


def dot_nn(a, b):
    return lax.dot_general(a, b, (((1,), (0,)), ((), ())), preferred_element_type=jnp.float32)


def fold(x, op):
    out = x[:, :HD]
    for i in range(1, x.shape[1] // HD):
        out = op(out, x[:, i * HD : (i + 1) * HD])
    return out


def start_of(position, lengths):
    end = jnp.int32(0)
    out = jnp.zeros_like(position)
    for i in range(lengths.shape[0]):
        end = end + lengths[i]
        out = jnp.where(position >= end, end, out)
    return out


def sound(total):
    return (jnp.min(total) >= LEAST) & (jnp.max(total) <= MOST)


def prefill_kernel(tok, heads, meta, lengths, q, keys_all, values_all, *refs):
    out, qs, peak, total, acc = refs[-5:]
    for j in range(heads):
        qs[j * tok : (j + 1) * tok] = q[:, j * HD : (j + 1) * HD]
    total[...] = jnp.zeros_like(total)
    acc[...] = jnp.zeros_like(acc)

    begin = meta[0]
    finish = begin + tok
    low = start_of(begin, lengths)
    high = start_of(finish - 1, lengths)
    blocks = lax.div(finish - low + SPAN - 1, SPAN)
    clear = lax.div(finish - high, SPAN)

    def first_of(k):
        return jnp.maximum(finish - (k + 1) * SPAN, 0)

    def load(k):
        here = pl.ds(pl.multiple_of(first_of(k), HD), SPAN)
        return keys_all[:, here], values_all[here, :]

    def allowed_in(k):
        t = begin + lax.broadcasted_iota(jnp.int32, (tok, 1), 0)
        u = first_of(k) + lax.broadcasted_iota(jnp.int32, (tok, SPAN), 1)
        last = jnp.minimum(t, finish - k * SPAN - 1)
        return (u <= last) & (u >= start_of(t, lengths))

    def keep(allowed, x, other):
        some = x.shape[0] // tok
        return jnp.where(allowed[None], x.reshape(some, tok, SPAN), other).reshape(x.shape)

    def block(k, masked):
        keys, values = load(k)
        allowed = allowed_in(k) if masked else None
        for j in range(0, heads, PAIR):
            here = slice(j * tok, min(j + PAIR, heads) * tok)
            p = jnp.exp2(dot_nn(qs[here], keys) * FACTOR)
            if masked:
                p = keep(allowed, p, 0.0)
            total[here] += fold(p, jnp.add)
            acc[here] += dot_nn(p.astype(jnp.bfloat16), values)

    block(0, True)

    @pl.loop(1, jnp.maximum(clear, 1))
    def _(k):
        block(k, False)

    @pl.loop(jnp.maximum(clear, 1), blocks)
    def _(k):
        block(k, True)

    def write():
        whole = jnp.sum(total[...], axis=1, keepdims=True)
        result = (acc[...] / whole).astype(out.dtype)
        for j in range(heads):
            out[:, j * HD : (j + 1) * HD] = result[j * tok : (j + 1) * tok]
        return whole

    fine = sound(write())

    @pl.when(jnp.logical_not(fine))
    def _():
        peak[...] = jnp.full_like(peak, NEG)
        total[...] = jnp.zeros_like(total)
        acc[...] = jnp.zeros_like(acc)

        @pl.loop(0, blocks)
        def _(k):
            keys, values = load(k)
            allowed = allowed_in(k)

            @pl.loop(0, heads)
            def _(j):
                here = pl.ds(pl.multiple_of(j * tok, tok), tok)
                s = jnp.where(allowed, dot_nn(qs[here], keys) * FACTOR, NEG)
                top = jnp.maximum(peak[here], jnp.max(s, axis=1, keepdims=True))
                p = jnp.where(allowed, jnp.exp2(s - top[:, :1]), 0.0)
                shrink = jnp.exp2(peak[here] - top)
                total[here] = total[here] * shrink + fold(p, jnp.add)
                acc[here] = acc[here] * shrink + dot_nn(p.astype(jnp.bfloat16), values)
                peak[here] = top

        write()


def prefill(q, keys, values, meta, lengths, groups, columns, name, before=None):
    tok = q.shape[0]
    count = values.shape[0]
    heads = H // KVH
    rows = heads * tok
    pairs = rows * count // 2 * groups
    extra = [] if before is None else [before]
    return pl.pallas_call(
        functools.partial(prefill_kernel, tok, heads),
        out_shape=jax.ShapeDtypeStruct((tok, columns), jnp.bfloat16),
        grid_spec=pltpu.PrefetchScalarGridSpec(
            num_scalar_prefetch=2,
            grid=(groups,),
            in_specs=[
                pl.BlockSpec((tok, heads * HD), lambda g, meta, lengths: (0, meta[1] + g)),
                pl.BlockSpec((HD, count), lambda g, meta, lengths: (meta[2] + g, 0)),
                pl.BlockSpec((count, HD), lambda g, meta, lengths: (0, meta[2] + g)),
            ]
            + [HBM] * len(extra),
            out_specs=pl.BlockSpec((tok, heads * HD), lambda g, meta, lengths: (0, meta[3] + g)),
            scratch_shapes=[
                pltpu.VMEM((rows, HD), jnp.bfloat16),
                pltpu.VMEM((rows, HD), jnp.float32),
                pltpu.VMEM((rows, HD), jnp.float32),
                pltpu.VMEM((rows, HD), jnp.float32),
            ],
        ),
        compiler_params=pltpu.CompilerParams(vmem_limit_bytes=ROOM),
        cost_estimate=pl.CostEstimate(
            flops=pairs * HD * 8, bytes_accessed=count * HD * 4 * groups, transcendentals=pairs
        ),
        input_output_aliases={} if before is None else {5: 0},
        name=name,
    )(meta, lengths, q, keys, values, *extra)


def settle_kernel(meta, piece, whole, out, sem):
    width = piece.shape[1]
    where = pl.ds(pl.multiple_of((1 - meta[CORE]) * width, width), width)
    copy = pltpu.make_async_copy(piece, out.at[:, where], sem)
    copy.start()
    copy.wait()


def settle(whole, piece, meta):
    return pl.pallas_call(
        settle_kernel,
        out_shape=jax.ShapeDtypeStruct(whole.shape, whole.dtype),
        in_specs=[SMEM, VMEM, HBM],
        out_specs=HBM,
        scratch_shapes=[pltpu.SemaphoreType.DMA],
        input_output_aliases={2: 0},
        compiler_params=pltpu.CompilerParams(vmem_limit_bytes=LITTLE),
        cost_estimate=pl.CostEstimate(flops=0, bytes_accessed=piece.size * 4, transcendentals=0),
        name="settle",
    )(meta, piece, whole)


def allowed_at(first, base, tok, length, lengths):
    t = first + lax.broadcasted_iota(jnp.int32, (tok, 1), 0)
    u = base + lax.broadcasted_iota(jnp.int32, (tok, length), 1)
    return (u <= t) & (u >= start_of(t, lengths))


def column_block(at):
    return pl.ds(pl.multiple_of(at, HD), HD)


def keys_of(upper, g):
    return upper[column_block(g * HD), :]


def values_of(lower, g):
    half = lower.shape[1] // 2
    both = [lower[:, column_block(side * half + g * HD)] for side in range(2)]
    return jnp.concatenate(both, axis=0)


def add_block(tok, heads, q_at, keys, values, allowed, sums, fresh=False):
    length = keys.shape[1]
    for j in range(0, heads, PAIR):
        some = min(PAIR, heads - j)
        p = jnp.exp2(dot_nn(q_at(j * tok, some * tok), keys) * FACTOR)
        if allowed is not None:
            p = p.reshape(some, tok, length)
            p = jnp.where(allowed[None], p, 0.0).reshape(some * tok, length)
        more = (fold(p, jnp.add), dot_nn(p.astype(jnp.bfloat16), values))
        for ref, value in zip(sums, more):
            here = slice(j * tok, (j + some) * tok)
            ref[here] = value if fresh else ref[here] + value


def relation(meta, part, side, tok, lengths):
    first = (meta[CHIP] * 2 + side) * tok
    base = meta[PARTS + part] * 2 * tok
    relevant = (base < first) & (meta[PARTS + part] != meta[CHIP])
    relevant = relevant & (base + 2 * tok > start_of(first, lengths))
    return relevant, base >= start_of(first + tok - 1, lengths), first, base


def side_rows(side, heads, tok):
    return pl.ds(pl.multiple_of(side * (heads * tok), HD), heads * tok)


def open_kernel(tok, heads, groups, meta, lengths, q, q_near, upper, lower, qs, total, acc):
    core = meta[CORE]
    rows = heads * tok
    for source, side, skip in ((q, core, core * groups * heads), (q_near, 1 - core, 0)):
        for g in range(groups):
            for j in range(heads):
                at = pl.ds(pl.multiple_of(side * rows + j * tok, HD), tok)
                qs[g, at] = source[:, column_block((skip + g * heads + j) * HD)]

    @pl.loop(0, groups)
    def _(g):
        keys, values = keys_of(upper, g), values_of(lower, g)
        for side in range(2):
            length = (side + 1) * tok
            first = (meta[CHIP] * 2 + side) * tok
            allowed = allowed_at(first, meta[CHIP] * 2 * tok, tok, length, lengths)
            here = side_rows(side, heads, tok)
            q_at = lambda at, count: qs[g, pl.ds(side * rows + at, count)]
            add_block(tok, heads, q_at, keys[:, :length], values[:length], allowed,
                      (total.at[g, here], acc.at[g, here]), True)


def open_sums(q, q_near, block, meta, lengths):
    tok = q.shape[0]
    heads = H // KVH
    groups = q_near.shape[1] // (heads * HD)
    rows = 2 * heads * tok
    sums = jax.ShapeDtypeStruct((groups, rows, HD), jnp.float32)
    pairs = groups * rows * tok * 2
    return pl.pallas_call(
        functools.partial(open_kernel, tok, heads, groups),
        out_shape=[jax.ShapeDtypeStruct((groups, rows, HD), jnp.bfloat16), sums, sums],
        in_specs=[SMEM, SMEM, VMEM, VMEM, VMEM, VMEM],
        out_specs=[VMEM] * 3,
        compiler_params=pltpu.CompilerParams(vmem_limit_bytes=2 * LITTLE),
        cost_estimate=BRIEF,
        name="open",
    )(meta, lengths, q, q_near, *block)


def stage_body(tok, heads, groups, first_part, meta, lengths, qs, before, pair, total, acc, held):
    for i in range(2):
        held[0][i], held[1][i] = pair[2 * i][...], pair[2 * i + 1][...]
    total[...], acc[...] = before[0][...], before[1][...]

    @pl.loop(0, 4 * groups)
    def _(step):
        which, rest = lax.div(step, 2 * groups), lax.rem(step, 2 * groups)
        g, side = lax.div(rest, 2), lax.rem(rest, 2)
        relevant, clear, first, base = relation(meta, first_part + which, side, tok, lengths)
        here = side_rows(side, heads, tok)
        sums = (total.at[g, here], acc.at[g, here])
        at = side * (heads * tok)
        q_at = lambda off, count: qs[g, pl.ds(pl.multiple_of(at + off, HD), count)]
        upper, lower = held[0].at[which], held[1].at[which]

        @pl.when(relevant & clear)
        def _():
            add_block(tok, heads, q_at, keys_of(upper, g), values_of(lower, g), None, sums)

        @pl.when(relevant & jnp.logical_not(clear))
        def _():
            allowed = allowed_at(first, base, tok, 2 * tok, lengths)
            add_block(tok, heads, q_at, keys_of(upper, g), values_of(lower, g), allowed, sums)


def stage_kernel(tok, heads, groups, first_part, own, *refs):
    meta, lengths, qs, total_in, acc_in = refs[:5]
    pair = refs[5:9]
    if own is None:
        total, acc, *held = refs[9:]
    else:
        sources, table = refs[9:12], refs[12]
        total, acc, state, held = refs[13], refs[14], refs[15:21], refs[21:23]
        q3, k3, v3, sems = refs[23:]
        copies = request_copies(own, meta, sources, (q3, k3, v3), sems)
        for copy in copies:
            copy.start()
    before = (total_in, acc_in)
    stage_body(tok, heads, groups, first_part, meta, lengths, qs, before, pair, total, acc, held)
    if own is not None:
        for copy in copies:
            copy.wait()
        requests_body(own, heads, groups, 2 * tok, meta, table, *state, q3, k3, v3)


def stage(state, pair, first_part, meta, lengths, requests=None):
    qs, total, acc = state
    groups, rows, unused = qs.shape
    flat = [x for block in pair for x in block]
    tok = flat[0].shape[1] // 2
    heads = rows // (2 * tok)
    out_shape = [jax.ShapeDtypeStruct(x.shape, x.dtype) for x in (total, acc)]
    scratch = [pltpu.VMEM((2, *x.shape), x.dtype) for x in pair[0]]
    sources, own = [], None
    if requests is not None:
        *sources, own = requests
        steps = sources[0].shape[1]
        width = sources[1].shape[2] // 2
        size = heads * own * steps
        sums = jax.ShapeDtypeStruct((groups, size, HD), jnp.float32)
        new = jax.ShapeDtypeStruct((own * steps, width), jnp.bfloat16)
        out_shape += [
            sums, sums, jax.ShapeDtypeStruct((groups, size, HD), jnp.bfloat16), new, new,
            jax.ShapeDtypeStruct((own, (LEVELS - PARTS) * 2 * tok), jnp.float32),
        ]
        scratch += [
            pltpu.VMEM((own, steps, groups * heads * HD), jnp.bfloat16),
            pltpu.VMEM((own, steps, width), jnp.bfloat16),
            pltpu.VMEM((own, steps, width), jnp.bfloat16),
            pltpu.SemaphoreType.DMA((3,)),
        ]
    new = pl.pallas_call(
        functools.partial(stage_kernel, tok, heads, groups, first_part, own),
        out_shape=out_shape,
        in_specs=[SMEM, SMEM] + [VMEM] * 7 + ([HBM] * 3 + [VMEM] if sources else []),
        out_specs=[VMEM] * len(out_shape),
        scratch_shapes=scratch,
        input_output_aliases={3: 0, 4: 1},
        compiler_params=pltpu.CompilerParams(vmem_limit_bytes=ROOM),
        cost_estimate=BRIEF,
        name=f"stage{first_part}",
    )(meta, lengths, qs, total, acc, *flat, *sources)
    return (qs, *new[:2]), new[2:]


def finish_kernel(tok, heads, groups, done, meta, lengths, qs, total, acc, *refs):
    near, out, held_k, held_v, peak, total_now, acc_now, result, sem = refs[-9:]
    parts = held_k.shape[0]
    rows = heads * tok
    core = meta[CORE]

    def fill(first):
        for i in range(first, parts):
            held_k[i], held_v[i] = refs[2 * i][...], refs[2 * i + 1][...]

    def turn_of(step):
        turn, g = lax.div(step, groups), lax.rem(step, groups)
        side = jnp.where(turn == 0, 1 - core, core)
        at = side * rows
        q_at = lambda off, count: qs[g, pl.ds(pl.multiple_of(at + off, HD), count)]
        return turn, g, side, q_at

    def write(turn, g):
        whole = jnp.sum(total_now[...], axis=1, keepdims=True)
        value = (acc_now[...] / whole).astype(result.dtype)
        for j in range(heads):
            result[turn, :, column_block((g * heads + j) * HD)] = value[j * tok : (j + 1) * tok]
        return sound(whole)

    def one_turn(step, fine):
        turn, g, side, q_at = turn_of(step)
        here = side_rows(side, heads, tok)
        total_now[...] = total[g, here]
        acc_now[...] = acc[g, here]

        @pl.loop(done, parts)
        def _(i):
            relevant, clear, first, base = relation(meta, i, side, tok, lengths)
            upper, lower = held_k.at[i], held_v.at[i]
            sums = (total_now, acc_now)

            @pl.when(relevant & clear)
            def _():
                add_block(tok, heads, q_at, keys_of(upper, g), values_of(lower, g), None, sums)

            @pl.when(relevant & jnp.logical_not(clear))
            def _():
                allowed = allowed_at(first, base, tok, 2 * tok, lengths)
                add_block(tok, heads, q_at, keys_of(upper, g), values_of(lower, g), allowed, sums)

        return fine & write(turn, g).astype(jnp.int32)

    fill(done)
    fine = lax.fori_loop(0, 2 * groups, one_turn, jnp.int32(1))

    @pl.when(fine == 0)
    def _():
        fill(0)

        @pl.loop(0, 2 * groups)
        def _(step):
            turn, g, side, q_at = turn_of(step)
            first = (meta[CHIP] * 2 + side) * tok
            peak[...] = jnp.full_like(peak, NEG)
            total_now[...] = jnp.zeros_like(total_now)
            acc_now[...] = jnp.zeros_like(acc_now)

            @pl.loop(0, parts * heads)
            def _(step):
                i, j = lax.div(step, heads), lax.rem(step, heads)
                keys, values = keys_of(held_k.at[i], g), values_of(held_v.at[i], g)
                allowed = allowed_at(first, meta[PARTS + i] * 2 * tok, tok, 2 * tok, lengths)
                mine = pl.ds(pl.multiple_of(j * tok, tok), tok)
                s = jnp.where(allowed, dot_nn(q_at(j * tok, tok), keys) * FACTOR, NEG)
                top = jnp.maximum(peak[mine], jnp.max(s, axis=1, keepdims=True))
                p = jnp.where(allowed, jnp.exp2(s - top[:, :1]), 0.0)
                shrink = jnp.exp2(peak[mine] - top)
                total_now[mine] = total_now[mine] * shrink + fold(p, jnp.add)
                acc_now[mine] = acc_now[mine] * shrink + dot_nn(p.astype(jnp.bfloat16), values)
                peak[mine] = top

            write(turn, g)

    width = near.shape[1]
    where = pl.ds(pl.multiple_of(core * width, width), width)
    copy = pltpu.make_async_copy(result.at[1], out.at[:, where], sem)
    copy.start()
    near[...] = result[0]
    copy.wait()


def finish(state, blocks, done, meta, lengths):
    qs, total, acc = state
    groups, rows, unused = qs.shape
    flat = [x for block in blocks for x in block]
    tok = flat[0].shape[1] // 2
    heads = rows // (2 * tok)
    width = groups * heads * HD
    sums = pltpu.VMEM((heads * tok, HD), jnp.float32)
    return pl.pallas_call(
        functools.partial(finish_kernel, tok, heads, groups, done),
        out_shape=[
            jax.ShapeDtypeStruct((tok, width), jnp.bfloat16),
            jax.ShapeDtypeStruct((tok, 2 * width), jnp.bfloat16),
        ],
        in_specs=[SMEM, SMEM] + [VMEM] * (3 + len(flat)),
        out_specs=[VMEM, HBM],
        scratch_shapes=[
            *[pltpu.VMEM((len(blocks), *x.shape), x.dtype) for x in blocks[0]],
            sums, sums, sums,
            pltpu.VMEM((2, tok, width), jnp.bfloat16),
            pltpu.SemaphoreType.DMA,
        ],
        compiler_params=pltpu.CompilerParams(vmem_limit_bytes=ROOM),
        cost_estimate=pl.CostEstimate(
            flops=groups * rows * tok * HD * 8, bytes_accessed=tok * width * 4,
            transcendentals=groups * rows * tok * 2,
        ),
        name="finish",
    )(meta, lengths, qs, total, acc, *flat)


def request_sums(query, keys, values, mask):
    p = jnp.exp2(dot_nn(query, keys) * FACTOR)
    p = jnp.where(mask[None], p.reshape(-1, *mask.shape), 0.0).reshape(p.shape)
    return fold(p, jnp.add), dot_nn(p.astype(jnp.bfloat16), values)


def fresh_scores(query, newk, own):
    s = dot_nt(query, newk) * FACTOR
    size = newk.shape[0]
    row = lax.broadcasted_iota(jnp.int32, (size, size), 0)
    col = lax.broadcasted_iota(jnp.int32, (size, size), 1)
    ok = (lax.rem(row, own) == lax.rem(col, own)) & (lax.div(col, own) <= lax.div(row, own))
    return s.reshape(-1, size, size), ok


def request_copies(own, meta, sources, held, sems):
    requests = pl.ds(lax.div(meta[CHIP], 2) * own, own)
    copies = []
    for i, (source, target) in enumerate(zip(sources, held)):
        width = target.shape[2]
        where = pl.ds(pl.multiple_of(meta[CORE] * width, width), width)
        copies.append(pltpu.make_async_copy(source.at[requests, :, where], target, sems.at[i]))
    return copies


def requests_body(own, heads, groups, length, meta, table, total, acc, query, newk, newv, mask, q3, k3, v3):
    steps = q3.shape[1]
    level = lax.div(meta[CHIP], 2)
    pick = lax.broadcasted_iota(jnp.int32, (own, table.shape[1]), 1) - level * own
    pick = (pick == lax.broadcasted_iota(jnp.int32, pick.shape, 0)).astype(jnp.float32)
    rows = dot_nt(pick.astype(jnp.bfloat16), table[...].astype(jnp.float32).astype(jnp.bfloat16))
    lane = lax.div(lax.broadcasted_iota(jnp.int32, (own, length), 1), BLK)
    for i in range(mask.shape[1] // length):
        number = (lane + meta[PARTS + i] * (length // BLK)).astype(jnp.float32)
        hit = rows[:, :1] == number
        for j in range(1, rows.shape[1]):
            hit = hit | (rows[:, j : j + 1] == number)
        mask[:, i * length : (i + 1) * length] = hit.astype(jnp.float32)
    for s in range(steps):
        for g in range(groups):
            col = slice(g * HD, (g + 1) * HD)
            at = slice(s * own, (s + 1) * own)
            newk[at, col] = k3[:, s, col]
            newv[at, col] = v3[:, s, col]
            for j in range(heads):
                first = (g * heads + j) * HD
                row = (j * steps + s) * own
                query[g, row : row + own] = q3[:, s, first : first + HD]

    @pl.loop(0, groups)
    def _(g):
        col = column_block(g * HD)
        s, ok = fresh_scores(query[g], newk[:, col], own)
        p = jnp.where(ok[None], jnp.exp2(s), 0.0).reshape(-1, s.shape[2])
        first = jnp.sum(p, axis=1, keepdims=True)
        lead = lax.broadcasted_iota(jnp.int32, (p.shape[0], HD), 1) == 0
        total[g] = jnp.where(lead, first, 0.0)
        acc[g] = dot_nn(p.astype(jnp.bfloat16), newv[:, col])


def early_kernel(groups, total_in, acc_in, query, mask, *refs):
    total, acc = refs[-2:]
    length = refs[0].shape[1]

    @pl.loop(0, groups)
    def _(g):
        sums = [total_in[g], acc_in[g]]
        for i in range(len(refs) // 2 - 1):
            open_to = mask[:, i * length : (i + 1) * length] > 0
            keys, values = keys_of(refs[2 * i], g), values_of(refs[2 * i + 1], g)
            more = request_sums(query[g], keys, values, open_to)
            sums = [x + y for x, y in zip(sums, more)]
        total[g], acc[g] = sums


def early_decode(state, blocks):
    total, acc, query, newk, newv, mask = state
    groups, rows, unused = query.shape
    flat = [x for block in blocks for x in block]
    sums = jax.ShapeDtypeStruct(total.shape, total.dtype)
    new = pl.pallas_call(
        functools.partial(early_kernel, groups),
        out_shape=[sums, sums],
        in_specs=[VMEM] * (4 + len(flat)),
        out_specs=[VMEM] * 2,
        input_output_aliases={0: 0, 1: 1},
        compiler_params=pltpu.CompilerParams(vmem_limit_bytes=2 * LITTLE),
        cost_estimate=BRIEF,
        name="early_decode",
    )(total, acc, query, mask, *flat)
    return [*new, query, newk, newv, mask]


def late_kernel(own, steps, heads, groups, done, meta, total, acc, query, newk, newv, mask, *refs):
    parts, out = len(refs) // 2, refs[-1]
    length = refs[0].shape[1]
    size = own * steps

    def write(g, sums, whole):
        result = (sums / whole).astype(out.dtype)
        for j in range(heads):
            out[:, column_block((g * heads + j) * HD)] = result[j * size : (j + 1) * size]

    def one_group(g, fine):
        sums = [total[g], acc[g]]
        for i in range(done, parts):
            open_to = mask[:, i * length : (i + 1) * length] > 0
            keys, values = keys_of(refs[2 * i], g), values_of(refs[2 * i + 1], g)
            more = request_sums(query[g], keys, values, open_to)
            sums = [x + y for x, y in zip(sums, more)]
        whole = jnp.sum(sums[0], axis=1, keepdims=True)
        write(g, sums[1], whole)
        return fine & sound(whole).astype(jnp.int32)

    fine = lax.fori_loop(0, groups, one_group, jnp.int32(1))

    @pl.when(fine == 0)
    def _():
        @pl.loop(0, groups)
        def _(g):
            col = column_block(g * HD)
            fresh, ok = fresh_scores(query[g], newk[:, col], own)
            fresh = jnp.where(ok[None], fresh, NEG).reshape(-1, size)
            top = jnp.max(fresh, axis=1, keepdims=True)
            p = jnp.exp2(fresh - top)
            whole = jnp.sum(p, axis=1, keepdims=True)
            sums = dot_nn(p.astype(jnp.bfloat16), newv[:, col])
            for i in range(parts):
                s = dot_nn(query[g], keys_of(refs[2 * i], g)) * FACTOR
                open_to = mask[:, i * length : (i + 1) * length] > 0
                s = jnp.where(open_to[None], s.reshape(-1, own, length), NEG).reshape(s.shape)
                higher = jnp.maximum(top, jnp.max(s, axis=1, keepdims=True))
                p = jnp.exp2(s - higher)
                shrink = jnp.exp2(top - higher)
                whole = whole * shrink + jnp.sum(p, axis=1, keepdims=True)
                sums = sums * shrink + dot_nn(p.astype(jnp.bfloat16), values_of(refs[2 * i + 1], g))
                top = higher
            write(g, sums, whole)


def late_decode(early, blocks, done, own, steps, meta):
    groups, rows, unused = early[0].shape
    heads = H // KVH
    flat = [x for block in blocks for x in block]
    parts, length = len(blocks), flat[0].shape[1]
    pairs = groups * rows * (parts - done) * length
    return pl.pallas_call(
        functools.partial(late_kernel, own, steps, heads, groups, done),
        out_shape=jax.ShapeDtypeStruct((own * steps, groups * heads * HD), jnp.bfloat16),
        in_specs=[SMEM] + [VMEM] * (len(early) + len(flat)),
        out_specs=VMEM,
        compiler_params=pltpu.CompilerParams(vmem_limit_bytes=ROOM),
        cost_estimate=pl.CostEstimate(
            flops=pairs * HD * 8, bytes_accessed=rows * HD, transcendentals=pairs
        ),
        name="late_decode",
    )(meta, *early, *flat)


def decode_kernel(parts, steps, heads, groups, starts, q, mask, newk, newv, *refs):
    kheld, vheld = refs[:parts], refs[parts : 2 * parts]
    out, kall, vall, sems, scores = refs[2 * parts :]
    own = q.shape[0]
    rows = heads * own
    length = kheld[0].shape[1]
    copies = []
    for i in range(parts):
        where = pl.ds(pl.multiple_of(starts[i], HD), length)
        copies.append(pltpu.make_async_copy(kheld[i], kall.at[:, where], sems.at[2 * i]))
        copies.append(pltpu.make_async_copy(vheld[i], vall.at[where], sems.at[2 * i + 1]))
    for copy in copies:
        copy.start()
    row = lax.broadcasted_iota(jnp.int32, (own, own), 0)
    col = lax.broadcasted_iota(jnp.int32, (own, own), 1)
    fresh_ok = (lax.div(row, steps) == lax.div(col, steps)) & (col <= row)

    def columns(g):
        return slice(g * HD, (g + 1) * HD)

    def stacked(g):
        first = g * heads
        slices = [q[:, (first + j) * HD : (first + j + 1) * HD] for j in range(heads)]
        return jnp.concatenate([x.astype(jnp.float32) for x in slices], 0).astype(jnp.bfloat16)

    def keep(allowed, x, other):
        y = x.reshape(heads, own, x.shape[1])
        return jnp.where(allowed[None], y, other).reshape(x.shape)

    def open_to(i):
        return mask[:, pl.ds(pl.multiple_of(starts[i], HD), length)] > 0

    def write(g, acc, whole):
        result = acc / whole
        for j in range(heads):
            out[:, (g * heads + j) * HD : (g * heads + j + 1) * HD] = result[
                j * own : (j + 1) * own
            ].astype(out.dtype)

    fine = None
    for g in range(groups):
        query = stacked(g)
        p = keep(fresh_ok, jnp.exp2(dot_nt(query, newk[:, columns(g)]) * FACTOR), 0.0)
        whole = jnp.sum(p, axis=1, keepdims=True)
        acc = dot_nn(p.astype(jnp.bfloat16), newv[:, columns(g)])
        total = jnp.zeros((rows, HD), jnp.float32)
        for i in range(parts):
            p = jnp.exp2(dot_nn(query, kheld[i][columns(g)]) * FACTOR)
            p = keep(open_to(i), p, 0.0)
            total = total + fold(p, jnp.add)
            acc = acc + dot_nn(p.astype(jnp.bfloat16), vheld[i][:, columns(g)])
        whole = whole + jnp.sum(total, axis=1, keepdims=True)
        write(g, acc, whole)
        fine = sound(whole) if fine is None else fine & sound(whole)

    @pl.when(jnp.logical_not(fine))
    def _():
        for g in range(groups):
            query = stacked(g)
            fresh = keep(fresh_ok, dot_nt(query, newk[:, columns(g)]) * FACTOR, NEG)
            top = jnp.max(fresh, axis=1, keepdims=True)
            for i in range(parts):
                s = keep(open_to(i), dot_nn(query, kheld[i][columns(g)]) * FACTOR, NEG)
                scores[:, i * length : (i + 1) * length] = s
                top = jnp.maximum(top, jnp.max(s, axis=1, keepdims=True))
            p = jnp.exp2(fresh - top)
            whole = jnp.sum(p, axis=1, keepdims=True)
            acc = dot_nn(p.astype(jnp.bfloat16), newv[:, columns(g)])
            for i in range(parts):
                p = jnp.exp2(scores[:, i * length : (i + 1) * length] - top)
                whole = whole + jnp.sum(p, axis=1, keepdims=True)
                acc = acc + dot_nn(p.astype(jnp.bfloat16), vheld[i][:, columns(g)])
            write(g, acc, whole)

    for copy in copies:
        copy.wait()


def decode(q, mask, newk, newv, kparts, vparts, starts, steps):
    own = q.shape[0]
    parts = len(kparts)
    length, width = vparts[0].shape
    count = parts * length
    heads = H // KVH
    groups = width // HD
    rows = heads * own
    pairs = groups * rows * count
    return pl.pallas_call(
        functools.partial(decode_kernel, parts, steps, heads, groups),
        out_shape=[
            jax.ShapeDtypeStruct(q.shape, jnp.bfloat16),
            jax.ShapeDtypeStruct((width, count), jnp.bfloat16),
            jax.ShapeDtypeStruct((count, width), jnp.bfloat16),
        ],
        grid_spec=pltpu.PrefetchScalarGridSpec(
            num_scalar_prefetch=1,
            grid=(),
            in_specs=[VMEM] * (4 + 2 * parts),
            out_specs=[VMEM, HBM, HBM],
            scratch_shapes=[
                pltpu.SemaphoreType.DMA((2 * parts,)),
                pltpu.VMEM((rows, count), jnp.float32),
            ],
        ),
        compiler_params=pltpu.CompilerParams(vmem_limit_bytes=ROOM),
        cost_estimate=pl.CostEstimate(
            flops=pairs * HD * 4, bytes_accessed=count * width * 4, transcendentals=pairs
        ),
        name="decode",
    )(starts, q, mask, newk, newv, *kparts, *vparts)


def prepare_kernel(meta, k, v, send, keys, values):
    width = k.shape[1] // 2
    mine = pl.ds(pl.multiple_of(meta[0] * width, width), width)
    other = pl.ds(pl.multiple_of((1 - meta[0]) * width, width), width)
    send[:width] = k[:, other].astype(jnp.float32).T.astype(send.dtype)
    send[width:] = v[:, other]
    keys[:, mine] = k[:, mine].astype(jnp.float32).T.astype(keys.dtype)
    values[:, mine] = v[:, mine]


def prepare(k, v, core):
    tok, width = k.shape[0], k.shape[1] // 2
    assert tok == width
    block = jax.ShapeDtypeStruct((width, 2 * tok), k.dtype)
    return pl.pallas_call(
        prepare_kernel,
        out_shape=[jax.ShapeDtypeStruct((2 * tok, width), k.dtype), block, block],
        in_specs=[SMEM, VMEM, VMEM],
        out_specs=[VMEM] * 3,
        compiler_params=pltpu.CompilerParams(vmem_limit_bytes=LITTLE),
        name="prepare",
    )(core[None], k, v)


def join_kernel(meta, keys_in, values_in, theirs, q, keys, values, send_q, sem):
    columns = send_q.shape[1]
    where = pl.ds(pl.multiple_of((1 - meta[0]) * columns, columns), columns)
    copy = pltpu.make_async_copy(q.at[:, where], send_q, sem)
    copy.start()
    width = theirs.shape[1]
    other = pl.ds(pl.multiple_of((1 - meta[0]) * width, width), width)
    keys[...], values[...] = keys_in[...], values_in[...]
    keys[:, other] = theirs[:width]
    values[:, other] = theirs[width:]
    copy.wait()


def join(keys, values, theirs, q, core):
    return pl.pallas_call(
        join_kernel,
        out_shape=[
            jax.ShapeDtypeStruct(keys.shape, keys.dtype),
            jax.ShapeDtypeStruct(values.shape, values.dtype),
            jax.ShapeDtypeStruct((q.shape[0], q.shape[1] // 2), q.dtype),
        ],
        in_specs=[SMEM, VMEM, VMEM, VMEM, HBM],
        out_specs=[VMEM] * 3,
        scratch_shapes=[pltpu.SemaphoreType.DMA],
        compiler_params=pltpu.CompilerParams(vmem_limit_bytes=LITTLE),
        name="join",
    )(core[None], keys, values, theirs, q)


def take_kernel(meta, whole, out, sem):
    width = out.shape[1]
    where = pl.ds(pl.multiple_of((1 - meta[CORE]) * width, width), width)
    copy = pltpu.make_async_copy(whole.at[:, where], out, sem)
    copy.start()
    copy.wait()


def take_other_half(whole, meta):
    return pl.pallas_call(
        take_kernel,
        out_shape=jax.ShapeDtypeStruct((whole.shape[0], whole.shape[1] // 2), whole.dtype),
        in_specs=[SMEM, HBM],
        out_specs=VMEM,
        scratch_shapes=[pltpu.SemaphoreType.DMA],
        compiler_params=pltpu.CompilerParams(vmem_limit_bytes=LITTLE),
        name="take",
    )(meta, whole)


def project_kernel(meta, *refs):
    pieces, (whole, other), outs, (sorted_rows,) = refs[:-7], refs[-7:-5], refs[-5:-1], refs[-1:]
    parts = len(pieces)
    rows = pieces[0].shape[0]
    for i, piece in enumerate(pieces):
        at = pl.ds(pl.multiple_of(meta[LEVELS + i] * rows, rows), rows)
        sorted_rows[at] = piece[...]
    depth = other.shape[1]
    mine = whole[:, pl.ds(pl.multiple_of(meta[CORE] * depth, depth), depth)]
    half = parts * rows // 2
    here = pl.ds(pl.multiple_of(meta[ACROSS] * half, half), half)
    there = pl.ds(pl.multiple_of((1 - meta[ACROSS]) * half, half), half)
    kept, beside, across, corner = outs
    for at, near, far in ((here, kept, beside), (there, across, corner)):
        some = sorted_rows[at]
        near[...] = dot_nt(mine, some).astype(near.dtype)
        far[...] = dot_nt(other[...], some).astype(far.dtype)


def project(pieces, whole, other, meta):
    rows = len(pieces) * pieces[0].shape[0]
    width, depth = other.shape
    block = jax.ShapeDtypeStruct((width, rows // 2), jnp.bfloat16)
    return pl.pallas_call(
        project_kernel,
        out_shape=[jax.ShapeDtypeStruct(block.shape, jnp.float32)] + [block] * 3,
        in_specs=[SMEM] + [VMEM] * (len(pieces) + 2),
        out_specs=[VMEM] * 4,
        scratch_shapes=[pltpu.VMEM((rows, depth), jnp.bfloat16)],
        compiler_params=pltpu.CompilerParams(vmem_limit_bytes=2 * LITTLE),
        cost_estimate=pl.CostEstimate(
            flops=rows * width * depth * 4, bytes_accessed=width * depth * 4, transcendentals=0
        ),
        name="project",
    )(meta, *pieces, whole, other)


def index(z, y, c):
    return (z * 2 + y) * 2 + c


def on_ring(r, chips):
    return (r, 0) if r < chips // 2 else (chips - 1 - r, 1)


def ring_perm(chips, d):
    return [
        (index(*on_ring(r, chips), c), index(*on_ring((r + d) % chips, chips), c))
        for r in range(chips)
        for c in range(2)
    ]


def ring_place(r, chips):
    r = lax.rem(r + 2 * chips, chips)
    return jnp.where(r < chips // 2, r * 2, (chips - 1 - r) * 2 + 1)


def spread(x, n):
    place = lax.axis_index("seq")
    deep = n // 4
    everyone = [(z, y, c) for z in range(deep) for y in range(2) for c in range(2)]
    z, y, c = place // 4, (place // 2) % 2, place % 2
    held = [(x, z, y, c)]
    for d in range(1, deep):
        perm = [(index(*p), index((p[0] - d) % deep, p[1], p[2])) for p in everyone]
        held.append((lax.ppermute(x, "seq", perm), lax.rem(z + d, deep), y, c))
    perm = [(index(*p), index(p[0], 1 - p[1], p[2])) for p in everyone]
    held += [(lax.ppermute(b, "seq", perm), bz, 1 - by, bc) for b, bz, by, bc in held]
    perm = [(index(*p), index(p[0], p[1], 1 - p[2])) for p in everyone]
    held += [(lax.ppermute(b, "seq", perm), bz, by, 1 - bc) for b, bz, by, bc in held]
    return [b for b, *_ in held], jnp.stack([index(bz, by, bc) for _, bz, by, bc in held])


def open_blocks(table, steps, count):
    number = lax.broadcasted_iota(jnp.int32, (*table.shape, count), 2) // BLK
    mask = jnp.any(table[:, :, None] == number, axis=1).astype(jnp.float32)
    return jnp.repeat(mask, steps, axis=0)


def whole_heads(n, q_pre, k_cache, v_cache, lengths, q_dec, k_new, v_new, block_table, w_out):
    tok = q_pre.shape[0]
    place = lax.axis_index("seq").astype(jnp.int32)
    rows, steps = q_dec.shape[0], q_dec.shape[1]
    own = rows // n
    kparts, sources = spread(k_cache.T, n)
    vparts, _ = spread(v_cache, n)
    starts = sources.astype(jnp.int32) * tok

    def mine(x):
        y = lax.dynamic_slice_in_dim(x, place * own, own, 0)
        return y.reshape(own * steps, -1) if x.ndim == 3 else y

    mask = open_blocks(mine(block_table), steps, n * tok)
    attn_own, keys, values = decode(
        mine(q_dec), mask, mine(k_new), mine(v_new), kparts, vparts, starts, steps
    )
    attn = lax.all_gather(attn_own, "seq", axis=0, tiled=True)
    flat = jnp.dot(attn, w_out, preferred_element_type=jnp.float32).astype(jnp.bfloat16)
    dec_out = lax.psum_scatter(
        flat.reshape(rows, steps, -1), "tp", scatter_dimension=0, tiled=True
    )
    zero = jnp.zeros((), jnp.int32)
    meta = jnp.stack([place * tok, zero, zero, zero])
    groups = k_cache.shape[1] // HD
    pre_out = prefill(
        q_pre, keys, values, meta, lengths, groups, q_pre.shape[1], "prefill"
    )
    return (pre_out, dec_out)


def split_heads(n, q_pre, k_cache, v_cache, lengths, q_dec, k_new, v_new, block_table, w_out):
    place = lax.axis_index("seq").astype(jnp.int32)
    across = lax.axis_index("tp").astype(jnp.int32)
    core, chip = lax.rem(place, 2), lax.div(place, 2)
    chips = n // 2
    far, deep = chips // 2, chips // 2
    z, y = lax.div(chip, 2), lax.rem(chip, 2)
    r = jnp.where(y == 0, z, chips - 1 - z)
    rows, steps = q_dec.shape[0], q_dec.shape[1]
    own = rows // deep
    sibling = [(i, i ^ 1) for i in range(n)]
    everyone = [(a, b, c) for a in range(deep) for b in range(2) for c in range(2)]

    order = [0] + [o for d in range(1, far) for o in (-d, d)] + [far]
    numbers = [ring_place(r + o, chips) for o in order]
    levels = [z] + [lax.rem(z + deep - d, deep) for d in range(1, deep)]
    assert len(numbers) == LEVELS - PARTS
    meta = jnp.stack([core, chip, across] + numbers + levels).astype(jnp.int32)

    send, keys, values = prepare(k_cache, v_cache, core)
    theirs = lax.ppermute(send, "seq", sibling)
    theirs, meta = lax.optimization_barrier((theirs, meta))
    held_k, held_v = {}, {}
    held_k[0], held_v[0], send_q = join(keys, values, theirs, q_pre, core)
    near_q = lax.ppermute(send_q, "seq", sibling)

    up, down = ring_perm(chips, 1), ring_perm(chips, -1)
    early, w_near = (), w_out
    for d in range(1, far + 1):
        held_k[-d] = lax.ppermute(held_k[1 - d], "seq", up)
        held_v[d] = lax.ppermute(held_v[d - 1], "seq", down)
        if d < far:
            held_k[d] = lax.ppermute(held_k[d - 1], "seq", down)
            held_v[-d] = lax.ppermute(held_v[1 - d], "seq", up)
            sides = (-d, d)
        else:
            held_k[d] = held_k[-d]
            sides = (d,)
        if d == 1:
            state = open_sums(q_pre, near_q, (held_k[0], held_v[0]), meta, lengths)
        elif d < far:
            requests = (q_dec, k_new, v_new, block_table.T, own) if d == 2 else None
            pair = [(held_k[o], held_v[o]) for o in (1 - d, d - 1)]
            state, more = stage(state, pair, 2 * d - 3, meta, lengths, requests)
            early = early or more
        else:
            blocks = [(held_k[o], held_v[o]) for o in order[:-1]]
            early = early_decode(early, blocks)
        for x in (held_k, held_v):
            moved, state, early = lax.optimization_barrier(([x[o] for o in sides], state, early))
            x.update(zip(sides, moved))
        if d == 3:
            w_near, state = lax.optimization_barrier((w_near, state))
            weights = w_near.T
            w_near = lax.ppermute(take_other_half(weights, meta), "seq", sibling)
    w_near, early = lax.optimization_barrier((w_near, early))
    blocks = [(held_k[o], held_v[o]) for o in order]
    attn_own = late_decode(early, blocks, len(blocks) - 1, own, steps, meta)

    pieces = [attn_own]
    for d in range(1, deep):
        perm = [(index(*p), index((p[0] + d) % deep, p[1], p[2])) for p in everyone]
        pieces.append(lax.ppermute(attn_own, "seq", perm))
    attn_own, state = lax.optimization_barrier((attn_own, state))
    near, pre_out = finish(state, blocks, 2 * far - 3, meta, lengths)
    pieces, near, pre_out = lax.optimization_barrier((pieces, near, pre_out))
    back = lax.ppermute(near, "seq", sibling)
    pre_out = settle(pre_out, back, meta)

    total, *sent = project(pieces, weights, w_near, meta)
    got = []
    for piece, (dc, dx) in zip(sent, ((1, 0), (0, 1), (1, 1))):
        perm = [
            (i * 2 + x, (i ^ dc) * 2 + (x ^ dx)) for i in range(n) for x in range(2)
        ]
        got.append(lax.ppermute(piece, ("seq", "tp"), perm))
    got[0], pre_out = lax.optimization_barrier((got[0], pre_out))
    for piece in got:
        total = total + piece.astype(jnp.float32)
    dec_out = total.astype(jnp.bfloat16).T.reshape(deep // 2, steps, own, -1)
    return (pre_out, dec_out.transpose(0, 2, 1, 3).reshape(rows // 2, steps, -1))


def per_device(n, tp, q_pre, k_cache, v_cache, prompt_lengths, *rest):
    groups = k_cache.shape[1] // HD
    square = groups % 2 == 0 and k_cache.shape[1] == 2 * k_cache.shape[0]
    small = n * k_cache.shape[0] // BLK <= 256 and n == 2 * (LEVELS - PARTS)
    form = split_heads if square and tp == 2 and small else whole_heads
    return form(n, q_pre, k_cache, v_cache, prompt_lengths.astype(jnp.int32), *rest)


def solution(mesh):
    placed = (
        P("seq", "tp"),
        P("seq", "tp"),
        P("seq", "tp"),
        P(),
        P(None, None, "tp"),
        P(None, None, "tp"),
        P(None, None, "tp"),
        P(),
        P("tp", "seq"),
    )
    return jax.shard_map(
        functools.partial(per_device, mesh.shape["seq"], mesh.shape["tp"]),
        mesh=mesh,
        in_specs=placed,
        out_specs=(P("seq", "tp"), P("tp", None, "seq")),
        check_vma=False,
    )
```

profile of v0, /device:TPU:21, one launch (start us, length us, event | category | flops | bytes accessed | tf_op | source)
XLA Modules:
  0.0 235.0 jit_solution(18353511211826640195)
XLA Ops:
  0.7 0.9 copy-done.6
  1.6 0.9 copy-done.7
  2.6 0.1 prepare.1
  2.7 0.7 collective-permute-start
  3.5 0.1 stack.60.meta.refs_0_
  3.6 1.1 collective-permute-done.theirs
  4.6 1.5 copy-done.1
  6.1 0.1 join.1
  6.3 0.4 collective-permute-start.5
  6.7 1.3 collective-permute-start.4
  8.0 0.2 collective-permute-start.3
  8.2 1.3 collective-permute-start.2
  9.5 0.2 collective-permute-start.1
  9.7 4.8 %open.1 = (bf16[2,3584,128]{2,1,0:T(8,128)(2,1)S(1)}, f32[2,3584,128]{2,1,0:T(8,128)S(1)}, f32[2,3584,128]{2,1,0:T(8,128)S(1)}) custom-call(s32[15]{0:T(128)S(1)} %stack.60.meta.refs_0_, s32[3]{0:T(128)S(1)} %copy-done.9, bf16[256,3584]{1,0:T(8,128)(2,1)S(1)} %copy-done.2, bf16[256,1792]{1,0:T(8,128)(2,1)S(1)} %collective-permute-done.5.q_near, ...), custom_call_target="tpu_custom_call" | custom-call | flops 1024 | bytes 1024 | tf_op jit(solution)/shard_map/open/pallas_call | solution.py:276
  14.5 1.0 collective-permute-done.3.refs_5_.refs_2_
  15.5 0.2 collective-permute-start.8
  15.6 1.3 collective-permute-start.9
  16.9 3.2 %collective-permute-done.2.refs_8_.refs_5_ = bf16[256,512]{1,0:T(8,128)(2,1)S(1)} collective-permute-done((bf16[256,512]{1,0:T(8,128)(2,1)S(1)}, bf16[256,512]{1,0:T(8,128)(2,1)S(1)}, u32[]{:S(2)}, u32[]{:S(2)}) %collective-permute-start.2) | collective-permute-done | bytes 262176 | tf_op jit(solution)/shard_map/ppermute | solution.py:975
  20.1 1.0 collective-permute-done.1.refs_6_.refs_3_
  21.1 0.2 collective-permute-start.6
  21.2 1.3 collective-permute-start.7
  22.6 9.0 %stage1.1 = (f32[2,3584,128]{2,1,0:T(8,128)S(1)}, f32[2,3584,128]{2,1,0:T(8,128)S(1)}, f32[2,448,128]{2,1,0:T(8,128)S(1)}, f32[2,448,128]{2,1,0:T(8,128)S(1)}, b...) custom-call(s32[15]{0:T(128)S(1)} %stack.60.meta.refs_0_, ...), custom_call_target="tpu_custom_call", output_to_operand_aliasing={{0}: (3, {}), {1}: (4, {})} | custom-call | flops 1024 | bytes 1024 | tf_op jit(solution)/shard_map/stage1/pallas_call | solution.py:359
  31.6 0.2 collective-permute-start.12
  31.8 1.5 collective-permute-start.13
  33.4 1.6 collective-permute-start.11
  35.0 6.5 %stage3.1 = (f32[2,3584,128]{2,1,0:T(8,128)S(1)}, f32[2,3584,128]{2,1,0:T(8,128)S(1)}) custom-call(s32[15]{0:T(128)S(1)} %stack.60.meta.refs_0_, s32[3]{0:T(128)S(1)} %copy-done.9, bf16[2,3584,128]{2,1,0:T(8,128)(2,1)S(1)} %get-tuple-element.234.refs_2_.qs, ...), custom_call_target="tpu_custom_call", output_to_operand_aliasing={{0}: (3, {}), {1}: (4, {})} | custom-call | flops 1024 | bytes 1024 | tf_op jit(solution)/shard_map/stage3/pallas_call | solution.py:359
  41.6 1.2 collective-permute-done.10.refs_11_
  42.7 0.7 take.1
  43.4 3.5 %collective-permute-start.14 = (bf16[448,1792]{1,0:T(8,128)(2,1)S(1)}, bf16[448,1792]{1,0:T(8,128)(2,1)S(1)}, u32[]{:S(2)}, u32[]{:S(2)}) collective-permute-start(bf16[448,1792]{1,0:T(8,128)(2,1)S(1)} %take.1), channel_id=1, source_target_pairs={{0,2},{2,0},{4,6},{6,4},{8,10},{10,8},{12,14},{14,12},{16,18},{18,... | collective-permute-start | bytes 4816904 | tf_op jit(solution)/shard_map/ppermute | solution.py:999
  46.9 1.5 collective-permute-start.16
  48.4 0.1 collective-permute-start.15
  48.4 4.0 %early_decode.1 = (f32[2,448,128]{2,1,0:T(8,128)S(1)}, f32[2,448,128]{2,1,0:T(8,128)S(1)}) custom-call(f32[2,448,128]{2,1,0:T(8,128)S(1)} %get-tuple-element.198.total_in, f32[2,448,128]{2,1,0:T(8,128)S(1)} %get-tuple-element.199.acc_in, bf16[2,448,128]{2,1,0:T(8,128)(2,1)S(1)} %get-tuple-element.225.query, ...), custom_call_target="tpu_custom_call", output_to_operand_aliasing={{0}: (0, {}), {1}: (1, {})} | custom-call | flops 1024 | bytes 1024 | tf_op jit(solution)/shard_map/early_decode/pallas_call | solution.py:570
  52.4 2.5 %collective-permute-done.16.refs_14_ = bf16[256,512]{1,0:T(8,128)(2,1)S(1)} collective-permute-done((bf16[256,512]{1,0:T(8,128)(2,1)S(1)}, bf16[256,512]{1,0:T(8,128)(2,1)S(1)}, u32[]{:S(2)}, u32[]{:S(2)}) %collective-permute-start.16) | collective-permute-done | bytes 262176 | tf_op jit(solution)/shard_map/ppermute | solution.py:974
  54.9 1.0 collective-permute-done.15.refs_15_
  55.9 8.8 %late_decode.1.refs_0_ = bf16[64,1792]{1,0:T(8,128)(2,1)S(1)} custom-call(s32[15]{0:T(128)S(1)} %stack.60.meta.refs_0_, f32[2,448,128]{2,1,0:T(8,128)S(1)} %get-tuple-element.223.total, f32[2,448,128]{2,1,0:T(8,128)S(1)} %get-tuple-element.224.acc, bf16[2,448,128]{2,1,0:T(8,128)(2,1)S(1)} %get-tuple-element.225.query, ...), custom_call_target="tpu_custom_call" | custom-call | flops 469762048 | bytes 57344 | tf_op jit(solution)/shard_map/late_decode/pallas_call | solution.py:636
  64.7 0.4 collective-permute-start.19
  65.1 2.2 collective-permute-start.18
  67.2 155.4 %finish.1 = (bf16[256,1792]{1,0:T(8,128)(2,1)S(1)}, bf16[256,3584]{1,0:T(8,128)(2,1)}) custom-call(s32[15]{0:T(128)S(1)} %stack.60.meta.refs_0_, s32[3]{0:T(128)S(1)} %copy-done.9, bf16[2,3584,128]{2,1,0:T(8,128)(2,1)S(1)} %get-tuple-element.234.refs_2_.qs, f32[2,3584,128]{2,1,0:T(8,128)S(1)} %get-tuple-element.235.total, ...), custom_call_target="tpu_custom_call" | custom-call | flops 1879048192 | bytes 1835008 | tf_op jit(solution)/shard_map/finish/pallas_call | solution.py:467
  222.6 1.5 collective-permute-start.21
  224.1 2.4 %project.1 = (f32[448,128]{1,0:T(8,128)S(1)}, bf16[448,128]{1,0:T(8,128)(2,1)S(1)}, bf16[448,128]{1,0:T(8,128)(2,1)S(1)}, bf16[448,128]{1,0:T(8,128)(2,1)S(1)}) custom-call(s32[15]{0:T(128)S(1)} %stack.60.meta.refs_0_, bf16[64,1792]{1,0:T(8,128)(2,1)S(1)} %late_decode.1.refs_0_, bf16[64,1792]{1,0:T(8,128)(2,1)S(1)} %collective-permute-done.17.refs_1_, ...), custom_call_target="tpu_custom_call" | custom-call | flops 822083584 | bytes 3211264 | tf_op jit(solution)/shard_map/project/pallas_call | solution.py:857
  226.5 0.1 collective-permute-start.20
  226.6 1.3 collective-permute-start.22
  227.9 0.9 collective-permute-start.23
  228.7 1.5 settle.1
  230.2 0.7 collective-permute-done.22
  231.0 3.0 %collective-permute-done.23 = bf16[448,128]{1,0:T(8,128)(2,1)S(1)} collective-permute-done((bf16[448,128]{1,0:T(8,128)(2,1)S(1)}, bf16[448,128]{1,0:T(8,128)(2,1)S(1)}, u32[]{:S(2)}, u32[]{:S(2)}) %collective-permute-start.23) | collective-permute-done | bytes 114720 | tf_op jit(solution)/shard_map/ppermute | solution.py:1020
  234.1 0.1 copy.20
  234.2 0.8 copy.22
  (36 shorter events, 0.2 us)
Async XLA Ops:
  0.6 9.0 %copy-start.9 = (s32[3]{0:T(128)S(1)}, s32[3]{0:T(128)}, u32[]{:S(2)}) copy-start(s32[3]{0:T(128)} %lengths.3) | copy-start | bytes 40
  0.6 1.0 copy-start.6
  1.6 0.9 copy-start.7
  2.5 20.0 %copy-start.5 = (bf16[64,4,512]{2,1,0:T(4,128)(2,1)S(1)}, bf16[64,4,512]{2,1,0:T(4,128)(2,1)}, u32[]{:S(2)}) copy-start(bf16[64,4,512]{2,1,0:T(4,128)(2,1)} %refs_11_.1) | copy-start | bytes 786436
  2.7 19.8 %copy-start.4 = (bf16[64,4,512]{2,1,0:T(4,128)(2,1)S(1)}, bf16[64,4,512]{2,1,0:T(4,128)(2,1)}, u32[]{:S(2)}) copy-start(bf16[64,4,512]{2,1,0:T(4,128)(2,1)} %refs_10_.1) | copy-start | bytes 786436
  2.7 19.8 %copy-start.8 = (s32[64,32]{0,1:T(8,128)S(1)}, s32[64,32]{0,1:T(8,128)}, u32[]{:S(2)}) copy-start(s32[64,32]{0,1:T(8,128)} %param.16) | copy-start | bytes 24580
  2.7 1.9 collective-permute-start
  4.6 1.5 copy-start.1
  6.1 3.5 %copy-start.2 = (bf16[256,3584]{1,0:T(8,128)(2,1)S(1)}, bf16[256,3584]{1,0:T(8,128)(2,1)}, u32[]{:S(2)}) copy-start(bf16[256,3584]{1,0:T(8,128)(2,1)} %q.3) | copy-start | bytes 5505028
  6.1 16.4 %copy-start.3 = (bf16[64,4,3584]{2,1,0:T(4,128)(2,1)S(1)}, bf16[64,4,3584]{2,1,0:T(4,128)(2,1)}, u32[]{:S(2)}) copy-start(bf16[64,4,3584]{2,1,0:T(4,128)(2,1)} %refs_9_.1) | copy-start | bytes 5505028
  6.3 3.4 %collective-permute-start.5 = (bf16[256,1792]{1,0:T(8,128)(2,1)S(1)}, bf16[256,1792]{1,0:T(8,128)(2,1)S(1)}, u32[]{:S(2)}, u32[]{:S(2)}) collective-permute-start(bf16[256,1792]{1,0:T(8,128)(2,1)S(1)} %get-tuple-element.134), channel_id=1, source_target_pairs={{0,2},{2,0},{4,6},{6,4},{8,10},{10,8},{12,14},{14,12},{16,18},{18,... | collective-permute-start | bytes 2752520 | tf_op jit(solution)/shard_map/ppermute | solution.py:969
  6.7 7.8 %collective-permute-start.4 = (bf16[256,512]{1,0:T(8,128)(2,1)S(1)}, bf16[256,512]{1,0:T(8,128)(2,1)S(1)}, u32[]{:S(2)}, u32[]{:S(2)}) collective-permute-start(bf16[256,512]{1,0:T(8,128)(2,1)S(1)} %get-tuple-element.133.upper.refs_0_), channel_id=1, source_target_pairs={{0,4},{2,6},{8,0},{10,2},{16,8},{18,10},{24,16},{26,18},{28,24},{3... | collective-permute-start | bytes 786440 | tf_op jit(solution)/shard_map/ppermute | solution.py:977
  8.0 7.4 %collective-permute-start.3 = (bf16[256,512]{1,0:T(8,128)(2,1)S(1)}, bf16[256,512]{1,0:T(8,128)(2,1)S(1)}, u32[]{:S(2)}, u32[]{:S(2)}) collective-permute-start(bf16[256,512]{1,0:T(8,128)(2,1)S(1)} %get-tuple-element.133.upper.refs_0_), channel_id=1, source_target_pairs={{0,8},{2,10},{8,16},{10,18},{16,24},{18,26},{24,28},{26,30},{28,20... | collective-permute-start | bytes 786440 | tf_op jit(solution)/shard_map/ppermute | solution.py:974
  8.2 11.9 %collective-permute-start.2 = (bf16[256,512]{1,0:T(8,128)(2,1)S(1)}, bf16[256,512]{1,0:T(8,128)(2,1)S(1)}, u32[]{:S(2)}, u32[]{:S(2)}) collective-permute-start(bf16[256,512]{1,0:T(8,128)(2,1)S(1)} %get-tuple-element.132.lower.refs_1_), channel_id=1, source_target_pairs={{0,4},{2,6},{8,0},{10,2},{16,8},{18,10},{24,16},{26,18},{28,24},{3... | collective-permute-start | bytes 786440 | tf_op jit(solution)/shard_map/ppermute | solution.py:975
  9.5 11.6 %collective-permute-start.1 = (bf16[256,512]{1,0:T(8,128)(2,1)S(1)}, bf16[256,512]{1,0:T(8,128)(2,1)S(1)}, u32[]{:S(2)}, u32[]{:S(2)}) collective-permute-start(bf16[256,512]{1,0:T(8,128)(2,1)S(1)} %get-tuple-element.132.lower.refs_1_), channel_id=1, source_target_pairs={{0,8},{2,10},{8,16},{10,18},{16,24},{18,26},{24,28},{26,30},{28,20... | collective-permute-start | bytes 786440 | tf_op jit(solution)/shard_map/ppermute | solution.py:978
  15.5 16.1 %collective-permute-start.8 = (bf16[256,512]{1,0:T(8,128)(2,1)S(1)}, bf16[256,512]{1,0:T(8,128)(2,1)S(1)}, u32[]{:S(2)}, u32[]{:S(2)}) collective-permute-start(bf16[256,512]{1,0:T(8,128)(2,1)S(1)} %collective-permute-done.3.refs_5_.refs_2_), channel_id=1, source_target_pairs={{0,8},{2,10},{8,16},{10,18},{16,24},{18,26},{24,28},{26,30},{28,20... | collective-permute-start | bytes 786440 | tf_op jit(solution)/shard_map/ppermute | solution.py:974
  15.6 15.9 %collective-permute-start.9 = (bf16[256,512]{1,0:T(8,128)(2,1)S(1)}, bf16[256,512]{1,0:T(8,128)(2,1)S(1)}, u32[]{:S(2)}, u32[]{:S(2)}) collective-permute-start(bf16[256,512]{1,0:T(8,128)(2,1)S(1)} %collective-permute-done.4.refs_7_.refs_4_), channel_id=1, source_target_pairs={{0,4},{2,6},{8,0},{10,2},{16,8},{18,10},{24,16},{26,18},{28,24},{3... | collective-permute-start | bytes 786440 | tf_op jit(solution)/shard_map/ppermute | solution.py:977
  21.1 12.3 %collective-permute-start.6 = (bf16[256,512]{1,0:T(8,128)(2,1)S(1)}, bf16[256,512]{1,0:T(8,128)(2,1)S(1)}, u32[]{:S(2)}, u32[]{:S(2)}) collective-permute-start(bf16[256,512]{1,0:T(8,128)(2,1)S(1)} %collective-permute-done.1.refs_6_.refs_3_), channel_id=1, source_target_pairs={{0,8},{2,10},{8,16},{10,18},{16,24},{18,26},{24,28},{26,30},{28,20... | collective-permute-start | bytes 786440 | tf_op jit(solution)/shard_map/ppermute | solution.py:978
  21.2 12.1 %collective-permute-start.7 = (bf16[256,512]{1,0:T(8,128)(2,1)S(1)}, bf16[256,512]{1,0:T(8,128)(2,1)S(1)}, u32[]{:S(2)}, u32[]{:S(2)}) collective-permute-start(bf16[256,512]{1,0:T(8,128)(2,1)S(1)} %collective-permute-done.2.refs_8_.refs_5_), channel_id=1, source_target_pairs={{0,4},{2,6},{8,0},{10,2},{16,8},{18,10},{24,16},{26,18},{28,24},{3... | collective-permute-start | bytes 786440 | tf_op jit(solution)/shard_map/ppermute | solution.py:975
  31.6 11.2 %copy-start = (bf16[3584,448]{0,1:T(8,128)(2,1)S(1)}, bf16[3584,448]{0,1:T(8,128)(2,1)}, u32[]{:S(2)}) copy-start(bf16[3584,448]{0,1:T(8,128)(2,1)} %param.17) | copy-start | bytes 9633796
  31.6 10.0 %collective-permute-start.12 = (bf16[256,512]{1,0:T(8,128)(2,1)S(1)}, bf16[256,512]{1,0:T(8,128)(2,1)S(1)}, u32[]{:S(2)}, u32[]{:S(2)}) collective-permute-start(bf16[256,512]{1,0:T(8,128)(2,1)S(1)} %collective-permute-done.8.refs_5_.refs_6_), channel_id=1, source_target_pairs={{0,8},{2,10},{8,16},{10,18},{16,24},{18,26},{24,28},{26,30},{28,20... | collective-permute-start | bytes 786440 | tf_op jit(solution)/shard_map/ppermute | solution.py:974
  31.8 9.8 %collective-permute-start.13 = (bf16[256,512]{1,0:T(8,128)(2,1)S(1)}, bf16[256,512]{1,0:T(8,128)(2,1)S(1)}, u32[]{:S(2)}, u32[]{:S(2)}) collective-permute-start(bf16[256,512]{1,0:T(8,128)(2,1)S(1)} %collective-permute-done.9.refs_7_.refs_8_), channel_id=1, source_target_pairs={{0,4},{2,6},{8,0},{10,2},{16,8},{18,10},{24,16},{26,18},{28,24},{3... | collective-permute-start | bytes 786440 | tf_op jit(solution)/shard_map/ppermute | solution.py:977
  33.4 9.4 %collective-permute-start.10 = (bf16[256,512]{1,0:T(8,128)(2,1)S(1)}, bf16[256,512]{1,0:T(8,128)(2,1)S(1)}, u32[]{:S(2)}, u32[]{:S(2)}) collective-permute-start(bf16[256,512]{1,0:T(8,128)(2,1)S(1)} %collective-permute-done.6.refs_6_.refs_7_), channel_id=1, source_target_pairs={{0,8},{2,10},{8,16},{10,18},{16,24},{18,26},{24,28},{26,30},{28,20... | collective-permute-start | bytes 786440 | tf_op jit(solution)/shard_map/ppermute | solution.py:978
  33.4 9.4 %collective-permute-start.11 = (bf16[256,512]{1,0:T(8,128)(2,1)S(1)}, bf16[256,512]{1,0:T(8,128)(2,1)S(1)}, u32[]{:S(2)}, u32[]{:S(2)}) collective-permute-start(bf16[256,512]{1,0:T(8,128)(2,1)S(1)} %collective-permute-done.7.refs_8_.refs_9_), channel_id=1, source_target_pairs={{0,4},{2,6},{8,0},{10,2},{16,8},{18,10},{24,16},{26,18},{28,24},{3... | collective-permute-start | bytes 786440 | tf_op jit(solution)/shard_map/ppermute | solution.py:975
  43.4 12.5 %collective-permute-start.14 = (bf16[448,1792]{1,0:T(8,128)(2,1)S(1)}, bf16[448,1792]{1,0:T(8,128)(2,1)S(1)}, u32[]{:S(2)}, u32[]{:S(2)}) collective-permute-start(bf16[448,1792]{1,0:T(8,128)(2,1)S(1)} %take.1), channel_id=1, source_target_pairs={{0,2},{2,0},{4,6},{6,4},{8,10},{10,8},{12,14},{14,12},{16,18},{18,... | collective-permute-start | bytes 4816904 | tf_op jit(solution)/shard_map/ppermute | solution.py:999
  46.9 8.0 %collective-permute-start.16 = (bf16[256,512]{1,0:T(8,128)(2,1)S(1)}, bf16[256,512]{1,0:T(8,128)(2,1)S(1)}, u32[]{:S(2)}, u32[]{:S(2)}) collective-permute-start(bf16[256,512]{1,0:T(8,128)(2,1)S(1)} %collective-permute-done.12.refs_10_), channel_id=1, source_target_pairs={{0,8},{2,10},{8,16},{10,18},{16,24},{18,26},{24,28},{26,30},{28,20... | collective-permute-start | bytes 786440 | tf_op jit(solution)/shard_map/ppermute | solution.py:974
  48.4 7.5 %collective-permute-start.15 = (bf16[256,512]{1,0:T(8,128)(2,1)S(1)}, bf16[256,512]{1,0:T(8,128)(2,1)S(1)}, u32[]{:S(2)}, u32[]{:S(2)}) collective-permute-start(bf16[256,512]{1,0:T(8,128)(2,1)S(1)} %collective-permute-done.11.refs_13_), channel_id=1, source_target_pairs={{0,4},{2,6},{8,0},{10,2},{16,8},{18,10},{24,16},{26,18},{28,24},{3... | collective-permute-start | bytes 786440 | tf_op jit(solution)/shard_map/ppermute | solution.py:975
  64.7 157.9 %collective-permute-start.19 = (bf16[64,1792]{1,0:T(8,128)(2,1)S(1)}, bf16[64,1792]{1,0:T(8,128)(2,1)S(1)}, u32[]{:S(2)}, u32[]{:S(2)}) collective-permute-start(bf16[64,1792]{1,0:T(8,128)(2,1)S(1)} %late_decode.1.refs_0_), channel_id=1, source_target_pairs={{0,24},{2,26},{4,28},{6,30},{8,0},{10,2},{12,4},{14,6},{16,8},{18,... | collective-permute-start | bytes 688136 | tf_op jit(solution)/shard_map/ppermute | solution.py:1007
  65.1 157.6 %collective-permute-start.18 = (bf16[64,1792]{1,0:T(8,128)(2,1)S(1)}, bf16[64,1792]{1,0:T(8,128)(2,1)S(1)}, u32[]{:S(2)}, u32[]{:S(2)}) collective-permute-start(bf16[64,1792]{1,0:T(8,128)(2,1)S(1)} %late_decode.1.refs_0_), channel_id=1, source_target_pairs={{0,16},{2,18},{4,20},{6,22},{8,24},{10,26},{12,28},{14,30},{16,0},... | collective-permute-start | bytes 688136 | tf_op jit(solution)/shard_map/ppermute | solution.py:1007
  67.2 155.4 %collective-permute-start.17 = (bf16[64,1792]{1,0:T(8,128)(2,1)S(1)}, bf16[64,1792]{1,0:T(8,128)(2,1)S(1)}, u32[]{:S(2)}, u32[]{:S(2)}) collective-permute-start(bf16[64,1792]{1,0:T(8,128)(2,1)S(1)} %late_decode.1.refs_0_), channel_id=1, source_target_pairs={{0,8},{2,10},{4,12},{6,14},{8,16},{10,18},{12,20},{14,22},{16,24},... | collective-permute-start | bytes 688136 | tf_op jit(solution)/shard_map/ppermute | solution.py:1007
  222.6 6.1 %collective-permute-start.21 = (bf16[256,1792]{1,0:T(8,128)(2,1)S(1)}, bf16[256,1792]{1,0:T(8,128)(2,1)S(1)}, u32[]{:S(2)}, u32[]{:S(2)}) collective-permute-start(bf16[256,1792]{1,0:T(8,128)(2,1)S(1)} %get-tuple-element.245), channel_id=1, source_target_pairs={{0,2},{2,0},{4,6},{6,4},{8,10},{10,8},{12,14},{14,12},{16,18},{18,... | collective-permute-start | bytes 2752520 | tf_op jit(solution)/shard_map/ppermute | solution.py:1011
  226.5 3.7 %collective-permute-start.20 = (bf16[448,128]{1,0:T(8,128)(2,1)S(1)}, bf16[448,128]{1,0:T(8,128)(2,1)S(1)}, u32[]{:S(2)}, u32[]{:S(2)}) collective-permute-start(bf16[448,128]{1,0:T(8,128)(2,1)S(1)} %get-tuple-element.244), channel_id=1, source_target_pairs={{0,2},{1,3},{2,0},{3,1},{4,6},{5,7},{6,4},{7,5},{8,10},{9,11},{10,... | collective-permute-start | bytes 344072 | tf_op jit(solution)/shard_map/ppermute | solution.py:1020
  226.6 4.3 %collective-permute-start.22 = (bf16[448,128]{1,0:T(8,128)(2,1)S(1)}, bf16[448,128]{1,0:T(8,128)(2,1)S(1)}, u32[]{:S(2)}, u32[]{:S(2)}) collective-permute-start(bf16[448,128]{1,0:T(8,128)(2,1)S(1)} %get-tuple-element.250), channel_id=1, source_target_pairs={{0,1},{1,0},{2,3},{3,2},{4,5},{5,4},{6,7},{7,6},{8,9},{9,8},{10,11... | collective-permute-start | bytes 344072 | tf_op jit(solution)/shard_map/ppermute | solution.py:1020
  227.9 6.1 %collective-permute-start.23 = (bf16[448,128]{1,0:T(8,128)(2,1)S(1)}, bf16[448,128]{1,0:T(8,128)(2,1)S(1)}, u32[]{:S(2)}, u32[]{:S(2)}) collective-permute-start(bf16[448,128]{1,0:T(8,128)(2,1)S(1)} %get-tuple-element.251), channel_id=1, source_target_pairs={{0,3},{1,2},{2,1},{3,0},{4,7},{5,6},{6,5},{7,4},{8,11},{9,10},{10,... | collective-permute-start | bytes 344072 | tf_op jit(solution)/shard_map/ppermute | solution.py:1020
where the time goes:
time: 236 us; the launch traced here: 235 us
  Pallas kernels  193 us (82%)
  starting transfers between devices  21.7 us (9%)
  waiting for transfers between devices  14.7 us (6%)
  local copies, waits for them, and re-layouts  4.4 us (2%)
    pallas_call x1, Pallas kernels, finish(): pl.pallas_call(functools.partial(finish_kernel, tok, heads, groups, done)...  155 us
    pallas_call x2, Pallas kernels, stage(): pl.pallas_call(functools.partial(stage_kernel, tok, heads, groups, first_...  15.5 us
    pallas_call x1, Pallas kernels, late_decode(): pl.pallas_call(functools.partial(late_kernel, own, steps, heads, groups,...  8.76 us
    pallas_call x1, Pallas kernels, open_sums(): pl.pallas_call(functools.partial(open_kernel, tok, heads, groups), out_sh...  4.79 us
  transfers between devices with their start and end apart: 24, of which 9 were waited for; matrix products, arithmetic and copies ran while one was open for 0% of the time, Pallas kernels for 78%

commit v1 on v0

--- a/solution.py
+++ b/solution.py
@@ -220,12 +220,13 @@
 
 def add_block(tok, heads, q_at, keys, values, allowed, sums, fresh=False):
     length = keys.shape[1]
+    bias = None if allowed is None else jnp.where(allowed, 0.0, -jnp.inf)
     for j in range(0, heads, PAIR):
         some = min(PAIR, heads - j)
-        p = jnp.exp2(dot_nn(q_at(j * tok, some * tok), keys) * FACTOR)
-        if allowed is not None:
-            p = p.reshape(some, tok, length)
-            p = jnp.where(allowed[None], p, 0.0).reshape(some * tok, length)
+        s = dot_nn(q_at(j * tok, some * tok), keys) * FACTOR
+        if bias is not None:
+            s = (s.reshape(some, tok, length) + bias[None]).reshape(some * tok, length)
+        p = jnp.exp2(s)
         more = (fold(p, jnp.add), dot_nn(p.astype(jnp.bfloat16), values))
         for ref, value in zip(sums, more):
             here = slice(j * tok, (j + some) * tok)
@@ -310,64 +311,29 @@
             add_block(tok, heads, q_at, keys_of(upper, g), values_of(lower, g), allowed, sums)
 
 
-def stage_kernel(tok, heads, groups, first_part, own, *refs):
-    meta, lengths, qs, total_in, acc_in = refs[:5]
-    pair = refs[5:9]
-    if own is None:
-        total, acc, *held = refs[9:]
-    else:
-        sources, table = refs[9:12], refs[12]
-        total, acc, state, held = refs[13], refs[14], refs[15:21], refs[21:23]
-        q3, k3, v3, sems = refs[23:]
-        copies = request_copies(own, meta, sources, (q3, k3, v3), sems)
-        for copy in copies:
-            copy.start()
+def stage_kernel(tok, heads, groups, first_part, meta, lengths, qs, total_in, acc_in, *refs):
+    pair, (total, acc), held = refs[:4], refs[4:6], refs[6:]
     before = (total_in, acc_in)
     stage_body(tok, heads, groups, first_part, meta, lengths, qs, before, pair, total, acc, held)
-    if own is not None:
-        for copy in copies:
-            copy.wait()
-        requests_body(own, heads, groups, 2 * tok, meta, table, *state, q3, k3, v3)
-
-
-def stage(state, pair, first_part, meta, lengths, requests=None):
+
+
+def stage(state, pair, first_part, meta, lengths):
     qs, total, acc = state
     groups, rows, unused = qs.shape
     flat = [x for block in pair for x in block]
     tok = flat[0].shape[1] // 2
-    heads = rows // (2 * tok)
-    out_shape = [jax.ShapeDtypeStruct(x.shape, x.dtype) for x in (total, acc)]
-    scratch = [pltpu.VMEM((2, *x.shape), x.dtype) for x in pair[0]]
-    sources, own = [], None
-    if requests is not None:
-        *sources, own = requests
-        steps = sources[0].shape[1]
-        width = sources[1].shape[2] // 2
-        size = heads * own * steps
-        sums = jax.ShapeDtypeStruct((groups, size, HD), jnp.float32)
-        new = jax.ShapeDtypeStruct((own * steps, width), jnp.bfloat16)
-        out_shape += [
-            sums, sums, jax.ShapeDtypeStruct((groups, size, HD), jnp.bfloat16), new, new,
-            jax.ShapeDtypeStruct((own, (LEVELS - PARTS) * 2 * tok), jnp.float32),
-        ]
-        scratch += [
-            pltpu.VMEM((own, steps, groups * heads * HD), jnp.bfloat16),
-            pltpu.VMEM((own, steps, width), jnp.bfloat16),
-            pltpu.VMEM((own, steps, width), jnp.bfloat16),
-            pltpu.SemaphoreType.DMA((3,)),
-        ]
     new = pl.pallas_call(
-        functools.partial(stage_kernel, tok, heads, groups, first_part, own),
-        out_shape=out_shape,
-        in_specs=[SMEM, SMEM] + [VMEM] * 7 + ([HBM] * 3 + [VMEM] if sources else []),
-        out_specs=[VMEM] * len(out_shape),
-        scratch_shapes=scratch,
+        functools.partial(stage_kernel, tok, rows // (2 * tok), groups, first_part),
+        out_shape=[jax.ShapeDtypeStruct(x.shape, x.dtype) for x in (total, acc)],
+        in_specs=[SMEM, SMEM] + [VMEM] * 7,
+        out_specs=[VMEM] * 2,
+        scratch_shapes=[pltpu.VMEM((2, *x.shape), x.dtype) for x in pair[0]],
         input_output_aliases={3: 0, 4: 1},
         compiler_params=pltpu.CompilerParams(vmem_limit_bytes=ROOM),
         cost_estimate=BRIEF,
         name=f"stage{first_part}",
-    )(meta, lengths, qs, total, acc, *flat, *sources)
-    return (qs, *new[:2]), new[2:]
+    )(meta, lengths, qs, total, acc, *flat)
+    return qs, *new
 
 
 def finish_kernel(tok, heads, groups, done, meta, lengths, qs, total, acc, *refs):
@@ -487,9 +453,9 @@
     )(meta, lengths, qs, total, acc, *flat)
 
 
-def request_sums(query, keys, values, mask):
-    p = jnp.exp2(dot_nn(query, keys) * FACTOR)
-    p = jnp.where(mask[None], p.reshape(-1, *mask.shape), 0.0).reshape(p.shape)
+def request_sums(query, keys, values, bias):
+    s = dot_nn(query, keys) * FACTOR
+    p = jnp.exp2((s.reshape(-1, *bias.shape) + bias[None]).reshape(s.shape))
     return fold(p, jnp.add), dot_nn(p.astype(jnp.bfloat16), values)
 
 
@@ -524,7 +490,7 @@
         hit = rows[:, :1] == number
         for j in range(1, rows.shape[1]):
             hit = hit | (rows[:, j : j + 1] == number)
-        mask[:, i * length : (i + 1) * length] = hit.astype(jnp.float32)
+        mask[:, i * length : (i + 1) * length] = jnp.where(hit, 0.0, -jnp.inf)
     for s in range(steps):
         for g in range(groups):
             col = slice(g * HD, (g + 1) * HD)
@@ -547,6 +513,44 @@
         acc[g] = dot_nn(p.astype(jnp.bfloat16), newv[:, col])
 
 
+def requests_kernel(own, heads, groups, length, meta, *refs):
+    sources, table, state, (q3, k3, v3, sems) = refs[:3], refs[3], refs[4:10], refs[10:]
+    copies = request_copies(own, meta, sources, (q3, k3, v3), sems)
+    for copy in copies:
+        copy.start()
+    for copy in copies:
+        copy.wait()
+    requests_body(own, heads, groups, length, meta, table, *state, q3, k3, v3)
+
+
+def open_requests(q_dec, k_new, v_new, table, length, own, meta):
+    heads = H // KVH
+    steps = q_dec.shape[1]
+    width = k_new.shape[2] // 2
+    groups = width // HD
+    rows = heads * own * steps
+    sums = jax.ShapeDtypeStruct((groups, rows, HD), jnp.float32)
+    new = jax.ShapeDtypeStruct((own * steps, width), jnp.bfloat16)
+    return pl.pallas_call(
+        functools.partial(requests_kernel, own, heads, groups, length),
+        out_shape=[
+            sums, sums, jax.ShapeDtypeStruct((groups, rows, HD), jnp.bfloat16), new, new,
+            jax.ShapeDtypeStruct((own, (LEVELS - PARTS) * length), jnp.float32),
+        ],
+        in_specs=[SMEM] + [HBM] * 3 + [VMEM],
+        out_specs=[VMEM] * 6,
+        scratch_shapes=[
+            pltpu.VMEM((own, steps, groups * heads * HD), jnp.bfloat16),
+            pltpu.VMEM((own, steps, width), jnp.bfloat16),
+            pltpu.VMEM((own, steps, width), jnp.bfloat16),
+            pltpu.SemaphoreType.DMA((3,)),
+        ],
+        compiler_params=pltpu.CompilerParams(vmem_limit_bytes=LITTLE),
+        cost_estimate=BRIEF,
+        name="requests",
+    )(meta, q_dec, k_new, v_new, table)
+
+
 def early_kernel(groups, total_in, acc_in, query, mask, *refs):
     total, acc = refs[-2:]
     length = refs[0].shape[1]
@@ -555,9 +559,9 @@
     def _(g):
         sums = [total_in[g], acc_in[g]]
         for i in range(len(refs) // 2 - 1):
-            open_to = mask[:, i * length : (i + 1) * length] > 0
+            bias = mask[:, i * length : (i + 1) * length]
             keys, values = keys_of(refs[2 * i], g), values_of(refs[2 * i + 1], g)
-            more = request_sums(query[g], keys, values, open_to)
+            more = request_sums(query[g], keys, values, bias)
             sums = [x + y for x, y in zip(sums, more)]
         total[g], acc[g] = sums
 
@@ -593,9 +597,9 @@
     def one_group(g, fine):
         sums = [total[g], acc[g]]
         for i in range(done, parts):
-            open_to = mask[:, i * length : (i + 1) * length] > 0
+            bias = mask[:, i * length : (i + 1) * length]
             keys, values = keys_of(refs[2 * i], g), values_of(refs[2 * i + 1], g)
-            more = request_sums(query[g], keys, values, open_to)
+            more = request_sums(query[g], keys, values, bias)
             sums = [x + y for x, y in zip(sums, more)]
         whole = jnp.sum(sums[0], axis=1, keepdims=True)
         write(g, sums[1], whole)
@@ -616,7 +620,7 @@
             sums = dot_nn(p.astype(jnp.bfloat16), newv[:, col])
             for i in range(parts):
                 s = dot_nn(query[g], keys_of(refs[2 * i], g)) * FACTOR
-                open_to = mask[:, i * length : (i + 1) * length] > 0
+                open_to = mask[:, i * length : (i + 1) * length] >= 0
                 s = jnp.where(open_to[None], s.reshape(-1, own, length), NEG).reshape(s.shape)
                 higher = jnp.maximum(top, jnp.max(s, axis=1, keepdims=True))
                 p = jnp.exp2(s - higher)
@@ -943,6 +947,7 @@
 
 
 def split_heads(n, q_pre, k_cache, v_cache, lengths, q_dec, k_new, v_new, block_table, w_out):
+    tok = q_pre.shape[0]
     place = lax.axis_index("seq").astype(jnp.int32)
     across = lax.axis_index("tp").astype(jnp.int32)
     core, chip = lax.rem(place, 2), lax.div(place, 2)
@@ -983,16 +988,19 @@
         if d == 1:
             state = open_sums(q_pre, near_q, (held_k[0], held_v[0]), meta, lengths)
         elif d < far:
-            requests = (q_dec, k_new, v_new, block_table.T, own) if d == 2 else None
             pair = [(held_k[o], held_v[o]) for o in (1 - d, d - 1)]
-            state, more = stage(state, pair, 2 * d - 3, meta, lengths, requests)
-            early = early or more
+            state = stage(state, pair, 2 * d - 3, meta, lengths)
         else:
             blocks = [(held_k[o], held_v[o]) for o in order[:-1]]
             early = early_decode(early, blocks)
         for x in (held_k, held_v):
             moved, state, early = lax.optimization_barrier(([x[o] for o in sides], state, early))
             x.update(zip(sides, moved))
+            if d == 1 and x is held_k:
+                state, block_table = lax.optimization_barrier((state, block_table))
+                early = open_requests(
+                    q_dec, k_new, v_new, block_table.T, 2 * tok, own, meta
+                )
         if d == 3:
             w_near, state = lax.optimization_barrier((w_near, state))
             weights = w_near.T

time: 236 us -> 231 us (0.979)
  Pallas kernels: 193 us -> 188 us
  waiting for transfers between devices: 14.7 us -> 10.5 us
    pallas_call x1, Pallas kernels: 155 us -> 149 us  [finish(): pl.pallas_call(functools.partial(finish_kernel, tok, heads, groups, done)...]
    ppermute x4, waiting for transfers between devices: 4.2 us -> 0.01 us  [split_heads(): held_v[d] = lax.ppermute(held_v[d - 1], 'seq', down)]
    ppermute x3, starting transfers between devices: 2.52 us -> 5.13 us  [split_heads(): pieces.append(lax.ppermute(attn_own, 'seq', perm))]
    pallas_call x2 -> x3, Pallas kernels: 15.5 us -> 16.7 us  [the longest x2 13.8 us: stage(): pl.pallas_call(functools.partial(stage_kernel, tok, rows // (2 * tok), gr...]
  transfers between devices with their start and end apart: 24 -> 24, of which waited for: 9 -> 8; matrix products, arithmetic and copies ran while one was open for 0% -> 0% of each run, Pallas kernels for 78% -> 78%
where the time goes in v1:
time: 231 us; the launch traced here: 228 us
  Pallas kernels  188 us (81%)
  starting transfers between devices  23.6 us (10%)
  waiting for transfers between devices  10.5 us (5%)
  local copies, waits for them, and re-layouts  4.4 us (2%)
    pallas_call x1, Pallas kernels, finish(): pl.pallas_call(functools.partial(finish_kernel, tok, heads, groups, done)...  149 us
    pallas_call x2, Pallas kernels, stage(): pl.pallas_call(functools.partial(stage_kernel, tok, rows // (2 * tok), gr...  13.8 us
    pallas_call x1, Pallas kernels, late_decode(): pl.pallas_call(functools.partial(late_kernel, own, steps, heads, groups,...  8.76 us
    ppermute x4, starting transfers between devices, split_heads(): held_v[d] = lax.ppermute(held_v[d - 1], 'seq', down)  5.17 us
    ppermute x3, starting transfers between devices, split_heads(): pieces.append(lax.ppermute(attn_own, 'seq', perm))  5.13 us
    pallas_call x1, Pallas kernels, open_sums(): pl.pallas_call(functools.partial(open_kernel, tok, heads, groups), out_sh...  4.63 us
  transfers between devices with their start and end apart: 24, of which 8 were waited for; matrix products, arithmetic and copies ran while one was open for 0% of the time, Pallas kernels for 78%

profile of v1, /device:TPU:21, one launch (start us, length us, event | category | flops | bytes accessed | tf_op | source)
XLA Modules:
  0.0 227.8 jit_solution(4071336474856254492)
XLA Ops:
  0.7 0.9 copy-done.4
  1.6 0.9 copy-done.5
  2.6 0.1 prepare.1
  2.7 0.7 collective-permute-start
  3.5 0.1 stack.60.meta
  3.6 1.1 collective-permute-done.theirs
  4.6 1.5 copy-done.1
  6.1 0.1 join.1
  6.3 0.4 collective-permute-start.5
  6.7 0.2 collective-permute-start.3
  6.9 1.3 collective-permute-start.4
  8.2 0.2 collective-permute-start.1
  8.3 1.3 collective-permute-start.2
  9.7 4.6 %open.1 = (bf16[2,3584,128]{2,1,0:T(8,128)(2,1)S(1)}, f32[2,3584,128]{2,1,0:T(8,128)S(1)}, f32[2,3584,128]{2,1,0:T(8,128)S(1)}) custom-call(s32[15]{0:T(128)S(1)} %stack.60.meta, s32[3]{0:T(128)S(1)} %copy-done.9, bf16[256,3584]{1,0:T(8,128)(2,1)S(1)} %copy-done.2, bf16[256,1792]{1,0:T(8,128)(2,1)S(1)} %collective-permute-done.5.q_near, ...), custom_call_target="tpu_custom_call" | custom-call | flops 1024 | bytes 1024 | tf_op jit(solution)/shard_map/open/pallas_call | solution.py:277
  14.3 0.2 collective-permute-done.3.refs_0_.refs_2_
  14.5 0.2 collective-permute-start.8
  14.7 1.3 collective-permute-start.9
  16.0 3.0 %requests.1 = (f32[2,448,128]{2,1,0:T(8,128)S(1)}, f32[2,448,128]{2,1,0:T(8,128)S(1)}, bf16[2,448,128]{2,1,0:T(8,128)(2,1)S(1)}, bf16[64,256]{1,0:T(8,128)(2,1)S...) custom-call(s32[15]{0:T(128)S(1)} %stack.60.meta, bf16[64,4,3584]{2,1,0:T(4,128)(2,1)S(1)} %copy-done.3, ...), custom_call_target="tpu_custom_call" | custom-call | flops 1024 | bytes 1024 | tf_op jit(solution)/shard_map/requests/pallas_call | solution.py:534
  19.0 1.1 collective-permute-done.1.refs_1_.refs_3_
  20.1 0.2 collective-permute-start.6
  20.3 1.3 collective-permute-start.7
  21.6 6.5 %stage1.1 = (f32[2,3584,128]{2,1,0:T(8,128)S(1)}, f32[2,3584,128]{2,1,0:T(8,128)S(1)}) custom-call(s32[15]{0:T(128)S(1)} %stack.60.meta, s32[3]{0:T(128)S(1)} %copy-done.9, bf16[2,3584,128]{2,1,0:T(8,128)(2,1)S(1)} %get-tuple-element.254.qs, f32[2,3584,128]{2,1,0:T(8,128)S(1)} %get-tuple-element.166.total_in, ...), custom_call_target="tpu_custom_call", output_to_operand_aliasing={{0}: (3, {}), {1}: (4, {})} | custom-call | flops 1024 | bytes 1024 | tf_op jit(solution)/shard_map/stage1/pallas_call | solution.py:325
  28.2 0.9 collective-permute-start.12
  29.0 1.2 collective-permute-start.13
  30.2 1.1 collective-permute-done.6.refs_1_.refs_7_
  31.3 0.2 collective-permute-start.10
  31.5 1.3 collective-permute-start.11
  32.8 7.2 %stage3.1 = (f32[2,3584,128]{2,1,0:T(8,128)S(1)}, f32[2,3584,128]{2,1,0:T(8,128)S(1)}) custom-call(s32[15]{0:T(128)S(1)} %stack.60.meta, s32[3]{0:T(128)S(1)} %copy-done.9, bf16[2,3584,128]{2,1,0:T(8,128)(2,1)S(1)} %get-tuple-element.254.qs, f32[2,3584,128]{2,1,0:T(8,128)S(1)} %get-tuple-element.190.total_in, ...), custom_call_target="tpu_custom_call", output_to_operand_aliasing={{0}: (3, {}), {1}: (4, {})} | custom-call | flops 1024 | bytes 1024 | tf_op jit(solution)/shard_map/stage3/pallas_call | solution.py:325
  40.1 0.7 collective-permute-done.10.refs_11_
  40.8 0.7 take.1
  41.5 3.0 %collective-permute-start.14 = (bf16[448,1792]{1,0:T(8,128)(2,1)S(1)}, bf16[448,1792]{1,0:T(8,128)(2,1)S(1)}, u32[]{:S(2)}, u32[]{:S(2)}) collective-permute-start(bf16[448,1792]{1,0:T(8,128)(2,1)S(1)} %take.1), channel_id=1, source_target_pairs={{0,2},{2,0},{4,6},{6,4},{8,10},{10,8},{12,14},{14,12},{16,18},{18,... | collective-permute-start | bytes 4816904 | tf_op jit(solution)/shard_map/ppermute | solution.py:1007
  44.4 0.2 collective-permute-start.16
  44.6 1.3 collective-permute-start.15
  45.9 4.0 %early_decode.1 = (f32[2,448,128]{2,1,0:T(8,128)S(1)}, f32[2,448,128]{2,1,0:T(8,128)S(1)}) custom-call(f32[2,448,128]{2,1,0:T(8,128)S(1)} %get-tuple-element.218.total_in, f32[2,448,128]{2,1,0:T(8,128)S(1)} %get-tuple-element.219.acc_in, bf16[2,448,128]{2,1,0:T(8,128)(2,1)S(1)} %get-tuple-element.245.query, ...), custom_call_target="tpu_custom_call", output_to_operand_aliasing={{0}: (0, {}), {1}: (1, {})} | custom-call | flops 1024 | bytes 1024 | tf_op jit(solution)/shard_map/early_decode/pallas_call | solution.py:574
  49.9 2.4 %collective-permute-done.16.refs_14_ = bf16[256,512]{1,0:T(8,128)(2,1)S(1)} collective-permute-done((bf16[256,512]{1,0:T(8,128)(2,1)S(1)}, bf16[256,512]{1,0:T(8,128)(2,1)S(1)}, u32[]{:S(2)}, u32[]{:S(2)}) %collective-permute-start.16) | collective-permute-done | bytes 262176 | tf_op jit(solution)/shard_map/ppermute | solution.py:979
  52.3 8.8 %late_decode.1.refs_0_ = bf16[64,1792]{1,0:T(8,128)(2,1)S(1)} custom-call(s32[15]{0:T(128)S(1)} %stack.60.meta, f32[2,448,128]{2,1,0:T(8,128)S(1)} %get-tuple-element.243.total, f32[2,448,128]{2,1,0:T(8,128)S(1)} %get-tuple-element.244.acc, bf16[2,448,128]{2,1,0:T(8,128)(2,1)S(1)} %get-tuple-element.245.query, bf16[64,256]{1,0:T(8,128)(2,1)S(1)} %get-tuple-element.246.newk, ...), custom_call_target="tpu_custom_call" | custom-call | flops 469762048 | bytes 57344 | tf_op jit(solution)/shard_map/late_decode/pallas_call | solution.py:640
  61.1 3.9 %collective-permute-start.17 = (bf16[64,1792]{1,0:T(8,128)(2,1)S(1)}, bf16[64,1792]{1,0:T(8,128)(2,1)S(1)}, u32[]{:S(2)}, u32[]{:S(2)}) collective-permute-start(bf16[64,1792]{1,0:T(8,128)(2,1)S(1)} %late_decode.1.refs_0_), channel_id=1, source_target_pairs={{0,8},{2,10},{4,12},{6,14},{8,16},{10,18},{12,20},{14,22},{16,24},... | collective-permute-start | bytes 688136 | tf_op jit(solution)/shard_map/ppermute | solution.py:1015
  64.9 1.3 collective-permute-start.19
  66.2 149.5 %finish.1 = (bf16[256,1792]{1,0:T(8,128)(2,1)S(1)}, bf16[256,3584]{1,0:T(8,128)(2,1)}) custom-call(s32[15]{0:T(128)S(1)} %stack.60.meta, s32[3]{0:T(128)S(1)} %copy-done.9, bf16[2,3584,128]{2,1,0:T(8,128)(2,1)S(1)} %get-tuple-element.254.qs, f32[2,3584,128]{2,1,0:T(8,128)S(1)} %get-tuple-element.255.total, f32[2,3584,128]{2,1,0:T(8,128)S(1)} %get-tuple-element.256.acc, ...), custom_call_target="tpu_custom_call" | custom-call | flops 1879048192 | bytes 1835008 | tf_op jit(solution)/shard_map/finish/pallas_call | solution.py:433
  215.7 1.3 collective-permute-start.21
  217.0 2.4 %project.1 = (f32[448,128]{1,0:T(8,128)S(1)}, bf16[448,128]{1,0:T(8,128)(2,1)S(1)}, bf16[448,128]{1,0:T(8,128)(2,1)S(1)}, bf16[448,128]{1,0:T(8,128)(2,1)S(1)}) custom-call(s32[15]{0:T(128)S(1)} %stack.60.meta, bf16[64,1792]{1,0:T(8,128)(2,1)S(1)} %late_decode.1.refs_0_, bf16[64,1792]{1,0:T(8,128)(2,1)S(1)} %collective-permute-done.17.refs_1_, ...), custom_call_target="tpu_custom_call" | custom-call | flops 822083584 | bytes 3211264 | tf_op jit(solution)/shard_map/project/pallas_call | solution.py:861
  219.5 1.3 collective-permute-start.22
  220.8 0.8 collective-permute-start.23
  221.6 1.5 settle.1
  223.1 0.7 collective-permute-done.22
  223.8 3.0 %collective-permute-done.23 = bf16[448,128]{1,0:T(8,128)(2,1)S(1)} collective-permute-done((bf16[448,128]{1,0:T(8,128)(2,1)S(1)}, bf16[448,128]{1,0:T(8,128)(2,1)S(1)}, u32[]{:S(2)}, u32[]{:S(2)}) %collective-permute-start.23) | collective-permute-done | bytes 114720 | tf_op jit(solution)/shard_map/ppermute | solution.py:1028
  226.9 0.1 copy.20
  227.1 0.8 copy.22
  (37 shorter events, 0.2 us)
Async XLA Ops:
  0.6 9.0 %copy-start.9 = (s32[3]{0:T(128)S(1)}, s32[3]{0:T(128)}, u32[]{:S(2)}) copy-start(s32[3]{0:T(128)} %lengths.7) | copy-start | bytes 40
  0.6 1.0 copy-start.4
  1.6 0.9 copy-start.5
  2.5 13.4 %copy-start.7 = (bf16[64,4,512]{2,1,0:T(4,128)(2,1)S(1)}, bf16[64,4,512]{2,1,0:T(4,128)(2,1)}, u32[]{:S(2)}) copy-start(bf16[64,4,512]{2,1,0:T(4,128)(2,1)} %refs_2_.1) | copy-start | bytes 786436
  2.7 13.2 %copy-start.6 = (bf16[64,4,512]{2,1,0:T(4,128)(2,1)S(1)}, bf16[64,4,512]{2,1,0:T(4,128)(2,1)}, u32[]{:S(2)}) copy-start(bf16[64,4,512]{2,1,0:T(4,128)(2,1)} %refs_1_.1) | copy-start | bytes 786436
  2.7 13.2 %copy-start.8 = (s32[64,32]{0,1:T(8,128)S(1)}, s32[64,32]{0,1:T(8,128)}, u32[]{:S(2)}) copy-start(s32[64,32]{0,1:T(8,128)} %param.16) | copy-start | bytes 24580
  2.7 1.9 collective-permute-start
  4.6 1.5 copy-start.1
  6.1 3.5 %copy-start.2 = (bf16[256,3584]{1,0:T(8,128)(2,1)S(1)}, bf16[256,3584]{1,0:T(8,128)(2,1)}, u32[]{:S(2)}) copy-start(bf16[256,3584]{1,0:T(8,128)(2,1)} %q.3) | copy-start | bytes 5505028
  6.1 9.8 %copy-start.3 = (bf16[64,4,3584]{2,1,0:T(4,128)(2,1)S(1)}, bf16[64,4,3584]{2,1,0:T(4,128)(2,1)}, u32[]{:S(2)}) copy-start(bf16[64,4,3584]{2,1,0:T(4,128)(2,1)} %refs_0_.1) | copy-start | bytes 5505028
  6.3 3.4 %collective-permute-start.5 = (bf16[256,1792]{1,0:T(8,128)(2,1)S(1)}, bf16[256,1792]{1,0:T(8,128)(2,1)S(1)}, u32[]{:S(2)}, u32[]{:S(2)}) collective-permute-start(bf16[256,1792]{1,0:T(8,128)(2,1)S(1)} %get-tuple-element.144), channel_id=1, source_target_pairs={{0,2},{2,0},{4,6},{6,4},{8,10},{10,8},{12,14},{14,12},{16,18},{18,... | collective-permute-start | bytes 2752520 | tf_op jit(solution)/shard_map/ppermute | solution.py:974
  6.7 7.8 %collective-permute-start.3 = (bf16[256,512]{1,0:T(8,128)(2,1)S(1)}, bf16[256,512]{1,0:T(8,128)(2,1)S(1)}, u32[]{:S(2)}, u32[]{:S(2)}) collective-permute-start(bf16[256,512]{1,0:T(8,128)(2,1)S(1)} %get-tuple-element.143.upper.refs_0_), channel_id=1, source_target_pairs={{0,8},{2,10},{8,16},{10,18},{16,24},{18,26},{24,28},{26,30},{28,20... | collective-permute-start | bytes 786440 | tf_op jit(solution)/shard_map/ppermute | solution.py:979
  6.9 7.6 %collective-permute-start.4 = (bf16[256,512]{1,0:T(8,128)(2,1)S(1)}, bf16[256,512]{1,0:T(8,128)(2,1)S(1)}, u32[]{:S(2)}, u32[]{:S(2)}) collective-permute-start(bf16[256,512]{1,0:T(8,128)(2,1)S(1)} %get-tuple-element.143.upper.refs_0_), channel_id=1, source_target_pairs={{0,4},{2,6},{8,0},{10,2},{16,8},{18,10},{24,16},{26,18},{28,24},{3... | collective-permute-start | bytes 786440 | tf_op jit(solution)/shard_map/ppermute | solution.py:982
  8.2 11.9 %collective-permute-start.1 = (bf16[256,512]{1,0:T(8,128)(2,1)S(1)}, bf16[256,512]{1,0:T(8,128)(2,1)S(1)}, u32[]{:S(2)}, u32[]{:S(2)}) collective-permute-start(bf16[256,512]{1,0:T(8,128)(2,1)S(1)} %get-tuple-element.142.lower.refs_1_), channel_id=1, source_target_pairs={{0,8},{2,10},{8,16},{10,18},{16,24},{18,26},{24,28},{26,30},{28,20... | collective-permute-start | bytes 786440 | tf_op jit(solution)/shard_map/ppermute | solution.py:983
  8.3 11.8 %collective-permute-start.2 = (bf16[256,512]{1,0:T(8,128)(2,1)S(1)}, bf16[256,512]{1,0:T(8,128)(2,1)S(1)}, u32[]{:S(2)}, u32[]{:S(2)}) collective-permute-start(bf16[256,512]{1,0:T(8,128)(2,1)S(1)} %get-tuple-element.142.lower.refs_1_), channel_id=1, source_target_pairs={{0,4},{2,6},{8,0},{10,2},{16,8},{18,10},{24,16},{26,18},{28,24},{3... | collective-permute-start | bytes 786440 | tf_op jit(solution)/shard_map/ppermute | solution.py:980
  14.5 13.6 %collective-permute-start.8 = (bf16[256,512]{1,0:T(8,128)(2,1)S(1)}, bf16[256,512]{1,0:T(8,128)(2,1)S(1)}, u32[]{:S(2)}, u32[]{:S(2)}) collective-permute-start(bf16[256,512]{1,0:T(8,128)(2,1)S(1)} %collective-permute-done.3.refs_0_.refs_2_), channel_id=1, source_target_pairs={{0,8},{2,10},{8,16},{10,18},{16,24},{18,26},{24,28},{26,30},{28,20... | collective-permute-start | bytes 786440 | tf_op jit(solution)/shard_map/ppermute | solution.py:979
  14.7 13.5 %collective-permute-start.9 = (bf16[256,512]{1,0:T(8,128)(2,1)S(1)}, bf16[256,512]{1,0:T(8,128)(2,1)S(1)}, u32[]{:S(2)}, u32[]{:S(2)}) collective-permute-start(bf16[256,512]{1,0:T(8,128)(2,1)S(1)} %collective-permute-done.4.refs_2_.refs_4_), channel_id=1, source_target_pairs={{0,4},{2,6},{8,0},{10,2},{16,8},{18,10},{24,16},{26,18},{28,24},{3... | collective-permute-start | bytes 786440 | tf_op jit(solution)/shard_map/ppermute | solution.py:982
  20.1 11.2 %collective-permute-start.6 = (bf16[256,512]{1,0:T(8,128)(2,1)S(1)}, bf16[256,512]{1,0:T(8,128)(2,1)S(1)}, u32[]{:S(2)}, u32[]{:S(2)}) collective-permute-start(bf16[256,512]{1,0:T(8,128)(2,1)S(1)} %collective-permute-done.1.refs_1_.refs_3_), channel_id=1, source_target_pairs={{0,8},{2,10},{8,16},{10,18},{16,24},{18,26},{24,28},{26,30},{28,20... | collective-permute-start | bytes 786440 | tf_op jit(solution)/shard_map/ppermute | solution.py:983
  20.3 11.1 %collective-permute-start.7 = (bf16[256,512]{1,0:T(8,128)(2,1)S(1)}, bf16[256,512]{1,0:T(8,128)(2,1)S(1)}, u32[]{:S(2)}, u32[]{:S(2)}) collective-permute-start(bf16[256,512]{1,0:T(8,128)(2,1)S(1)} %collective-permute-done.2.refs_3_.refs_5_), channel_id=1, source_target_pairs={{0,4},{2,6},{8,0},{10,2},{16,8},{18,10},{24,16},{26,18},{28,24},{3... | collective-permute-start | bytes 786440 | tf_op jit(solution)/shard_map/ppermute | solution.py:980
  28.1 12.7 %copy-start = (bf16[3584,448]{0,1:T(8,128)(2,1)S(1)}, bf16[3584,448]{0,1:T(8,128)(2,1)}, u32[]{:S(2)}) copy-start(bf16[3584,448]{0,1:T(8,128)(2,1)} %param.17) | copy-start | bytes 9633796
  28.2 11.9 %collective-permute-start.12 = (bf16[256,512]{1,0:T(8,128)(2,1)S(1)}, bf16[256,512]{1,0:T(8,128)(2,1)S(1)}, u32[]{:S(2)}, u32[]{:S(2)}) collective-permute-start(bf16[256,512]{1,0:T(8,128)(2,1)S(1)} %collective-permute-done.8.refs_0_.refs_6_), channel_id=1, source_target_pairs={{0,8},{2,10},{8,16},{10,18},{16,24},{18,26},{24,28},{26,30},{28,20... | collective-permute-start | bytes 786440 | tf_op jit(solution)/shard_map/ppermute | solution.py:979
  29.0 11.0 %collective-permute-start.13 = (bf16[256,512]{1,0:T(8,128)(2,1)S(1)}, bf16[256,512]{1,0:T(8,128)(2,1)S(1)}, u32[]{:S(2)}, u32[]{:S(2)}) collective-permute-start(bf16[256,512]{1,0:T(8,128)(2,1)S(1)} %collective-permute-done.9.refs_2_.refs_8_), channel_id=1, source_target_pairs={{0,4},{2,6},{8,0},{10,2},{16,8},{18,10},{24,16},{26,18},{28,24},{3... | collective-permute-start | bytes 786440 | tf_op jit(solution)/shard_map/ppermute | solution.py:982
  31.3 9.5 %collective-permute-start.10 = (bf16[256,512]{1,0:T(8,128)(2,1)S(1)}, bf16[256,512]{1,0:T(8,128)(2,1)S(1)}, u32[]{:S(2)}, u32[]{:S(2)}) collective-permute-start(bf16[256,512]{1,0:T(8,128)(2,1)S(1)} %collective-permute-done.6.refs_1_.refs_7_), channel_id=1, source_target_pairs={{0,8},{2,10},{8,16},{10,18},{16,24},{18,26},{24,28},{26,30},{28,20... | collective-permute-start | bytes 786440 | tf_op jit(solution)/shard_map/ppermute | solution.py:983
  31.5 9.3 %collective-permute-start.11 = (bf16[256,512]{1,0:T(8,128)(2,1)S(1)}, bf16[256,512]{1,0:T(8,128)(2,1)S(1)}, u32[]{:S(2)}, u32[]{:S(2)}) collective-permute-start(bf16[256,512]{1,0:T(8,128)(2,1)S(1)} %collective-permute-done.7.refs_3_.refs_9_), channel_id=1, source_target_pairs={{0,4},{2,6},{8,0},{10,2},{16,8},{18,10},{24,16},{26,18},{28,24},{3... | collective-permute-start | bytes 786440 | tf_op jit(solution)/shard_map/ppermute | solution.py:980
  41.5 10.8 %collective-permute-start.14 = (bf16[448,1792]{1,0:T(8,128)(2,1)S(1)}, bf16[448,1792]{1,0:T(8,128)(2,1)S(1)}, u32[]{:S(2)}, u32[]{:S(2)}) collective-permute-start(bf16[448,1792]{1,0:T(8,128)(2,1)S(1)} %take.1), channel_id=1, source_target_pairs={{0,2},{2,0},{4,6},{6,4},{8,10},{10,8},{12,14},{14,12},{16,18},{18,... | collective-permute-start | bytes 4816904 | tf_op jit(solution)/shard_map/ppermute | solution.py:1007
  44.4 7.9 %collective-permute-start.16 = (bf16[256,512]{1,0:T(8,128)(2,1)S(1)}, bf16[256,512]{1,0:T(8,128)(2,1)S(1)}, u32[]{:S(2)}, u32[]{:S(2)}) collective-permute-start(bf16[256,512]{1,0:T(8,128)(2,1)S(1)} %collective-permute-done.12.refs_10_), channel_id=1, source_target_pairs={{0,8},{2,10},{8,16},{10,18},{16,24},{18,26},{24,28},{26,30},{28,20... | collective-permute-start | bytes 786440 | tf_op jit(solution)/shard_map/ppermute | solution.py:979
  44.6 7.7 %collective-permute-start.15 = (bf16[256,512]{1,0:T(8,128)(2,1)S(1)}, bf16[256,512]{1,0:T(8,128)(2,1)S(1)}, u32[]{:S(2)}, u32[]{:S(2)}) collective-permute-start(bf16[256,512]{1,0:T(8,128)(2,1)S(1)} %collective-permute-done.11.refs_13_), channel_id=1, source_target_pairs={{0,4},{2,6},{8,0},{10,2},{16,8},{18,10},{24,16},{26,18},{28,24},{3... | collective-permute-start | bytes 786440 | tf_op jit(solution)/shard_map/ppermute | solution.py:980
  61.1 154.6 %collective-permute-start.17 = (bf16[64,1792]{1,0:T(8,128)(2,1)S(1)}, bf16[64,1792]{1,0:T(8,128)(2,1)S(1)}, u32[]{:S(2)}, u32[]{:S(2)}) collective-permute-start(bf16[64,1792]{1,0:T(8,128)(2,1)S(1)} %late_decode.1.refs_0_), channel_id=1, source_target_pairs={{0,8},{2,10},{4,12},{6,14},{8,16},{10,18},{12,20},{14,22},{16,24},... | collective-permute-start | bytes 688136 | tf_op jit(solution)/shard_map/ppermute | solution.py:1015
  64.9 150.7 %collective-permute-start.18 = (bf16[64,1792]{1,0:T(8,128)(2,1)S(1)}, bf16[64,1792]{1,0:T(8,128)(2,1)S(1)}, u32[]{:S(2)}, u32[]{:S(2)}) collective-permute-start(bf16[64,1792]{1,0:T(8,128)(2,1)S(1)} %late_decode.1.refs_0_), channel_id=1, source_target_pairs={{0,16},{2,18},{4,20},{6,22},{8,24},{10,26},{12,28},{14,30},{16,0},... | collective-permute-start | bytes 688136 | tf_op jit(solution)/shard_map/ppermute | solution.py:1015
  64.9 150.7 %collective-permute-start.19 = (bf16[64,1792]{1,0:T(8,128)(2,1)S(1)}, bf16[64,1792]{1,0:T(8,128)(2,1)S(1)}, u32[]{:S(2)}, u32[]{:S(2)}) collective-permute-start(bf16[64,1792]{1,0:T(8,128)(2,1)S(1)} %late_decode.1.refs_0_), channel_id=1, source_target_pairs={{0,24},{2,26},{4,28},{6,30},{8,0},{10,2},{12,4},{14,6},{16,8},{18,... | collective-permute-start | bytes 688136 | tf_op jit(solution)/shard_map/ppermute | solution.py:1015
  215.7 5.9 %collective-permute-start.21 = (bf16[256,1792]{1,0:T(8,128)(2,1)S(1)}, bf16[256,1792]{1,0:T(8,128)(2,1)S(1)}, u32[]{:S(2)}, u32[]{:S(2)}) collective-permute-start(bf16[256,1792]{1,0:T(8,128)(2,1)S(1)} %get-tuple-element.265), channel_id=1, source_target_pairs={{0,2},{2,0},{4,6},{6,4},{8,10},{10,8},{12,14},{14,12},{16,18},{18,... | collective-permute-start | bytes 2752520 | tf_op jit(solution)/shard_map/ppermute | solution.py:1019
  219.4 3.7 %collective-permute-start.20 = (bf16[448,128]{1,0:T(8,128)(2,1)S(1)}, bf16[448,128]{1,0:T(8,128)(2,1)S(1)}, u32[]{:S(2)}, u32[]{:S(2)}) collective-permute-start(bf16[448,128]{1,0:T(8,128)(2,1)S(1)} %get-tuple-element.264), channel_id=1, source_target_pairs={{0,2},{1,3},{2,0},{3,1},{4,6},{5,7},{6,4},{7,5},{8,10},{9,11},{10,... | collective-permute-start | bytes 344072 | tf_op jit(solution)/shard_map/ppermute | solution.py:1028
  219.5 4.3 %collective-permute-start.22 = (bf16[448,128]{1,0:T(8,128)(2,1)S(1)}, bf16[448,128]{1,0:T(8,128)(2,1)S(1)}, u32[]{:S(2)}, u32[]{:S(2)}) collective-permute-start(bf16[448,128]{1,0:T(8,128)(2,1)S(1)} %get-tuple-element.270), channel_id=1, source_target_pairs={{0,1},{1,0},{2,3},{3,2},{4,5},{5,4},{6,7},{7,6},{8,9},{9,8},{10,11... | collective-permute-start | bytes 344072 | tf_op jit(solution)/shard_map/ppermute | solution.py:1028
  220.8 6.1 %collective-permute-start.23 = (bf16[448,128]{1,0:T(8,128)(2,1)S(1)}, bf16[448,128]{1,0:T(8,128)(2,1)S(1)}, u32[]{:S(2)}, u32[]{:S(2)}) collective-permute-start(bf16[448,128]{1,0:T(8,128)(2,1)S(1)} %get-tuple-element.271), channel_id=1, source_target_pairs={{0,3},{1,2},{2,1},{3,0},{4,7},{5,6},{6,5},{7,4},{8,11},{9,10},{10,... | collective-permute-start | bytes 344072 | tf_op jit(solution)/shard_map/ppermute | solution.py:1028

commit v2 on v1

--- a/solution.py
+++ b/solution.py
@@ -218,19 +218,26 @@
     return jnp.concatenate(both, axis=0)
 
 
-def add_block(tok, heads, q_at, keys, values, allowed, sums, fresh=False):
+def block_bias(first, base, tok, length, lengths):
+    start = start_of(first, lengths)
+    t = first + lax.broadcasted_iota(jnp.int32, (tok, HD), 0)
+    u = base + lax.broadcasted_iota(jnp.int32, (1, length), 1)
+    row = jnp.where(start_of(t, lengths) == start, 0.0, -jnp.inf)
+    return [jnp.concatenate([row] * (length // HD), axis=1), jnp.where(u >= start, 0.0, -jnp.inf)]
+
+
+def add_block(tok, heads, q_at, keys, values, biases, sums, old):
     length = keys.shape[1]
-    bias = None if allowed is None else jnp.where(allowed, 0.0, -jnp.inf)
     for j in range(0, heads, PAIR):
         some = min(PAIR, heads - j)
         s = dot_nn(q_at(j * tok, some * tok), keys) * FACTOR
-        if bias is not None:
+        for bias in biases:
             s = (s.reshape(some, tok, length) + bias[None]).reshape(some * tok, length)
         p = jnp.exp2(s)
         more = (fold(p, jnp.add), dot_nn(p.astype(jnp.bfloat16), values))
-        for ref, value in zip(sums, more):
-            here = slice(j * tok, (j + some) * tok)
-            ref[here] = value if fresh else ref[here] + value
+        here = slice(j * tok, (j + some) * tok)
+        for i in range(2):
+            sums[i][here] = more[i] if old is None else old[i][here] + more[i]
 
 
 def relation(meta, part, side, tok, lengths):
@@ -263,8 +270,9 @@
             allowed = allowed_at(first, meta[CHIP] * 2 * tok, tok, length, lengths)
             here = side_rows(side, heads, tok)
             q_at = lambda at, count: qs[g, pl.ds(side * rows + at, count)]
-            add_block(tok, heads, q_at, keys[:, :length], values[:length], allowed,
-                      (total.at[g, here], acc.at[g, here]), True)
+            bias = jnp.where(allowed, 0.0, -jnp.inf)
+            add_block(tok, heads, q_at, keys[:, :length], values[:length], [bias],
+                      (total.at[g, here], acc.at[g, here]), None)
 
 
 def open_sums(q, q_near, block, meta, lengths):
@@ -285,36 +293,43 @@
     )(meta, lengths, q, q_near, *block)
 
 
-def stage_body(tok, heads, groups, first_part, meta, lengths, qs, before, pair, total, acc, held):
-    for i in range(2):
-        held[0][i], held[1][i] = pair[2 * i][...], pair[2 * i + 1][...]
-    total[...], acc[...] = before[0][...], before[1][...]
-
-    @pl.loop(0, 4 * groups)
-    def _(step):
-        which, rest = lax.div(step, 2 * groups), lax.rem(step, 2 * groups)
-        g, side = lax.div(rest, 2), lax.rem(rest, 2)
-        relevant, clear, first, base = relation(meta, first_part + which, side, tok, lengths)
-        here = side_rows(side, heads, tok)
-        sums = (total.at[g, here], acc.at[g, here])
-        at = side * (heads * tok)
-        q_at = lambda off, count: qs[g, pl.ds(pl.multiple_of(at + off, HD), count)]
-        upper, lower = held[0].at[which], held[1].at[which]
-
-        @pl.when(relevant & clear)
-        def _():
-            add_block(tok, heads, q_at, keys_of(upper, g), values_of(lower, g), None, sums)
-
-        @pl.when(relevant & jnp.logical_not(clear))
-        def _():
-            allowed = allowed_at(first, base, tok, 2 * tok, lengths)
-            add_block(tok, heads, q_at, keys_of(upper, g), values_of(lower, g), allowed, sums)
+def stage_body(tok, heads, groups, first_part, meta, lengths, qs, before, pair, total, acc):
+    for which in range(2):
+        upper, lower = pair[2 * which], pair[2 * which + 1]
+
+        @pl.loop(0, 2 * groups)
+        def _(step):
+            g, side = lax.div(step, 2), lax.rem(step, 2)
+            relevant, clear, first, base = relation(meta, first_part + which, side, tok, lengths)
+            here = side_rows(side, heads, tok)
+            sums = (total.at[g, here], acc.at[g, here])
+            old = sums if which else [ref.at[g, here] for ref in before]
+            at = side * (heads * tok)
+            q_at = lambda off, count: qs[g, pl.ds(pl.multiple_of(at + off, HD), count)]
+
+            @pl.when(relevant & clear)
+            def _():
+                add_block(tok, heads, q_at, keys_of(upper, g), values_of(lower, g), [], sums, old)
+
+            @pl.when(relevant & jnp.logical_not(clear))
+            def _():
+                biases = block_bias(first, base, tok, 2 * tok, lengths)
+                add_block(
+                    tok, heads, q_at, keys_of(upper, g), values_of(lower, g), biases, sums, old
+                )
+
+            if which == 0:
+
+                @pl.when(jnp.logical_not(relevant))
+                def _():
+                    for i in range(2):
+                        sums[i][...] = old[i][...]
 
 
 def stage_kernel(tok, heads, groups, first_part, meta, lengths, qs, total_in, acc_in, *refs):
-    pair, (total, acc), held = refs[:4], refs[4:6], refs[6:]
+    pair, (total, acc) = refs[:4], refs[4:]
     before = (total_in, acc_in)
-    stage_body(tok, heads, groups, first_part, meta, lengths, qs, before, pair, total, acc, held)
+    stage_body(tok, heads, groups, first_part, meta, lengths, qs, before, pair, total, acc)
 
 
 def stage(state, pair, first_part, meta, lengths):
@@ -327,7 +342,6 @@
         out_shape=[jax.ShapeDtypeStruct(x.shape, x.dtype) for x in (total, acc)],
         in_specs=[SMEM, SMEM] + [VMEM] * 7,
         out_specs=[VMEM] * 2,
-        scratch_shapes=[pltpu.VMEM((2, *x.shape), x.dtype) for x in pair[0]],
         input_output_aliases={3: 0, 4: 1},
         compiler_params=pltpu.CompilerParams(vmem_limit_bytes=ROOM),
         cost_estimate=BRIEF,
@@ -374,12 +388,14 @@
 
             @pl.when(relevant & clear)
             def _():
-                add_block(tok, heads, q_at, keys_of(upper, g), values_of(lower, g), None, sums)
+                add_block(tok, heads, q_at, keys_of(upper, g), values_of(lower, g), [], sums, sums)
 
             @pl.when(relevant & jnp.logical_not(clear))
             def _():
-                allowed = allowed_at(first, base, tok, 2 * tok, lengths)
-                add_block(tok, heads, q_at, keys_of(upper, g), values_of(lower, g), allowed, sums)
+                biases = block_bias(first, base, tok, 2 * tok, lengths)
+                add_block(
+                    tok, heads, q_at, keys_of(upper, g), values_of(lower, g), biases, sums, sums
+                )
 
         return fine & write(turn, g).astype(jnp.int32)
 

time: 231 us -> 232 us (level)
  Pallas kernels: 188 us -> 183 us
  waiting for transfers between devices: 10.5 us -> 15.1 us
  starting transfers between devices: 23.6 us -> 27.8 us
    pallas_call x2, Pallas kernels: 13.8 us -> 8.06 us  [stage(): pl.pallas_call(functools.partial(stage_kernel, tok, rows // (2 * tok), gr...]
    ppermute x3, starting transfers between devices: 3.79 us -> 7.93 us  [split_heads(): held_k[d] = lax.ppermute(held_k[d - 1], 'seq', down)]
    ppermute x3, waiting for transfers between devices: 2.99 us -> 6.76 us  [split_heads(): held_v[-d] = lax.ppermute(held_v[1 - d], 'seq', up)]
    ppermute x4, starting transfers between devices: 5.17 us -> 8.42 us  [split_heads(): held_v[d] = lax.ppermute(held_v[d - 1], 'seq', down)]
    ppermute x3, starting transfers between devices: 5.13 us -> 2.58 us  [split_heads(): pieces.append(lax.ppermute(attn_own, 'seq', perm))]
  transfers between devices with their start and end apart: 24 -> 24, of which waited for: 8 -> 8; matrix products, arithmetic and copies ran while one was open for 0% -> 0% of each run, Pallas kernels for 78% -> 75%
where the time goes in v2:
time: 232 us; the launch traced here: 231 us
  Pallas kernels  183 us (79%)
  starting transfers between devices  27.8 us (12%)
  waiting for transfers between devices  15.1 us (7%)
  local copies, waits for them, and re-layouts  4.4 us (2%)
    pallas_call x1, Pallas kernels, finish(): pl.pallas_call(functools.partial(finish_kernel, tok, heads, groups, done)...  149 us
    pallas_call x1, Pallas kernels, late_decode(): pl.pallas_call(functools.partial(late_kernel, own, steps, heads, groups,...  8.76 us
    ppermute x4, starting transfers between devices, split_heads(): held_v[d] = lax.ppermute(held_v[d - 1], 'seq', down)  8.42 us
    pallas_call x2, Pallas kernels, stage(): pl.pallas_call(functools.partial(stage_kernel, tok, rows // (2 * tok), gr...  8.06 us
    ppermute x3, starting transfers between devices, split_heads(): held_k[d] = lax.ppermute(held_k[d - 1], 'seq', down)  7.93 us
    ppermute x3, waiting for transfers between devices, split_heads(): held_v[-d] = lax.ppermute(held_v[1 - d], 'seq', up)  6.76 us
  transfers between devices with their start and end apart: 24, of which 8 were waited for; matrix products, arithmetic and copies ran while one was open for 0% of the time, Pallas kernels for 75%

profile of v2, /device:TPU:21, one launch (start us, length us, event | category | flops | bytes accessed | tf_op | source)
XLA Modules:
  0.0 231.0 jit_solution(14501353087922853775)
XLA Ops:
  0.7 0.9 copy-done.4
  1.6 0.9 copy-done.5
  2.6 0.1 prepare.1
  2.7 0.7 collective-permute-start
  3.5 0.1 stack.60.meta
  3.6 1.1 collective-permute-done.theirs
  4.6 1.5 copy-done.1
  6.1 0.1 join.1
  6.3 0.4 collective-permute-start.5
  6.7 0.2 collective-permute-start.3
  6.9 1.3 collective-permute-start.4
  8.2 0.2 collective-permute-start.1
  8.3 1.3 collective-permute-start.2
  9.7 4.6 %open.1 = (bf16[2,3584,128]{2,1,0:T(8,128)(2,1)S(1)}, f32[2,3584,128]{2,1,0:T(8,128)S(1)}, f32[2,3584,128]{2,1,0:T(8,128)S(1)}) custom-call(s32[15]{0:T(128)S(1)} %stack.60.meta, s32[3]{0:T(128)S(1)} %copy-done.9, bf16[256,3584]{1,0:T(8,128)(2,1)S(1)} %copy-done.2, bf16[256,1792]{1,0:T(8,128)(2,1)S(1)} %collective-permute-done.5.q_near, ...), custom_call_target="tpu_custom_call" | custom-call | flops 1024 | bytes 1024 | tf_op jit(solution)/shard_map/open/pallas_call | solution.py:285
  14.3 0.2 collective-permute-done.3.refs_0_.refs_2_
  14.5 0.2 collective-permute-start.8
  14.7 1.3 collective-permute-start.9
  16.0 3.0 %requests.1 = (f32[2,448,128]{2,1,0:T(8,128)S(1)}, f32[2,448,128]{2,1,0:T(8,128)S(1)}, bf16[2,448,128]{2,1,0:T(8,128)(2,1)S(1)}, bf16[64,256]{1,0:T(8,128)(2,1)S...) custom-call(s32[15]{0:T(128)S(1)} %stack.60.meta, bf16[64,4,3584]{2,1,0:T(4,128)(2,1)S(1)} %copy-done.3, ...), custom_call_target="tpu_custom_call" | custom-call | flops 1024 | bytes 1024 | tf_op jit(solution)/shard_map/requests/pallas_call | solution.py:550
  19.0 1.1 collective-permute-done.1.refs_1_.refs_3_
  20.1 0.2 collective-permute-start.6
  20.3 1.3 collective-permute-start.7
  21.6 6.4 %stage1.1 = (f32[2,3584,128]{2,1,0:T(8,128)S(1)}, f32[2,3584,128]{2,1,0:T(8,128)S(1)}) custom-call(s32[15]{0:T(128)S(1)} %stack.60.meta, s32[3]{0:T(128)S(1)} %copy-done.9, bf16[2,3584,128]{2,1,0:T(8,128)(2,1)S(1)} %get-tuple-element.254.qs, f32[2,3584,128]{2,1,0:T(8,128)S(1)} %get-tuple-element.166.total_in, ...), custom_call_target="tpu_custom_call", output_to_operand_aliasing={{0}: (3, {}), {1}: (4, {})} | custom-call | flops 1024 | bytes 1024 | tf_op jit(solution)/shard_map/stage1/pallas_call | solution.py:340
  28.0 0.1 collective-permute-start.12
  28.1 5.3 %collective-permute-start.13 = (bf16[256,512]{1,0:T(8,128)(2,1)S(1)}, bf16[256,512]{1,0:T(8,128)(2,1)S(1)}, u32[]{:S(2)}, u32[]{:S(2)}) collective-permute-start(bf16[256,512]{1,0:T(8,128)(2,1)S(1)} %collective-permute-done.9.refs_2_.refs_8_), channel_id=1, source_target_pairs={{0,4},{2,6},{8,0},{10,2},{16,8},{18,10},{24,16},{26,18},{28,24},{3... | collective-permute-start | bytes 786440 | tf_op jit(solution)/shard_map/ppermute | solution.py:998
  33.4 1.6 collective-permute-start.11
  35.1 1.6 stage3.1
  36.7 0.7 collective-permute-done.12.refs_10_
  37.4 5.6 %collective-permute-done.10.refs_11_ = bf16[256,512]{1,0:T(8,128)(2,1)S(1)} collective-permute-done((bf16[256,512]{1,0:T(8,128)(2,1)S(1)}, bf16[256,512]{1,0:T(8,128)(2,1)S(1)}, u32[]{:S(2)}, u32[]{:S(2)}) %collective-permute-start.10) | collective-permute-done | bytes 262176 | tf_op jit(solution)/shard_map/ppermute | solution.py:999
  43.1 0.7 take.1
  43.7 3.3 %collective-permute-start.14 = (bf16[448,1792]{1,0:T(8,128)(2,1)S(1)}, bf16[448,1792]{1,0:T(8,128)(2,1)S(1)}, u32[]{:S(2)}, u32[]{:S(2)}) collective-permute-start(bf16[448,1792]{1,0:T(8,128)(2,1)S(1)} %take.1), channel_id=1, source_target_pairs={{0,2},{2,0},{4,6},{6,4},{8,10},{10,8},{12,14},{14,12},{16,18},{18,... | collective-permute-start | bytes 4816904 | tf_op jit(solution)/shard_map/ppermute | solution.py:1023
  47.0 4.2 %collective-permute-start.15 = (bf16[256,512]{1,0:T(8,128)(2,1)S(1)}, bf16[256,512]{1,0:T(8,128)(2,1)S(1)}, u32[]{:S(2)}, u32[]{:S(2)}) collective-permute-start(bf16[256,512]{1,0:T(8,128)(2,1)S(1)} %collective-permute-done.11.refs_13_), channel_id=1, source_target_pairs={{0,4},{2,6},{8,0},{10,2},{16,8},{18,10},{24,16},{26,18},{28,24},{3... | collective-permute-start | bytes 786440 | tf_op jit(solution)/shard_map/ppermute | solution.py:996
  51.2 4.0 %early_decode.1 = (f32[2,448,128]{2,1,0:T(8,128)S(1)}, f32[2,448,128]{2,1,0:T(8,128)S(1)}) custom-call(f32[2,448,128]{2,1,0:T(8,128)S(1)} %get-tuple-element.218.total_in, f32[2,448,128]{2,1,0:T(8,128)S(1)} %get-tuple-element.219.acc_in, bf16[2,448,128]{2,1,0:T(8,128)(2,1)S(1)} %get-tuple-element.245.query, ...), custom_call_target="tpu_custom_call", output_to_operand_aliasing={{0}: (0, {}), {1}: (1, {})} | custom-call | flops 1024 | bytes 1024 | tf_op jit(solution)/shard_map/early_decode/pallas_call | solution.py:590
  55.2 2.6 %collective-permute-done.16.refs_14_ = bf16[256,512]{1,0:T(8,128)(2,1)S(1)} collective-permute-done((bf16[256,512]{1,0:T(8,128)(2,1)S(1)}, bf16[256,512]{1,0:T(8,128)(2,1)S(1)}, u32[]{:S(2)}, u32[]{:S(2)}) %collective-permute-start.16) | collective-permute-done | bytes 262176 | tf_op jit(solution)/shard_map/ppermute | solution.py:995
  57.8 8.8 %late_decode.1.refs_0_ = bf16[64,1792]{1,0:T(8,128)(2,1)S(1)} custom-call(s32[15]{0:T(128)S(1)} %stack.60.meta, f32[2,448,128]{2,1,0:T(8,128)S(1)} %get-tuple-element.243.total, f32[2,448,128]{2,1,0:T(8,128)S(1)} %get-tuple-element.244.acc, bf16[2,448,128]{2,1,0:T(8,128)(2,1)S(1)} %get-tuple-element.245.query, bf16[64,256]{1,0:T(8,128)(2,1)S(1)} %get-tuple-element.246.newk, ...), custom_call_target="tpu_custom_call" | custom-call | flops 469762048 | bytes 57344 | tf_op jit(solution)/shard_map/late_decode/pallas_call | solution.py:656
  66.6 1.3 collective-permute-start.17
  67.9 1.3 collective-permute-start.19
  69.1 149.5 %finish.1 = (bf16[256,1792]{1,0:T(8,128)(2,1)S(1)}, bf16[256,3584]{1,0:T(8,128)(2,1)}) custom-call(s32[15]{0:T(128)S(1)} %stack.60.meta, s32[3]{0:T(128)S(1)} %copy-done.9, bf16[2,3584,128]{2,1,0:T(8,128)(2,1)S(1)} %get-tuple-element.254.qs, f32[2,3584,128]{2,1,0:T(8,128)S(1)} %get-tuple-element.255.total, f32[2,3584,128]{2,1,0:T(8,128)S(1)} %get-tuple-element.256.acc, ...), custom_call_target="tpu_custom_call" | custom-call | flops 1879048192 | bytes 1835008 | tf_op jit(solution)/shard_map/finish/pallas_call | solution.py:449
  218.6 1.5 collective-permute-start.21
  220.1 2.4 %project.1 = (f32[448,128]{1,0:T(8,128)S(1)}, bf16[448,128]{1,0:T(8,128)(2,1)S(1)}, bf16[448,128]{1,0:T(8,128)(2,1)S(1)}, bf16[448,128]{1,0:T(8,128)(2,1)S(1)}) custom-call(s32[15]{0:T(128)S(1)} %stack.60.meta, bf16[64,1792]{1,0:T(8,128)(2,1)S(1)} %late_decode.1.refs_0_, bf16[64,1792]{1,0:T(8,128)(2,1)S(1)} %collective-permute-done.17.refs_1_, ...), custom_call_target="tpu_custom_call" | custom-call | flops 822083584 | bytes 3211264 | tf_op jit(solution)/shard_map/project/pallas_call | solution.py:877
  222.5 0.1 collective-permute-start.20
  222.6 1.3 collective-permute-start.22
  223.9 0.9 collective-permute-start.23
  224.7 1.5 settle.1
  226.2 0.7 collective-permute-done.22
  227.0 3.0 %collective-permute-done.23 = bf16[448,128]{1,0:T(8,128)(2,1)S(1)} collective-permute-done((bf16[448,128]{1,0:T(8,128)(2,1)S(1)}, bf16[448,128]{1,0:T(8,128)(2,1)S(1)}, u32[]{:S(2)}, u32[]{:S(2)}) %collective-permute-start.23) | collective-permute-done | bytes 114720 | tf_op jit(solution)/shard_map/ppermute | solution.py:1044
  230.0 0.1 fusion
  230.1 0.1 copy.20
  230.2 0.8 copy.22
  (37 shorter events, 0.1 us)
Async XLA Ops:
  0.6 9.0 %copy-start.9 = (s32[3]{0:T(128)S(1)}, s32[3]{0:T(128)}, u32[]{:S(2)}) copy-start(s32[3]{0:T(128)} %lengths.7) | copy-start | bytes 40
  0.6 1.0 copy-start.4
  1.6 0.9 copy-start.5
  2.5 13.4 %copy-start.7 = (bf16[64,4,512]{2,1,0:T(4,128)(2,1)S(1)}, bf16[64,4,512]{2,1,0:T(4,128)(2,1)}, u32[]{:S(2)}) copy-start(bf16[64,4,512]{2,1,0:T(4,128)(2,1)} %refs_2_.1) | copy-start | bytes 786436
  2.7 13.2 %copy-start.6 = (bf16[64,4,512]{2,1,0:T(4,128)(2,1)S(1)}, bf16[64,4,512]{2,1,0:T(4,128)(2,1)}, u32[]{:S(2)}) copy-start(bf16[64,4,512]{2,1,0:T(4,128)(2,1)} %refs_1_.1) | copy-start | bytes 786436
  2.7 13.2 %copy-start.8 = (s32[64,32]{0,1:T(8,128)S(1)}, s32[64,32]{0,1:T(8,128)}, u32[]{:S(2)}) copy-start(s32[64,32]{0,1:T(8,128)} %param.16) | copy-start | bytes 24580
  2.7 1.9 collective-permute-start
  4.6 1.5 copy-start.1
  6.1 3.5 %copy-start.2 = (bf16[256,3584]{1,0:T(8,128)(2,1)S(1)}, bf16[256,3584]{1,0:T(8,128)(2,1)}, u32[]{:S(2)}) copy-start(bf16[256,3584]{1,0:T(8,128)(2,1)} %q.3) | copy-start | bytes 5505028
  6.1 9.8 %copy-start.3 = (bf16[64,4,3584]{2,1,0:T(4,128)(2,1)S(1)}, bf16[64,4,3584]{2,1,0:T(4,128)(2,1)}, u32[]{:S(2)}) copy-start(bf16[64,4,3584]{2,1,0:T(4,128)(2,1)} %refs_0_.1) | copy-start | bytes 5505028
  6.3 3.4 %collective-permute-start.5 = (bf16[256,1792]{1,0:T(8,128)(2,1)S(1)}, bf16[256,1792]{1,0:T(8,128)(2,1)S(1)}, u32[]{:S(2)}, u32[]{:S(2)}) collective-permute-start(bf16[256,1792]{1,0:T(8,128)(2,1)S(1)} %get-tuple-element.144), channel_id=1, source_target_pairs={{0,2},{2,0},{4,6},{6,4},{8,10},{10,8},{12,14},{14,12},{16,18},{18,... | collective-permute-start | bytes 2752520 | tf_op jit(solution)/shard_map/ppermute | solution.py:990
  6.7 7.8 %collective-permute-start.3 = (bf16[256,512]{1,0:T(8,128)(2,1)S(1)}, bf16[256,512]{1,0:T(8,128)(2,1)S(1)}, u32[]{:S(2)}, u32[]{:S(2)}) collective-permute-start(bf16[256,512]{1,0:T(8,128)(2,1)S(1)} %get-tuple-element.143.upper.refs_0_), channel_id=1, source_target_pairs={{0,8},{2,10},{8,16},{10,18},{16,24},{18,26},{24,28},{26,30},{28,20... | collective-permute-start | bytes 786440 | tf_op jit(solution)/shard_map/ppermute | solution.py:995
  6.9 7.6 %collective-permute-start.4 = (bf16[256,512]{1,0:T(8,128)(2,1)S(1)}, bf16[256,512]{1,0:T(8,128)(2,1)S(1)}, u32[]{:S(2)}, u32[]{:S(2)}) collective-permute-start(bf16[256,512]{1,0:T(8,128)(2,1)S(1)} %get-tuple-element.143.upper.refs_0_), channel_id=1, source_target_pairs={{0,4},{2,6},{8,0},{10,2},{16,8},{18,10},{24,16},{26,18},{28,24},{3... | collective-permute-start | bytes 786440 | tf_op jit(solution)/shard_map/ppermute | solution.py:998
  8.2 11.9 %collective-permute-start.1 = (bf16[256,512]{1,0:T(8,128)(2,1)S(1)}, bf16[256,512]{1,0:T(8,128)(2,1)S(1)}, u32[]{:S(2)}, u32[]{:S(2)}) collective-permute-start(bf16[256,512]{1,0:T(8,128)(2,1)S(1)} %get-tuple-element.142.lower.refs_1_), channel_id=1, source_target_pairs={{0,8},{2,10},{8,16},{10,18},{16,24},{18,26},{24,28},{26,30},{28,20... | collective-permute-start | bytes 786440 | tf_op jit(solution)/shard_map/ppermute | solution.py:999
  8.3 11.8 %collective-permute-start.2 = (bf16[256,512]{1,0:T(8,128)(2,1)S(1)}, bf16[256,512]{1,0:T(8,128)(2,1)S(1)}, u32[]{:S(2)}, u32[]{:S(2)}) collective-permute-start(bf16[256,512]{1,0:T(8,128)(2,1)S(1)} %get-tuple-element.142.lower.refs_1_), channel_id=1, source_target_pairs={{0,4},{2,6},{8,0},{10,2},{16,8},{18,10},{24,16},{26,18},{28,24},{3... | collective-permute-start | bytes 786440 | tf_op jit(solution)/shard_map/ppermute | solution.py:996
  14.5 13.5 %collective-permute-start.8 = (bf16[256,512]{1,0:T(8,128)(2,1)S(1)}, bf16[256,512]{1,0:T(8,128)(2,1)S(1)}, u32[]{:S(2)}, u32[]{:S(2)}) collective-permute-start(bf16[256,512]{1,0:T(8,128)(2,1)S(1)} %collective-permute-done.3.refs_0_.refs_2_), channel_id=1, source_target_pairs={{0,8},{2,10},{8,16},{10,18},{16,24},{18,26},{24,28},{26,30},{28,20... | collective-permute-start | bytes 786440 | tf_op jit(solution)/shard_map/ppermute | solution.py:995
  14.7 13.4 %collective-permute-start.9 = (bf16[256,512]{1,0:T(8,128)(2,1)S(1)}, bf16[256,512]{1,0:T(8,128)(2,1)S(1)}, u32[]{:S(2)}, u32[]{:S(2)}) collective-permute-start(bf16[256,512]{1,0:T(8,128)(2,1)S(1)} %collective-permute-done.4.refs_2_.refs_4_), channel_id=1, source_target_pairs={{0,4},{2,6},{8,0},{10,2},{16,8},{18,10},{24,16},{26,18},{28,24},{3... | collective-permute-start | bytes 786440 | tf_op jit(solution)/shard_map/ppermute | solution.py:998
  20.1 13.3 %collective-permute-start.6 = (bf16[256,512]{1,0:T(8,128)(2,1)S(1)}, bf16[256,512]{1,0:T(8,128)(2,1)S(1)}, u32[]{:S(2)}, u32[]{:S(2)}) collective-permute-start(bf16[256,512]{1,0:T(8,128)(2,1)S(1)} %collective-permute-done.1.refs_1_.refs_3_), channel_id=1, source_target_pairs={{0,8},{2,10},{8,16},{10,18},{16,24},{18,26},{24,28},{26,30},{28,20... | collective-permute-start | bytes 786440 | tf_op jit(solution)/shard_map/ppermute | solution.py:999
  20.3 13.2 %collective-permute-start.7 = (bf16[256,512]{1,0:T(8,128)(2,1)S(1)}, bf16[256,512]{1,0:T(8,128)(2,1)S(1)}, u32[]{:S(2)}, u32[]{:S(2)}) collective-permute-start(bf16[256,512]{1,0:T(8,128)(2,1)S(1)} %collective-permute-done.2.refs_3_.refs_5_), channel_id=1, source_target_pairs={{0,4},{2,6},{8,0},{10,2},{16,8},{18,10},{24,16},{26,18},{28,24},{3... | collective-permute-start | bytes 786440 | tf_op jit(solution)/shard_map/ppermute | solution.py:996
  28.0 15.0 %copy-start = (bf16[3584,448]{0,1:T(8,128)(2,1)S(1)}, bf16[3584,448]{0,1:T(8,128)(2,1)}, u32[]{:S(2)}) copy-start(bf16[3584,448]{0,1:T(8,128)(2,1)} %param.17) | copy-start | bytes 9633796
  28.0 9.4 %collective-permute-start.12 = (bf16[256,512]{1,0:T(8,128)(2,1)S(1)}, bf16[256,512]{1,0:T(8,128)(2,1)S(1)}, u32[]{:S(2)}, u32[]{:S(2)}) collective-permute-start(bf16[256,512]{1,0:T(8,128)(2,1)S(1)} %collective-permute-done.8.refs_0_.refs_6_), channel_id=1, source_target_pairs={{0,8},{2,10},{8,16},{10,18},{16,24},{18,26},{24,28},{26,30},{28,20... | collective-permute-start | bytes 786440 | tf_op jit(solution)/shard_map/ppermute | solution.py:995
  28.1 9.3 %collective-permute-start.13 = (bf16[256,512]{1,0:T(8,128)(2,1)S(1)}, bf16[256,512]{1,0:T(8,128)(2,1)S(1)}, u32[]{:S(2)}, u32[]{:S(2)}) collective-permute-start(bf16[256,512]{1,0:T(8,128)(2,1)S(1)} %collective-permute-done.9.refs_2_.refs_8_), channel_id=1, source_target_pairs={{0,4},{2,6},{8,0},{10,2},{16,8},{18,10},{24,16},{26,18},{28,24},{3... | collective-permute-start | bytes 786440 | tf_op jit(solution)/shard_map/ppermute | solution.py:998
  33.4 9.6 %collective-permute-start.10 = (bf16[256,512]{1,0:T(8,128)(2,1)S(1)}, bf16[256,512]{1,0:T(8,128)(2,1)S(1)}, u32[]{:S(2)}, u32[]{:S(2)}) collective-permute-start(bf16[256,512]{1,0:T(8,128)(2,1)S(1)} %collective-permute-done.6.refs_1_.refs_7_), channel_id=1, source_target_pairs={{0,8},{2,10},{8,16},{10,18},{16,24},{18,26},{24,28},{26,30},{28,20... | collective-permute-start | bytes 786440 | tf_op jit(solution)/shard_map/ppermute | solution.py:999
  33.4 9.6 %collective-permute-start.11 = (bf16[256,512]{1,0:T(8,128)(2,1)S(1)}, bf16[256,512]{1,0:T(8,128)(2,1)S(1)}, u32[]{:S(2)}, u32[]{:S(2)}) collective-permute-start(bf16[256,512]{1,0:T(8,128)(2,1)S(1)} %collective-permute-done.7.refs_3_.refs_9_), channel_id=1, source_target_pairs={{0,4},{2,6},{8,0},{10,2},{16,8},{18,10},{24,16},{26,18},{28,24},{3... | collective-permute-start | bytes 786440 | tf_op jit(solution)/shard_map/ppermute | solution.py:996
  43.7 14.1 %collective-permute-start.14 = (bf16[448,1792]{1,0:T(8,128)(2,1)S(1)}, bf16[448,1792]{1,0:T(8,128)(2,1)S(1)}, u32[]{:S(2)}, u32[]{:S(2)}) collective-permute-start(bf16[448,1792]{1,0:T(8,128)(2,1)S(1)} %take.1), channel_id=1, source_target_pairs={{0,2},{2,0},{4,6},{6,4},{8,10},{10,8},{12,14},{14,12},{16,18},{18,... | collective-permute-start | bytes 4816904 | tf_op jit(solution)/shard_map/ppermute | solution.py:1023
  47.0 10.8 %collective-permute-start.16 = (bf16[256,512]{1,0:T(8,128)(2,1)S(1)}, bf16[256,512]{1,0:T(8,128)(2,1)S(1)}, u32[]{:S(2)}, u32[]{:S(2)}) collective-permute-start(bf16[256,512]{1,0:T(8,128)(2,1)S(1)} %collective-permute-done.12.refs_10_), channel_id=1, source_target_pairs={{0,8},{2,10},{8,16},{10,18},{16,24},{18,26},{24,28},{26,30},{28,20... | collective-permute-start | bytes 786440 | tf_op jit(solution)/shard_map/ppermute | solution.py:995
  47.0 10.8 %collective-permute-start.15 = (bf16[256,512]{1,0:T(8,128)(2,1)S(1)}, bf16[256,512]{1,0:T(8,128)(2,1)S(1)}, u32[]{:S(2)}, u32[]{:S(2)}) collective-permute-start(bf16[256,512]{1,0:T(8,128)(2,1)S(1)} %collective-permute-done.11.refs_13_), channel_id=1, source_target_pairs={{0,4},{2,6},{8,0},{10,2},{16,8},{18,10},{24,16},{26,18},{28,24},{3... | collective-permute-start | bytes 786440 | tf_op jit(solution)/shard_map/ppermute | solution.py:996
  66.6 152.0 %collective-permute-start.17 = (bf16[64,1792]{1,0:T(8,128)(2,1)S(1)}, bf16[64,1792]{1,0:T(8,128)(2,1)S(1)}, u32[]{:S(2)}, u32[]{:S(2)}) collective-permute-start(bf16[64,1792]{1,0:T(8,128)(2,1)S(1)} %late_decode.1.refs_0_), channel_id=1, source_target_pairs={{0,8},{2,10},{4,12},{6,14},{8,16},{10,18},{12,20},{14,22},{16,24},... | collective-permute-start | bytes 688136 | tf_op jit(solution)/shard_map/ppermute | solution.py:1031
  67.9 150.7 %collective-permute-start.18 = (bf16[64,1792]{1,0:T(8,128)(2,1)S(1)}, bf16[64,1792]{1,0:T(8,128)(2,1)S(1)}, u32[]{:S(2)}, u32[]{:S(2)}) collective-permute-start(bf16[64,1792]{1,0:T(8,128)(2,1)S(1)} %late_decode.1.refs_0_), channel_id=1, source_target_pairs={{0,16},{2,18},{4,20},{6,22},{8,24},{10,26},{12,28},{14,30},{16,0},... | collective-permute-start | bytes 688136 | tf_op jit(solution)/shard_map/ppermute | solution.py:1031
  67.9 150.7 %collective-permute-start.19 = (bf16[64,1792]{1,0:T(8,128)(2,1)S(1)}, bf16[64,1792]{1,0:T(8,128)(2,1)S(1)}, u32[]{:S(2)}, u32[]{:S(2)}) collective-permute-start(bf16[64,1792]{1,0:T(8,128)(2,1)S(1)} %late_decode.1.refs_0_), channel_id=1, source_target_pairs={{0,24},{2,26},{4,28},{6,30},{8,0},{10,2},{12,4},{14,6},{16,8},{18,... | collective-permute-start | bytes 688136 | tf_op jit(solution)/shard_map/ppermute | solution.py:1031
  218.6 6.1 %collective-permute-start.21 = (bf16[256,1792]{1,0:T(8,128)(2,1)S(1)}, bf16[256,1792]{1,0:T(8,128)(2,1)S(1)}, u32[]{:S(2)}, u32[]{:S(2)}) collective-permute-start(bf16[256,1792]{1,0:T(8,128)(2,1)S(1)} %get-tuple-element.265), channel_id=1, source_target_pairs={{0,2},{2,0},{4,6},{6,4},{8,10},{10,8},{12,14},{14,12},{16,18},{18,... | collective-permute-start | bytes 2752520 | tf_op jit(solution)/shard_map/ppermute | solution.py:1035
  222.5 3.7 %collective-permute-start.20 = (bf16[448,128]{1,0:T(8,128)(2,1)S(1)}, bf16[448,128]{1,0:T(8,128)(2,1)S(1)}, u32[]{:S(2)}, u32[]{:S(2)}) collective-permute-start(bf16[448,128]{1,0:T(8,128)(2,1)S(1)} %get-tuple-element.264), channel_id=1, source_target_pairs={{0,2},{1,3},{2,0},{3,1},{4,6},{5,7},{6,4},{7,5},{8,10},{9,11},{10,... | collective-permute-start | bytes 344072 | tf_op jit(solution)/shard_map/ppermute | solution.py:1044
  222.6 4.3 %collective-permute-start.22 = (bf16[448,128]{1,0:T(8,128)(2,1)S(1)}, bf16[448,128]{1,0:T(8,128)(2,1)S(1)}, u32[]{:S(2)}, u32[]{:S(2)}) collective-permute-start(bf16[448,128]{1,0:T(8,128)(2,1)S(1)} %get-tuple-element.270), channel_id=1, source_target_pairs={{0,1},{1,0},{2,3},{3,2},{4,5},{5,4},{6,7},{7,6},{8,9},{9,8},{10,11... | collective-permute-start | bytes 344072 | tf_op jit(solution)/shard_map/ppermute | solution.py:1044
  223.9 6.1 %collective-permute-start.23 = (bf16[448,128]{1,0:T(8,128)(2,1)S(1)}, bf16[448,128]{1,0:T(8,128)(2,1)S(1)}, u32[]{:S(2)}, u32[]{:S(2)}) collective-permute-start(bf16[448,128]{1,0:T(8,128)(2,1)S(1)} %get-tuple-element.271), channel_id=1, source_target_pairs={{0,3},{1,2},{2,1},{3,0},{4,7},{5,6},{6,5},{7,4},{8,11},{9,10},{10,... | collective-permute-start | bytes 344072 | tf_op jit(solution)/shard_map/ppermute | solution.py:1044

commit v3 on v2

--- a/solution.py
+++ b/solution.py
@@ -228,14 +228,21 @@
 
 def add_block(tok, heads, q_at, keys, values, biases, sums, old):
     length = keys.shape[1]
-    for j in range(0, heads, PAIR):
-        some = min(PAIR, heads - j)
-        s = dot_nn(q_at(j * tok, some * tok), keys) * FACTOR
+    turns = [(j * tok, min(PAIR, heads - j)) for j in range(0, heads, PAIR)]
+
+    def score(at, some):
+        return dot_nn(q_at(at, some * tok), keys)
+
+    coming = score(*turns[0])
+    for number, (at, some) in enumerate(turns):
+        s = coming * FACTOR
+        if number + 1 < len(turns):
+            coming = score(*turns[number + 1])
         for bias in biases:
             s = (s.reshape(some, tok, length) + bias[None]).reshape(some * tok, length)
         p = jnp.exp2(s)
         more = (fold(p, jnp.add), dot_nn(p.astype(jnp.bfloat16), values))
-        here = slice(j * tok, (j + some) * tok)
+        here = slice(at, at + some * tok)
         for i in range(2):
             sums[i][here] = more[i] if old is None else old[i][here] + more[i]
 

time: 232 us -> 232 us (level)
  Pallas kernels: 183 us -> 191 us
  starting transfers between devices: 27.8 us -> 22 us
    pallas_call x1, Pallas kernels: 149 us -> 154 us  [finish(): pl.pallas_call(functools.partial(finish_kernel, tok, heads, groups, done)...]
    pallas_call x2, Pallas kernels: 8.06 us -> 12.5 us  [stage(): pl.pallas_call(functools.partial(stage_kernel, tok, rows // (2 * tok), gr...]
    ppermute x3, starting transfers between devices: 7.93 us -> 3.89 us  [split_heads(): held_k[d] = lax.ppermute(held_k[d - 1], 'seq', down)]
    ppermute x4, starting transfers between devices: 8.42 us -> 5.19 us  [split_heads(): held_v[d] = lax.ppermute(held_v[d - 1], 'seq', down)]
  transfers between devices with their start and end apart: 24 -> 24, of which waited for: 8 -> 8; matrix products, arithmetic and copies ran while one was open for 0% -> 0% of each run, Pallas kernels for 75% -> 78%
where the time goes in v3:
time: 232 us
  Pallas kernels  191 us (82%)
  starting transfers between devices  22 us (9%)
  waiting for transfers between devices  13.1 us (6%)
  local copies, waits for them, and re-layouts  4.4 us (2%)
    pallas_call x1, Pallas kernels, finish(): pl.pallas_call(functools.partial(finish_kernel, tok, heads, groups, done)...  154 us
    pallas_call x2, Pallas kernels, stage(): pl.pallas_call(functools.partial(stage_kernel, tok, rows // (2 * tok), gr...  12.5 us
    pallas_call x1, Pallas kernels, late_decode(): pl.pallas_call(functools.partial(late_kernel, own, steps, heads, groups,...  8.76 us
    ppermute x3, waiting for transfers between devices, split_heads(): held_v[-d] = lax.ppermute(held_v[1 - d], 'seq', up)  5.33 us
    ppermute x4, starting transfers between devices, split_heads(): held_v[d] = lax.ppermute(held_v[d - 1], 'seq', down)  5.19 us
  transfers between devices with their start and end apart: 24, of which 8 were waited for; matrix products, arithmetic and copies ran while one was open for 0% of the time, Pallas kernels for 78%

profile of v3, /device:TPU:21, one launch (start us, length us, event | category | flops | bytes accessed | tf_op | source)
XLA Modules:
  0.0 231.8 jit_solution(16470710673248259496)
XLA Ops:
  0.7 0.9 copy-done.4
  1.6 0.9 copy-done.5
  2.6 0.1 prepare.1
  2.7 0.7 collective-permute-start
  3.6 1.1 collective-permute-done.theirs
  4.6 1.5 copy-done.1
  6.1 0.1 join.1
  6.3 0.4 collective-permute-start.5
  6.7 0.2 collective-permute-start.3
  6.9 1.3 collective-permute-start.4
  8.2 0.2 collective-permute-start.1
  8.3 1.3 collective-permute-start.2
  9.7 4.3 %open.1 = (bf16[2,3584,128]{2,1,0:T(8,128)(2,1)S(1)}, f32[2,3584,128]{2,1,0:T(8,128)S(1)}, f32[2,3584,128]{2,1,0:T(8,128)S(1)}) custom-call(s32[15]{0:T(128)S(1)} %stack.60.meta, s32[3]{0:T(128)S(1)} %copy-done.9, bf16[256,3584]{1,0:T(8,128)(2,1)S(1)} %copy-done.2, bf16[256,1792]{1,0:T(8,128)(2,1)S(1)} %collective-permute-done.5.q_near, ...), custom_call_target="tpu_custom_call" | custom-call | flops 1024 | bytes 1024 | tf_op jit(solution)/shard_map/open/pallas_call | solution.py:292
  14.0 0.5 collective-permute-done.3.refs_0_.refs_2_
  14.5 0.2 collective-permute-start.8
  14.7 1.3 collective-permute-start.9
  16.0 3.0 %requests.1 = (f32[2,448,128]{2,1,0:T(8,128)S(1)}, f32[2,448,128]{2,1,0:T(8,128)S(1)}, bf16[2,448,128]{2,1,0:T(8,128)(2,1)S(1)}, bf16[64,256]{1,0:T(8,128)(2,1)S...) custom-call(s32[15]{0:T(128)S(1)} %stack.60.meta, bf16[64,4,3584]{2,1,0:T(4,128)(2,1)S(1)} %copy-done.3, ...), custom_call_target="tpu_custom_call" | custom-call | flops 1024 | bytes 1024 | tf_op jit(solution)/shard_map/requests/pallas_call | solution.py:557
  19.0 1.1 collective-permute-done.1.refs_1_.refs_3_
  20.1 0.2 collective-permute-start.6
  20.3 1.3 collective-permute-start.7
  21.6 6.3 %stage1.1 = (f32[2,3584,128]{2,1,0:T(8,128)S(1)}, f32[2,3584,128]{2,1,0:T(8,128)S(1)}) custom-call(s32[15]{0:T(128)S(1)} %stack.60.meta, s32[3]{0:T(128)S(1)} %copy-done.9, bf16[2,3584,128]{2,1,0:T(8,128)(2,1)S(1)} %get-tuple-element.254.qs, f32[2,3584,128]{2,1,0:T(8,128)S(1)} %get-tuple-element.166.total_in, ...), custom_call_target="tpu_custom_call", output_to_operand_aliasing={{0}: (3, {}), {1}: (4, {})} | custom-call | flops 1024 | bytes 1024 | tf_op jit(solution)/shard_map/stage1/pallas_call | solution.py:347
  27.9 0.2 collective-permute-start.12
  28.1 1.3 collective-permute-start.13
  29.4 1.9 collective-permute-done.6.refs_1_.refs_7_
  31.3 0.2 collective-permute-start.10
  31.5 1.3 collective-permute-start.11
  32.8 6.2 %stage3.1 = (f32[2,3584,128]{2,1,0:T(8,128)S(1)}, f32[2,3584,128]{2,1,0:T(8,128)S(1)}) custom-call(s32[15]{0:T(128)S(1)} %stack.60.meta, s32[3]{0:T(128)S(1)} %copy-done.9, bf16[2,3584,128]{2,1,0:T(8,128)(2,1)S(1)} %get-tuple-element.254.qs, f32[2,3584,128]{2,1,0:T(8,128)S(1)} %get-tuple-element.190.total_in, ...), custom_call_target="tpu_custom_call", output_to_operand_aliasing={{0}: (3, {}), {1}: (4, {})} | custom-call | flops 1024 | bytes 1024 | tf_op jit(solution)/shard_map/stage3/pallas_call | solution.py:347
  39.1 2.2 collective-permute-done.10.refs_11_
  41.3 0.7 take.1
  42.0 2.4 %collective-permute-start.14 = (bf16[448,1792]{1,0:T(8,128)(2,1)S(1)}, bf16[448,1792]{1,0:T(8,128)(2,1)S(1)}, u32[]{:S(2)}, u32[]{:S(2)}) collective-permute-start(bf16[448,1792]{1,0:T(8,128)(2,1)S(1)} %take.1), channel_id=1, source_target_pairs={{0,2},{2,0},{4,6},{6,4},{8,10},{10,8},{12,14},{14,12},{16,18},{18,... | collective-permute-start | bytes 4816904 | tf_op jit(solution)/shard_map/ppermute | solution.py:1030
  44.4 0.2 collective-permute-start.16
  44.6 1.3 collective-permute-start.15
  45.9 4.0 %early_decode.1 = (f32[2,448,128]{2,1,0:T(8,128)S(1)}, f32[2,448,128]{2,1,0:T(8,128)S(1)}) custom-call(f32[2,448,128]{2,1,0:T(8,128)S(1)} %get-tuple-element.218.total_in, f32[2,448,128]{2,1,0:T(8,128)S(1)} %get-tuple-element.219.acc_in, bf16[2,448,128]{2,1,0:T(8,128)(2,1)S(1)} %get-tuple-element.245.query, ...), custom_call_target="tpu_custom_call", output_to_operand_aliasing={{0}: (0, {}), {1}: (1, {})} | custom-call | flops 1024 | bytes 1024 | tf_op jit(solution)/shard_map/early_decode/pallas_call | solution.py:597
  49.9 2.4 %collective-permute-done.16.refs_14_ = bf16[256,512]{1,0:T(8,128)(2,1)S(1)} collective-permute-done((bf16[256,512]{1,0:T(8,128)(2,1)S(1)}, bf16[256,512]{1,0:T(8,128)(2,1)S(1)}, u32[]{:S(2)}, u32[]{:S(2)}) %collective-permute-start.16) | collective-permute-done | bytes 262176 | tf_op jit(solution)/shard_map/ppermute | solution.py:1002
  52.3 8.8 %late_decode.1.refs_0_ = bf16[64,1792]{1,0:T(8,128)(2,1)S(1)} custom-call(s32[15]{0:T(128)S(1)} %stack.60.meta, f32[2,448,128]{2,1,0:T(8,128)S(1)} %get-tuple-element.243.total, f32[2,448,128]{2,1,0:T(8,128)S(1)} %get-tuple-element.244.acc, bf16[2,448,128]{2,1,0:T(8,128)(2,1)S(1)} %get-tuple-element.245.query, bf16[64,256]{1,0:T(8,128)(2,1)S(1)} %get-tuple-element.246.newk, ...), custom_call_target="tpu_custom_call" | custom-call | flops 469762048 | bytes 57344 | tf_op jit(solution)/shard_map/late_decode/pallas_call | solution.py:663
  61.1 1.4 collective-permute-start.17
  62.4 0.4 collective-permute-start.18
  62.8 2.1 collective-permute-start.19
  64.8 153.9 %finish.1 = (bf16[256,1792]{1,0:T(8,128)(2,1)S(1)}, bf16[256,3584]{1,0:T(8,128)(2,1)}) custom-call(s32[15]{0:T(128)S(1)} %stack.60.meta, s32[3]{0:T(128)S(1)} %copy-done.9, bf16[2,3584,128]{2,1,0:T(8,128)(2,1)S(1)} %get-tuple-element.254.qs, f32[2,3584,128]{2,1,0:T(8,128)S(1)} %get-tuple-element.255.total, f32[2,3584,128]{2,1,0:T(8,128)S(1)} %get-tuple-element.256.acc, ...), custom_call_target="tpu_custom_call" | custom-call | flops 1879048192 | bytes 1835008 | tf_op jit(solution)/shard_map/finish/pallas_call | solution.py:456
  218.8 2.1 collective-permute-start.21
  220.9 2.4 %project.1 = (f32[448,128]{1,0:T(8,128)S(1)}, bf16[448,128]{1,0:T(8,128)(2,1)S(1)}, bf16[448,128]{1,0:T(8,128)(2,1)S(1)}, bf16[448,128]{1,0:T(8,128)(2,1)S(1)}) custom-call(s32[15]{0:T(128)S(1)} %stack.60.meta, bf16[64,1792]{1,0:T(8,128)(2,1)S(1)} %late_decode.1.refs_0_, bf16[64,1792]{1,0:T(8,128)(2,1)S(1)} %collective-permute-done.17.refs_1_, ...), custom_call_target="tpu_custom_call" | custom-call | flops 822083584 | bytes 3211264 | tf_op jit(solution)/shard_map/project/pallas_call | solution.py:884
  223.4 1.3 collective-permute-start.22
  224.7 0.8 collective-permute-start.23
  225.5 1.5 settle.1
  227.0 0.7 collective-permute-done.22
  227.8 3.0 %collective-permute-done.23 = bf16[448,128]{1,0:T(8,128)(2,1)S(1)} collective-permute-done((bf16[448,128]{1,0:T(8,128)(2,1)S(1)}, bf16[448,128]{1,0:T(8,128)(2,1)S(1)}, u32[]{:S(2)}, u32[]{:S(2)}) %collective-permute-start.23) | collective-permute-done | bytes 114720 | tf_op jit(solution)/shard_map/ppermute | solution.py:1051
  230.9 0.1 copy.20
  231.0 0.8 copy.22
  (37 shorter events, 0.3 us)
Async XLA Ops:
  0.6 9.0 %copy-start.9 = (s32[3]{0:T(128)S(1)}, s32[3]{0:T(128)}, u32[]{:S(2)}) copy-start(s32[3]{0:T(128)} %lengths.7) | copy-start | bytes 40
  0.6 1.0 copy-start.4
  1.6 0.9 copy-start.5
  2.5 13.4 %copy-start.7 = (bf16[64,4,512]{2,1,0:T(4,128)(2,1)S(1)}, bf16[64,4,512]{2,1,0:T(4,128)(2,1)}, u32[]{:S(2)}) copy-start(bf16[64,4,512]{2,1,0:T(4,128)(2,1)} %refs_2_.1) | copy-start | bytes 786436
  2.7 13.2 %copy-start.6 = (bf16[64,4,512]{2,1,0:T(4,128)(2,1)S(1)}, bf16[64,4,512]{2,1,0:T(4,128)(2,1)}, u32[]{:S(2)}) copy-start(bf16[64,4,512]{2,1,0:T(4,128)(2,1)} %refs_1_.1) | copy-start | bytes 786436
  2.7 13.2 %copy-start.8 = (s32[64,32]{0,1:T(8,128)S(1)}, s32[64,32]{0,1:T(8,128)}, u32[]{:S(2)}) copy-start(s32[64,32]{0,1:T(8,128)} %param.16) | copy-start | bytes 24580
  2.7 1.9 collective-permute-start
  4.6 1.5 copy-start.1
  6.1 3.5 %copy-start.2 = (bf16[256,3584]{1,0:T(8,128)(2,1)S(1)}, bf16[256,3584]{1,0:T(8,128)(2,1)}, u32[]{:S(2)}) copy-start(bf16[256,3584]{1,0:T(8,128)(2,1)} %q.3) | copy-start | bytes 5505028
  6.1 9.8 %copy-start.3 = (bf16[64,4,3584]{2,1,0:T(4,128)(2,1)S(1)}, bf16[64,4,3584]{2,1,0:T(4,128)(2,1)}, u32[]{:S(2)}) copy-start(bf16[64,4,3584]{2,1,0:T(4,128)(2,1)} %refs_0_.1) | copy-start | bytes 5505028
  6.3 3.4 %collective-permute-start.5 = (bf16[256,1792]{1,0:T(8,128)(2,1)S(1)}, bf16[256,1792]{1,0:T(8,128)(2,1)S(1)}, u32[]{:S(2)}, u32[]{:S(2)}) collective-permute-start(bf16[256,1792]{1,0:T(8,128)(2,1)S(1)} %get-tuple-element.144), channel_id=1, source_target_pairs={{0,2},{2,0},{4,6},{6,4},{8,10},{10,8},{12,14},{14,12},{16,18},{18,... | collective-permute-start | bytes 2752520 | tf_op jit(solution)/shard_map/ppermute | solution.py:997
  6.7 7.8 %collective-permute-start.3 = (bf16[256,512]{1,0:T(8,128)(2,1)S(1)}, bf16[256,512]{1,0:T(8,128)(2,1)S(1)}, u32[]{:S(2)}, u32[]{:S(2)}) collective-permute-start(bf16[256,512]{1,0:T(8,128)(2,1)S(1)} %get-tuple-element.143.upper.refs_0_), channel_id=1, source_target_pairs={{0,8},{2,10},{8,16},{10,18},{16,24},{18,26},{24,28},{26,30},{28,20... | collective-permute-start | bytes 786440 | tf_op jit(solution)/shard_map/ppermute | solution.py:1002
  6.9 7.6 %collective-permute-start.4 = (bf16[256,512]{1,0:T(8,128)(2,1)S(1)}, bf16[256,512]{1,0:T(8,128)(2,1)S(1)}, u32[]{:S(2)}, u32[]{:S(2)}) collective-permute-start(bf16[256,512]{1,0:T(8,128)(2,1)S(1)} %get-tuple-element.143.upper.refs_0_), channel_id=1, source_target_pairs={{0,4},{2,6},{8,0},{10,2},{16,8},{18,10},{24,16},{26,18},{28,24},{3... | collective-permute-start | bytes 786440 | tf_op jit(solution)/shard_map/ppermute | solution.py:1005
  8.2 11.9 %collective-permute-start.1 = (bf16[256,512]{1,0:T(8,128)(2,1)S(1)}, bf16[256,512]{1,0:T(8,128)(2,1)S(1)}, u32[]{:S(2)}, u32[]{:S(2)}) collective-permute-start(bf16[256,512]{1,0:T(8,128)(2,1)S(1)} %get-tuple-element.142.lower.refs_1_), channel_id=1, source_target_pairs={{0,8},{2,10},{8,16},{10,18},{16,24},{18,26},{24,28},{26,30},{28,20... | collective-permute-start | bytes 786440 | tf_op jit(solution)/shard_map/ppermute | solution.py:1006
  8.3 11.8 %collective-permute-start.2 = (bf16[256,512]{1,0:T(8,128)(2,1)S(1)}, bf16[256,512]{1,0:T(8,128)(2,1)S(1)}, u32[]{:S(2)}, u32[]{:S(2)}) collective-permute-start(bf16[256,512]{1,0:T(8,128)(2,1)S(1)} %get-tuple-element.142.lower.refs_1_), channel_id=1, source_target_pairs={{0,4},{2,6},{8,0},{10,2},{16,8},{18,10},{24,16},{26,18},{28,24},{3... | collective-permute-start | bytes 786440 | tf_op jit(solution)/shard_map/ppermute | solution.py:1003
  14.5 13.3 %collective-permute-start.8 = (bf16[256,512]{1,0:T(8,128)(2,1)S(1)}, bf16[256,512]{1,0:T(8,128)(2,1)S(1)}, u32[]{:S(2)}, u32[]{:S(2)}) collective-permute-start(bf16[256,512]{1,0:T(8,128)(2,1)S(1)} %collective-permute-done.3.refs_0_.refs_2_), channel_id=1, source_target_pairs={{0,8},{2,10},{8,16},{10,18},{16,24},{18,26},{24,28},{26,30},{28,20... | collective-permute-start | bytes 786440 | tf_op jit(solution)/shard_map/ppermute | solution.py:1002
  14.7 13.2 %collective-permute-start.9 = (bf16[256,512]{1,0:T(8,128)(2,1)S(1)}, bf16[256,512]{1,0:T(8,128)(2,1)S(1)}, u32[]{:S(2)}, u32[]{:S(2)}) collective-permute-start(bf16[256,512]{1,0:T(8,128)(2,1)S(1)} %collective-permute-done.4.refs_2_.refs_4_), channel_id=1, source_target_pairs={{0,4},{2,6},{8,0},{10,2},{16,8},{18,10},{24,16},{26,18},{28,24},{3... | collective-permute-start | bytes 786440 | tf_op jit(solution)/shard_map/ppermute | solution.py:1005
  20.1 11.2 %collective-permute-start.6 = (bf16[256,512]{1,0:T(8,128)(2,1)S(1)}, bf16[256,512]{1,0:T(8,128)(2,1)S(1)}, u32[]{:S(2)}, u32[]{:S(2)}) collective-permute-start(bf16[256,512]{1,0:T(8,128)(2,1)S(1)} %collective-permute-done.1.refs_1_.refs_3_), channel_id=1, source_target_pairs={{0,8},{2,10},{8,16},{10,18},{16,24},{18,26},{24,28},{26,30},{28,20... | collective-permute-start | bytes 786440 | tf_op jit(solution)/shard_map/ppermute | solution.py:1006
  20.3 11.1 %collective-permute-start.7 = (bf16[256,512]{1,0:T(8,128)(2,1)S(1)}, bf16[256,512]{1,0:T(8,128)(2,1)S(1)}, u32[]{:S(2)}, u32[]{:S(2)}) collective-permute-start(bf16[256,512]{1,0:T(8,128)(2,1)S(1)} %collective-permute-done.2.refs_3_.refs_5_), channel_id=1, source_target_pairs={{0,4},{2,6},{8,0},{10,2},{16,8},{18,10},{24,16},{26,18},{28,24},{3... | collective-permute-start | bytes 786440 | tf_op jit(solution)/shard_map/ppermute | solution.py:1003
  27.9 13.5 %copy-start = (bf16[3584,448]{0,1:T(8,128)(2,1)S(1)}, bf16[3584,448]{0,1:T(8,128)(2,1)}, u32[]{:S(2)}) copy-start(bf16[3584,448]{0,1:T(8,128)(2,1)} %param.17) | copy-start | bytes 9633796
  27.9 11.2 %collective-permute-start.12 = (bf16[256,512]{1,0:T(8,128)(2,1)S(1)}, bf16[256,512]{1,0:T(8,128)(2,1)S(1)}, u32[]{:S(2)}, u32[]{:S(2)}) collective-permute-start(bf16[256,512]{1,0:T(8,128)(2,1)S(1)} %collective-permute-done.8.refs_0_.refs_6_), channel_id=1, source_target_pairs={{0,8},{2,10},{8,16},{10,18},{16,24},{18,26},{24,28},{26,30},{28,20... | collective-permute-start | bytes 786440 | tf_op jit(solution)/shard_map/ppermute | solution.py:1002
  28.1 11.0 %collective-permute-start.13 = (bf16[256,512]{1,0:T(8,128)(2,1)S(1)}, bf16[256,512]{1,0:T(8,128)(2,1)S(1)}, u32[]{:S(2)}, u32[]{:S(2)}) collective-permute-start(bf16[256,512]{1,0:T(8,128)(2,1)S(1)} %collective-permute-done.9.refs_2_.refs_8_), channel_id=1, source_target_pairs={{0,4},{2,6},{8,0},{10,2},{16,8},{18,10},{24,16},{26,18},{28,24},{3... | collective-permute-start | bytes 786440 | tf_op jit(solution)/shard_map/ppermute | solution.py:1005
  31.3 10.0 %collective-permute-start.10 = (bf16[256,512]{1,0:T(8,128)(2,1)S(1)}, bf16[256,512]{1,0:T(8,128)(2,1)S(1)}, u32[]{:S(2)}, u32[]{:S(2)}) collective-permute-start(bf16[256,512]{1,0:T(8,128)(2,1)S(1)} %collective-permute-done.6.refs_1_.refs_7_), channel_id=1, source_target_pairs={{0,8},{2,10},{8,16},{10,18},{16,24},{18,26},{24,28},{26,30},{28,20... | collective-permute-start | bytes 786440 | tf_op jit(solution)/shard_map/ppermute | solution.py:1006
  31.5 9.8 %collective-permute-start.11 = (bf16[256,512]{1,0:T(8,128)(2,1)S(1)}, bf16[256,512]{1,0:T(8,128)(2,1)S(1)}, u32[]{:S(2)}, u32[]{:S(2)}) collective-permute-start(bf16[256,512]{1,0:T(8,128)(2,1)S(1)} %collective-permute-done.7.refs_3_.refs_9_), channel_id=1, source_target_pairs={{0,4},{2,6},{8,0},{10,2},{16,8},{18,10},{24,16},{26,18},{28,24},{3... | collective-permute-start | bytes 786440 | tf_op jit(solution)/shard_map/ppermute | solution.py:1003
  42.0 10.3 %collective-permute-start.14 = (bf16[448,1792]{1,0:T(8,128)(2,1)S(1)}, bf16[448,1792]{1,0:T(8,128)(2,1)S(1)}, u32[]{:S(2)}, u32[]{:S(2)}) collective-permute-start(bf16[448,1792]{1,0:T(8,128)(2,1)S(1)} %take.1), channel_id=1, source_target_pairs={{0,2},{2,0},{4,6},{6,4},{8,10},{10,8},{12,14},{14,12},{16,18},{18,... | collective-permute-start | bytes 4816904 | tf_op jit(solution)/shard_map/ppermute | solution.py:1030
  44.4 7.9 %collective-permute-start.16 = (bf16[256,512]{1,0:T(8,128)(2,1)S(1)}, bf16[256,512]{1,0:T(8,128)(2,1)S(1)}, u32[]{:S(2)}, u32[]{:S(2)}) collective-permute-start(bf16[256,512]{1,0:T(8,128)(2,1)S(1)} %collective-permute-done.12.refs_10_), channel_id=1, source_target_pairs={{0,8},{2,10},{8,16},{10,18},{16,24},{18,26},{24,28},{26,30},{28,20... | collective-permute-start | bytes 786440 | tf_op jit(solution)/shard_map/ppermute | solution.py:1002
  44.6 7.7 %collective-permute-start.15 = (bf16[256,512]{1,0:T(8,128)(2,1)S(1)}, bf16[256,512]{1,0:T(8,128)(2,1)S(1)}, u32[]{:S(2)}, u32[]{:S(2)}) collective-permute-start(bf16[256,512]{1,0:T(8,128)(2,1)S(1)} %collective-permute-done.11.refs_13_), channel_id=1, source_target_pairs={{0,4},{2,6},{8,0},{10,2},{16,8},{18,10},{24,16},{26,18},{28,24},{3... | collective-permute-start | bytes 786440 | tf_op jit(solution)/shard_map/ppermute | solution.py:1003
  61.1 157.7 %collective-permute-start.17 = (bf16[64,1792]{1,0:T(8,128)(2,1)S(1)}, bf16[64,1792]{1,0:T(8,128)(2,1)S(1)}, u32[]{:S(2)}, u32[]{:S(2)}) collective-permute-start(bf16[64,1792]{1,0:T(8,128)(2,1)S(1)} %late_decode.1.refs_0_), channel_id=1, source_target_pairs={{0,8},{2,10},{4,12},{6,14},{8,16},{10,18},{12,20},{14,22},{16,24},... | collective-permute-start | bytes 688136 | tf_op jit(solution)/shard_map/ppermute | solution.py:1038
  62.4 156.4 %collective-permute-start.18 = (bf16[64,1792]{1,0:T(8,128)(2,1)S(1)}, bf16[64,1792]{1,0:T(8,128)(2,1)S(1)}, u32[]{:S(2)}, u32[]{:S(2)}) collective-permute-start(bf16[64,1792]{1,0:T(8,128)(2,1)S(1)} %late_decode.1.refs_0_), channel_id=1, source_target_pairs={{0,16},{2,18},{4,20},{6,22},{8,24},{10,26},{12,28},{14,30},{16,0},... | collective-permute-start | bytes 688136 | tf_op jit(solution)/shard_map/ppermute | solution.py:1038
  62.8 156.0 %collective-permute-start.19 = (bf16[64,1792]{1,0:T(8,128)(2,1)S(1)}, bf16[64,1792]{1,0:T(8,128)(2,1)S(1)}, u32[]{:S(2)}, u32[]{:S(2)}) collective-permute-start(bf16[64,1792]{1,0:T(8,128)(2,1)S(1)} %late_decode.1.refs_0_), channel_id=1, source_target_pairs={{0,24},{2,26},{4,28},{6,30},{8,0},{10,2},{12,4},{14,6},{16,8},{18,... | collective-permute-start | bytes 688136 | tf_op jit(solution)/shard_map/ppermute | solution.py:1038
  218.8 6.7 %collective-permute-start.21 = (bf16[256,1792]{1,0:T(8,128)(2,1)S(1)}, bf16[256,1792]{1,0:T(8,128)(2,1)S(1)}, u32[]{:S(2)}, u32[]{:S(2)}) collective-permute-start(bf16[256,1792]{1,0:T(8,128)(2,1)S(1)} %get-tuple-element.265), channel_id=1, source_target_pairs={{0,2},{2,0},{4,6},{6,4},{8,10},{10,8},{12,14},{14,12},{16,18},{18,... | collective-permute-start | bytes 2752520 | tf_op jit(solution)/shard_map/ppermute | solution.py:1042
  223.3 3.7 %collective-permute-start.20 = (bf16[448,128]{1,0:T(8,128)(2,1)S(1)}, bf16[448,128]{1,0:T(8,128)(2,1)S(1)}, u32[]{:S(2)}, u32[]{:S(2)}) collective-permute-start(bf16[448,128]{1,0:T(8,128)(2,1)S(1)} %get-tuple-element.264), channel_id=1, source_target_pairs={{0,2},{1,3},{2,0},{3,1},{4,6},{5,7},{6,4},{7,5},{8,10},{9,11},{10,... | collective-permute-start | bytes 344072 | tf_op jit(solution)/shard_map/ppermute | solution.py:1051
  223.4 4.3 %collective-permute-start.22 = (bf16[448,128]{1,0:T(8,128)(2,1)S(1)}, bf16[448,128]{1,0:T(8,128)(2,1)S(1)}, u32[]{:S(2)}, u32[]{:S(2)}) collective-permute-start(bf16[448,128]{1,0:T(8,128)(2,1)S(1)} %get-tuple-element.270), channel_id=1, source_target_pairs={{0,1},{1,0},{2,3},{3,2},{4,5},{5,4},{6,7},{7,6},{8,9},{9,8},{10,11... | collective-permute-start | bytes 344072 | tf_op jit(solution)/shard_map/ppermute | solution.py:1051
  224.7 6.1 %collective-permute-start.23 = (bf16[448,128]{1,0:T(8,128)(2,1)S(1)}, bf16[448,128]{1,0:T(8,128)(2,1)S(1)}, u32[]{:S(2)}, u32[]{:S(2)}) collective-permute-start(bf16[448,128]{1,0:T(8,128)(2,1)S(1)} %get-tuple-element.271), channel_id=1, source_target_pairs={{0,3},{1,2},{2,1},{3,0},{4,7},{5,6},{6,5},{7,4},{8,11},{9,10},{10,... | collective-permute-start | bytes 344072 | tf_op jit(solution)/shard_map/ppermute | solution.py:1051

commit v4 on v3

--- a/solution.py
+++ b/solution.py
@@ -255,6 +255,15 @@
     return relevant, base >= start_of(first + tok - 1, lengths), first, base
 
 
+def postponed(meta, tok, lengths, first, end, parts):
+    def count(some):
+        pairs = [relation(meta, part, side, tok, lengths)[0] for part in some for side in range(2)]
+        return sum(pair.astype(jnp.int32) for pair in pairs)
+
+    here, later = count(range(first, end)), count(range(end, parts))
+    return (here == 2 * (end - first)) & (here + later <= 6)
+
+
 def side_rows(side, heads, tok):
     return pl.ds(pl.multiple_of(side * (heads * tok), HD), heads * tok)
 
@@ -300,7 +309,10 @@
     )(meta, lengths, q, q_near, *block)
 
 
-def stage_body(tok, heads, groups, first_part, meta, lengths, qs, before, pair, total, acc):
+def stage_body(tok, heads, groups, first_part, wait, meta, lengths, qs, before, pair, total, acc):
+    later = False
+    if wait:
+        later = postponed(meta, tok, lengths, first_part, first_part + 2, LEVELS - PARTS)
     for which in range(2):
         upper, lower = pair[2 * which], pair[2 * which + 1]
 
@@ -308,6 +320,7 @@
         def _(step):
             g, side = lax.div(step, 2), lax.rem(step, 2)
             relevant, clear, first, base = relation(meta, first_part + which, side, tok, lengths)
+            relevant = relevant & jnp.logical_not(later)
             here = side_rows(side, heads, tok)
             sums = (total.at[g, here], acc.at[g, here])
             old = sums if which else [ref.at[g, here] for ref in before]
@@ -333,19 +346,21 @@
                         sums[i][...] = old[i][...]
 
 
-def stage_kernel(tok, heads, groups, first_part, meta, lengths, qs, total_in, acc_in, *refs):
+def stage_kernel(tok, heads, groups, first_part, wait, meta, lengths, qs, total_in, acc_in, *refs):
     pair, (total, acc) = refs[:4], refs[4:]
     before = (total_in, acc_in)
-    stage_body(tok, heads, groups, first_part, meta, lengths, qs, before, pair, total, acc)
-
-
-def stage(state, pair, first_part, meta, lengths):
+    stage_body(
+        tok, heads, groups, first_part, wait, meta, lengths, qs, before, pair, total, acc
+    )
+
+
+def stage(state, pair, first_part, wait, meta, lengths):
     qs, total, acc = state
     groups, rows, unused = qs.shape
     flat = [x for block in pair for x in block]
     tok = flat[0].shape[1] // 2
     new = pl.pallas_call(
-        functools.partial(stage_kernel, tok, rows // (2 * tok), groups, first_part),
+        functools.partial(stage_kernel, tok, rows // (2 * tok), groups, first_part, wait),
         out_shape=[jax.ShapeDtypeStruct(x.shape, x.dtype) for x in (total, acc)],
         in_specs=[SMEM, SMEM] + [VMEM] * 7,
         out_specs=[VMEM] * 2,
@@ -390,6 +405,7 @@
         @pl.loop(done, parts)
         def _(i):
             relevant, clear, first, base = relation(meta, i, side, tok, lengths)
+            relevant = relevant & ((i >= done + 2) | later)
             upper, lower = held_k.at[i], held_v.at[i]
             sums = (total_now, acc_now)
 
@@ -406,6 +422,7 @@
 
         return fine & write(turn, g).astype(jnp.int32)
 
+    later = postponed(meta, tok, lengths, done, done + 2, parts)
     fill(done)
     fine = lax.fori_loop(0, 2 * groups, one_turn, jnp.int32(1))
 
@@ -1012,7 +1029,7 @@
             state = open_sums(q_pre, near_q, (held_k[0], held_v[0]), meta, lengths)
         elif d < far:
             pair = [(held_k[o], held_v[o]) for o in (1 - d, d - 1)]
-            state = stage(state, pair, 2 * d - 3, meta, lengths)
+            state = stage(state, pair, 2 * d - 3, d == far - 1, meta, lengths)
         else:
             blocks = [(held_k[o], held_v[o]) for o in order[:-1]]
             early = early_decode(early, blocks)
@@ -1037,7 +1054,7 @@
         perm = [(index(*p), index((p[0] + d) % deep, p[1], p[2])) for p in everyone]
         pieces.append(lax.ppermute(attn_own, "seq", perm))
     attn_own, state = lax.optimization_barrier((attn_own, state))
-    near, pre_out = finish(state, blocks, 2 * far - 3, meta, lengths)
+    near, pre_out = finish(state, blocks, 2 * far - 5, meta, lengths)
     pieces, near, pre_out = lax.optimization_barrier((pieces, near, pre_out))
     back = lax.ppermute(near, "seq", sibling)
     pre_out = settle(pre_out, back, meta)

time: 232 us -> 232 us (level)
  no operation moved by 1% of the time
where the time goes in v4:
time: 232 us; the launch traced here: 231 us
  Pallas kernels  191 us (82%)
  starting transfers between devices  21.7 us (9%)
  waiting for transfers between devices  13.1 us (6%)
  local copies, waits for them, and re-layouts  4.4 us (2%)
    pallas_call x1, Pallas kernels, finish(): pl.pallas_call(functools.partial(finish_kernel, tok, heads, groups, done)...  154 us
    pallas_call x2, Pallas kernels, stage(): pl.pallas_call(functools.partial(stage_kernel, tok, rows // (2 * tok), gr...  12.5 us
    pallas_call x1, Pallas kernels, late_decode(): pl.pallas_call(functools.partial(late_kernel, own, steps, heads, groups,...  8.76 us
    ppermute x3, waiting for transfers between devices, split_heads(): held_v[-d] = lax.ppermute(held_v[1 - d], 'seq', up)  5.29 us
    ppermute x4, starting transfers between devices, split_heads(): held_v[d] = lax.ppermute(held_v[d - 1], 'seq', down)  5.19 us
  transfers between devices with their start and end apart: 24, of which 8 were waited for; matrix products, arithmetic and copies ran while one was open for 0% of the time, Pallas kernels for 78%

profile of v4, /device:TPU:21, one launch (start us, length us, event | category | flops | bytes accessed | tf_op | source)
XLA Modules:
  0.0 231.3 jit_solution(8565760941018546515)
XLA Ops:
  0.7 0.9 copy-done.4
  1.6 0.9 copy-done.5
  2.6 0.1 prepare.1
  2.7 0.7 collective-permute-start
  3.5 0.1 stack.60.meta
  3.6 1.1 collective-permute-done.theirs
  4.6 1.5 copy-done.1
  6.1 0.1 join.1
  6.3 0.4 collective-permute-start.5
  6.7 0.2 collective-permute-start.3
  6.9 1.3 collective-permute-start.4
  8.2 0.2 collective-permute-start.1
  8.3 1.3 collective-permute-start.2
  9.7 4.3 %open.1 = (bf16[2,3584,128]{2,1,0:T(8,128)(2,1)S(1)}, f32[2,3584,128]{2,1,0:T(8,128)S(1)}, f32[2,3584,128]{2,1,0:T(8,128)S(1)}) custom-call(s32[15]{0:T(128)S(1)} %stack.60.meta, s32[3]{0:T(128)S(1)} %copy-done.9, bf16[256,3584]{1,0:T(8,128)(2,1)S(1)} %copy-done.2, bf16[256,1792]{1,0:T(8,128)(2,1)S(1)} %collective-permute-done.5.q_near, ...), custom_call_target="tpu_custom_call" | custom-call | flops 1024 | bytes 1024 | tf_op jit(solution)/shard_map/open/pallas_call | solution.py:301
  14.0 0.5 collective-permute-done.3.refs_0_.refs_2_
  14.5 0.2 collective-permute-start.8
  14.7 1.3 collective-permute-start.9
  16.0 3.0 %requests.1 = (f32[2,448,128]{2,1,0:T(8,128)S(1)}, f32[2,448,128]{2,1,0:T(8,128)S(1)}, bf16[2,448,128]{2,1,0:T(8,128)(2,1)S(1)}, bf16[64,256]{1,0:T(8,128)(2,1)S...) custom-call(s32[15]{0:T(128)S(1)} %stack.60.meta, bf16[64,4,3584]{2,1,0:T(4,128)(2,1)S(1)} %copy-done.3, ...), custom_call_target="tpu_custom_call" | custom-call | flops 1024 | bytes 1024 | tf_op jit(solution)/shard_map/requests/pallas_call | solution.py:574
  19.0 1.1 collective-permute-done.1.refs_1_.refs_3_
  20.1 0.2 collective-permute-start.6
  20.3 1.3 collective-permute-start.7
  21.6 6.3 %stage1.1 = (f32[2,3584,128]{2,1,0:T(8,128)S(1)}, f32[2,3584,128]{2,1,0:T(8,128)S(1)}) custom-call(s32[15]{0:T(128)S(1)} %stack.60.meta, s32[3]{0:T(128)S(1)} %copy-done.9, bf16[2,3584,128]{2,1,0:T(8,128)(2,1)S(1)} %get-tuple-element.254.qs, f32[2,3584,128]{2,1,0:T(8,128)S(1)} %get-tuple-element.166.total_in, ...), custom_call_target="tpu_custom_call", output_to_operand_aliasing={{0}: (3, {}), {1}: (4, {})} | custom-call | flops 1024 | bytes 1024 | tf_op jit(solution)/shard_map/stage1/pallas_call | solution.py:362
  27.9 0.2 collective-permute-start.12
  28.1 1.3 collective-permute-start.13
  29.4 1.9 collective-permute-done.6.refs_1_.refs_7_
  31.3 0.2 collective-permute-start.10
  31.5 1.3 collective-permute-start.11
  32.8 6.3 %stage3.1 = (f32[2,3584,128]{2,1,0:T(8,128)S(1)}, f32[2,3584,128]{2,1,0:T(8,128)S(1)}) custom-call(s32[15]{0:T(128)S(1)} %stack.60.meta, s32[3]{0:T(128)S(1)} %copy-done.9, bf16[2,3584,128]{2,1,0:T(8,128)(2,1)S(1)} %get-tuple-element.254.qs, f32[2,3584,128]{2,1,0:T(8,128)S(1)} %get-tuple-element.190.total_in, ...), custom_call_target="tpu_custom_call", output_to_operand_aliasing={{0}: (3, {}), {1}: (4, {})} | custom-call | flops 1024 | bytes 1024 | tf_op jit(solution)/shard_map/stage3/pallas_call | solution.py:362
  39.1 2.2 collective-permute-done.10.refs_11_
  41.3 0.7 take.1
  42.0 2.4 %collective-permute-start.14 = (bf16[448,1792]{1,0:T(8,128)(2,1)S(1)}, bf16[448,1792]{1,0:T(8,128)(2,1)S(1)}, u32[]{:S(2)}, u32[]{:S(2)}) collective-permute-start(bf16[448,1792]{1,0:T(8,128)(2,1)S(1)} %take.1), channel_id=1, source_target_pairs={{0,2},{2,0},{4,6},{6,4},{8,10},{10,8},{12,14},{14,12},{16,18},{18,... | collective-permute-start | bytes 4816904 | tf_op jit(solution)/shard_map/ppermute | solution.py:1047
  44.4 0.2 collective-permute-start.16
  44.6 1.3 collective-permute-start.15
  45.9 4.0 %early_decode.1 = (f32[2,448,128]{2,1,0:T(8,128)S(1)}, f32[2,448,128]{2,1,0:T(8,128)S(1)}) custom-call(f32[2,448,128]{2,1,0:T(8,128)S(1)} %get-tuple-element.218.total_in, f32[2,448,128]{2,1,0:T(8,128)S(1)} %get-tuple-element.219.acc_in, bf16[2,448,128]{2,1,0:T(8,128)(2,1)S(1)} %get-tuple-element.245.query, ...), custom_call_target="tpu_custom_call", output_to_operand_aliasing={{0}: (0, {}), {1}: (1, {})} | custom-call | flops 1024 | bytes 1024 | tf_op jit(solution)/shard_map/early_decode/pallas_call | solution.py:614
  49.9 2.4 %collective-permute-done.16.refs_14_ = bf16[256,512]{1,0:T(8,128)(2,1)S(1)} collective-permute-done((bf16[256,512]{1,0:T(8,128)(2,1)S(1)}, bf16[256,512]{1,0:T(8,128)(2,1)S(1)}, u32[]{:S(2)}, u32[]{:S(2)}) %collective-permute-start.16) | collective-permute-done | bytes 262176 | tf_op jit(solution)/shard_map/ppermute | solution.py:1019
  52.3 8.8 %late_decode.1.refs_0_ = bf16[64,1792]{1,0:T(8,128)(2,1)S(1)} custom-call(s32[15]{0:T(128)S(1)} %stack.60.meta, f32[2,448,128]{2,1,0:T(8,128)S(1)} %get-tuple-element.243.total, f32[2,448,128]{2,1,0:T(8,128)S(1)} %get-tuple-element.244.acc, bf16[2,448,128]{2,1,0:T(8,128)(2,1)S(1)} %get-tuple-element.245.query, bf16[64,256]{1,0:T(8,128)(2,1)S(1)} %get-tuple-element.246.newk, ...), custom_call_target="tpu_custom_call" | custom-call | flops 469762048 | bytes 57344 | tf_op jit(solution)/shard_map/late_decode/pallas_call | solution.py:680
  61.1 1.4 collective-permute-start.17
  62.5 2.1 collective-permute-start.19
  64.6 153.7 %finish.1 = (bf16[256,1792]{1,0:T(8,128)(2,1)S(1)}, bf16[256,3584]{1,0:T(8,128)(2,1)}) custom-call(s32[15]{0:T(128)S(1)} %stack.60.meta, s32[3]{0:T(128)S(1)} %copy-done.9, bf16[2,3584,128]{2,1,0:T(8,128)(2,1)S(1)} %get-tuple-element.254.qs, f32[2,3584,128]{2,1,0:T(8,128)S(1)} %get-tuple-element.255.total, f32[2,3584,128]{2,1,0:T(8,128)S(1)} %get-tuple-element.256.acc, ...), custom_call_target="tpu_custom_call" | custom-call | flops 1879048192 | bytes 1835008 | tf_op jit(solution)/shard_map/finish/pallas_call | solution.py:473
  218.3 2.1 collective-permute-start.21
  220.4 2.4 %project.1 = (f32[448,128]{1,0:T(8,128)S(1)}, bf16[448,128]{1,0:T(8,128)(2,1)S(1)}, bf16[448,128]{1,0:T(8,128)(2,1)S(1)}, bf16[448,128]{1,0:T(8,128)(2,1)S(1)}) custom-call(s32[15]{0:T(128)S(1)} %stack.60.meta, bf16[64,1792]{1,0:T(8,128)(2,1)S(1)} %late_decode.1.refs_0_, bf16[64,1792]{1,0:T(8,128)(2,1)S(1)} %collective-permute-done.17.refs_1_, ...), custom_call_target="tpu_custom_call" | custom-call | flops 822083584 | bytes 3211264 | tf_op jit(solution)/shard_map/project/pallas_call | solution.py:901
  222.9 1.3 collective-permute-start.22
  224.2 0.9 collective-permute-start.23
  225.1 1.5 settle.1
  226.6 0.7 collective-permute-done.22
  227.3 3.0 %collective-permute-done.23 = bf16[448,128]{1,0:T(8,128)(2,1)S(1)} collective-permute-done((bf16[448,128]{1,0:T(8,128)(2,1)S(1)}, bf16[448,128]{1,0:T(8,128)(2,1)S(1)}, u32[]{:S(2)}, u32[]{:S(2)}) %collective-permute-start.23) | collective-permute-done | bytes 114720 | tf_op jit(solution)/shard_map/ppermute | solution.py:1068
  230.4 0.1 copy.20
  230.5 0.8 copy.22
  (37 shorter events, 0.3 us)
Async XLA Ops:
  0.6 9.0 %copy-start.9 = (s32[3]{0:T(128)S(1)}, s32[3]{0:T(128)}, u32[]{:S(2)}) copy-start(s32[3]{0:T(128)} %lengths.7) | copy-start | bytes 40
  0.6 1.0 copy-start.4
  1.6 0.9 copy-start.5
  2.5 13.4 %copy-start.7 = (bf16[64,4,512]{2,1,0:T(4,128)(2,1)S(1)}, bf16[64,4,512]{2,1,0:T(4,128)(2,1)}, u32[]{:S(2)}) copy-start(bf16[64,4,512]{2,1,0:T(4,128)(2,1)} %refs_2_.1) | copy-start | bytes 786436
  2.7 13.2 %copy-start.6 = (bf16[64,4,512]{2,1,0:T(4,128)(2,1)S(1)}, bf16[64,4,512]{2,1,0:T(4,128)(2,1)}, u32[]{:S(2)}) copy-start(bf16[64,4,512]{2,1,0:T(4,128)(2,1)} %refs_1_.1) | copy-start | bytes 786436
  2.7 13.2 %copy-start.8 = (s32[64,32]{0,1:T(8,128)S(1)}, s32[64,32]{0,1:T(8,128)}, u32[]{:S(2)}) copy-start(s32[64,32]{0,1:T(8,128)} %param.16) | copy-start | bytes 24580
  2.7 1.9 collective-permute-start
  4.6 1.5 copy-start.1
  6.1 3.5 %copy-start.2 = (bf16[256,3584]{1,0:T(8,128)(2,1)S(1)}, bf16[256,3584]{1,0:T(8,128)(2,1)}, u32[]{:S(2)}) copy-start(bf16[256,3584]{1,0:T(8,128)(2,1)} %q.3) | copy-start | bytes 5505028
  6.1 9.8 %copy-start.3 = (bf16[64,4,3584]{2,1,0:T(4,128)(2,1)S(1)}, bf16[64,4,3584]{2,1,0:T(4,128)(2,1)}, u32[]{:S(2)}) copy-start(bf16[64,4,3584]{2,1,0:T(4,128)(2,1)} %refs_0_.1) | copy-start | bytes 5505028
  6.3 3.4 %collective-permute-start.5 = (bf16[256,1792]{1,0:T(8,128)(2,1)S(1)}, bf16[256,1792]{1,0:T(8,128)(2,1)S(1)}, u32[]{:S(2)}, u32[]{:S(2)}) collective-permute-start(bf16[256,1792]{1,0:T(8,128)(2,1)S(1)} %get-tuple-element.144), channel_id=1, source_target_pairs={{0,2},{2,0},{4,6},{6,4},{8,10},{10,8},{12,14},{14,12},{16,18},{18,... | collective-permute-start | bytes 2752520 | tf_op jit(solution)/shard_map/ppermute | solution.py:1014
  6.7 7.8 %collective-permute-start.3 = (bf16[256,512]{1,0:T(8,128)(2,1)S(1)}, bf16[256,512]{1,0:T(8,128)(2,1)S(1)}, u32[]{:S(2)}, u32[]{:S(2)}) collective-permute-start(bf16[256,512]{1,0:T(8,128)(2,1)S(1)} %get-tuple-element.143.upper.refs_0_), channel_id=1, source_target_pairs={{0,8},{2,10},{8,16},{10,18},{16,24},{18,26},{24,28},{26,30},{28,20... | collective-permute-start | bytes 786440 | tf_op jit(solution)/shard_map/ppermute | solution.py:1019
  6.9 7.6 %collective-permute-start.4 = (bf16[256,512]{1,0:T(8,128)(2,1)S(1)}, bf16[256,512]{1,0:T(8,128)(2,1)S(1)}, u32[]{:S(2)}, u32[]{:S(2)}) collective-permute-start(bf16[256,512]{1,0:T(8,128)(2,1)S(1)} %get-tuple-element.143.upper.refs_0_), channel_id=1, source_target_pairs={{0,4},{2,6},{8,0},{10,2},{16,8},{18,10},{24,16},{26,18},{28,24},{3... | collective-permute-start | bytes 786440 | tf_op jit(solution)/shard_map/ppermute | solution.py:1022
  8.2 11.9 %collective-permute-start.1 = (bf16[256,512]{1,0:T(8,128)(2,1)S(1)}, bf16[256,512]{1,0:T(8,128)(2,1)S(1)}, u32[]{:S(2)}, u32[]{:S(2)}) collective-permute-start(bf16[256,512]{1,0:T(8,128)(2,1)S(1)} %get-tuple-element.142.lower.refs_1_), channel_id=1, source_target_pairs={{0,8},{2,10},{8,16},{10,18},{16,24},{18,26},{24,28},{26,30},{28,20... | collective-permute-start | bytes 786440 | tf_op jit(solution)/shard_map/ppermute | solution.py:1023
  8.3 11.8 %collective-permute-start.2 = (bf16[256,512]{1,0:T(8,128)(2,1)S(1)}, bf16[256,512]{1,0:T(8,128)(2,1)S(1)}, u32[]{:S(2)}, u32[]{:S(2)}) collective-permute-start(bf16[256,512]{1,0:T(8,128)(2,1)S(1)} %get-tuple-element.142.lower.refs_1_), channel_id=1, source_target_pairs={{0,4},{2,6},{8,0},{10,2},{16,8},{18,10},{24,16},{26,18},{28,24},{3... | collective-permute-start | bytes 786440 | tf_op jit(solution)/shard_map/ppermute | solution.py:1020
  14.5 13.3 %collective-permute-start.8 = (bf16[256,512]{1,0:T(8,128)(2,1)S(1)}, bf16[256,512]{1,0:T(8,128)(2,1)S(1)}, u32[]{:S(2)}, u32[]{:S(2)}) collective-permute-start(bf16[256,512]{1,0:T(8,128)(2,1)S(1)} %collective-permute-done.3.refs_0_.refs_2_), channel_id=1, source_target_pairs={{0,8},{2,10},{8,16},{10,18},{16,24},{18,26},{24,28},{26,30},{28,20... | collective-permute-start | bytes 786440 | tf_op jit(solution)/shard_map/ppermute | solution.py:1019
  14.7 13.2 %collective-permute-start.9 = (bf16[256,512]{1,0:T(8,128)(2,1)S(1)}, bf16[256,512]{1,0:T(8,128)(2,1)S(1)}, u32[]{:S(2)}, u32[]{:S(2)}) collective-permute-start(bf16[256,512]{1,0:T(8,128)(2,1)S(1)} %collective-permute-done.4.refs_2_.refs_4_), channel_id=1, source_target_pairs={{0,4},{2,6},{8,0},{10,2},{16,8},{18,10},{24,16},{26,18},{28,24},{3... | collective-permute-start | bytes 786440 | tf_op jit(solution)/shard_map/ppermute | solution.py:1022
  20.1 11.2 %collective-permute-start.6 = (bf16[256,512]{1,0:T(8,128)(2,1)S(1)}, bf16[256,512]{1,0:T(8,128)(2,1)S(1)}, u32[]{:S(2)}, u32[]{:S(2)}) collective-permute-start(bf16[256,512]{1,0:T(8,128)(2,1)S(1)} %collective-permute-done.1.refs_1_.refs_3_), channel_id=1, source_target_pairs={{0,8},{2,10},{8,16},{10,18},{16,24},{18,26},{24,28},{26,30},{28,20... | collective-permute-start | bytes 786440 | tf_op jit(solution)/shard_map/ppermute | solution.py:1023
  20.3 11.1 %collective-permute-start.7 = (bf16[256,512]{1,0:T(8,128)(2,1)S(1)}, bf16[256,512]{1,0:T(8,128)(2,1)S(1)}, u32[]{:S(2)}, u32[]{:S(2)}) collective-permute-start(bf16[256,512]{1,0:T(8,128)(2,1)S(1)} %collective-permute-done.2.refs_3_.refs_5_), channel_id=1, source_target_pairs={{0,4},{2,6},{8,0},{10,2},{16,8},{18,10},{24,16},{26,18},{28,24},{3... | collective-permute-start | bytes 786440 | tf_op jit(solution)/shard_map/ppermute | solution.py:1020
  27.9 13.5 %copy-start = (bf16[3584,448]{0,1:T(8,128)(2,1)S(1)}, bf16[3584,448]{0,1:T(8,128)(2,1)}, u32[]{:S(2)}) copy-start(bf16[3584,448]{0,1:T(8,128)(2,1)} %param.17) | copy-start | bytes 9633796
  27.9 11.2 %collective-permute-start.12 = (bf16[256,512]{1,0:T(8,128)(2,1)S(1)}, bf16[256,512]{1,0:T(8,128)(2,1)S(1)}, u32[]{:S(2)}, u32[]{:S(2)}) collective-permute-start(bf16[256,512]{1,0:T(8,128)(2,1)S(1)} %collective-permute-done.8.refs_0_.refs_6_), channel_id=1, source_target_pairs={{0,8},{2,10},{8,16},{10,18},{16,24},{18,26},{24,28},{26,30},{28,20... | collective-permute-start | bytes 786440 | tf_op jit(solution)/shard_map/ppermute | solution.py:1019
  28.1 11.0 %collective-permute-start.13 = (bf16[256,512]{1,0:T(8,128)(2,1)S(1)}, bf16[256,512]{1,0:T(8,128)(2,1)S(1)}, u32[]{:S(2)}, u32[]{:S(2)}) collective-permute-start(bf16[256,512]{1,0:T(8,128)(2,1)S(1)} %collective-permute-done.9.refs_2_.refs_8_), channel_id=1, source_target_pairs={{0,4},{2,6},{8,0},{10,2},{16,8},{18,10},{24,16},{26,18},{28,24},{3... | collective-permute-start | bytes 786440 | tf_op jit(solution)/shard_map/ppermute | solution.py:1022
  31.3 10.0 %collective-permute-start.10 = (bf16[256,512]{1,0:T(8,128)(2,1)S(1)}, bf16[256,512]{1,0:T(8,128)(2,1)S(1)}, u32[]{:S(2)}, u32[]{:S(2)}) collective-permute-start(bf16[256,512]{1,0:T(8,128)(2,1)S(1)} %collective-permute-done.6.refs_1_.refs_7_), channel_id=1, source_target_pairs={{0,8},{2,10},{8,16},{10,18},{16,24},{18,26},{24,28},{26,30},{28,20... | collective-permute-start | bytes 786440 | tf_op jit(solution)/shard_map/ppermute | solution.py:1023
  31.5 9.8 %collective-permute-start.11 = (bf16[256,512]{1,0:T(8,128)(2,1)S(1)}, bf16[256,512]{1,0:T(8,128)(2,1)S(1)}, u32[]{:S(2)}, u32[]{:S(2)}) collective-permute-start(bf16[256,512]{1,0:T(8,128)(2,1)S(1)} %collective-permute-done.7.refs_3_.refs_9_), channel_id=1, source_target_pairs={{0,4},{2,6},{8,0},{10,2},{16,8},{18,10},{24,16},{26,18},{28,24},{3... | collective-permute-start | bytes 786440 | tf_op jit(solution)/shard_map/ppermute | solution.py:1020
  42.0 10.3 %collective-permute-start.14 = (bf16[448,1792]{1,0:T(8,128)(2,1)S(1)}, bf16[448,1792]{1,0:T(8,128)(2,1)S(1)}, u32[]{:S(2)}, u32[]{:S(2)}) collective-permute-start(bf16[448,1792]{1,0:T(8,128)(2,1)S(1)} %take.1), channel_id=1, source_target_pairs={{0,2},{2,0},{4,6},{6,4},{8,10},{10,8},{12,14},{14,12},{16,18},{18,... | collective-permute-start | bytes 4816904 | tf_op jit(solution)/shard_map/ppermute | solution.py:1047
  44.4 7.9 %collective-permute-start.16 = (bf16[256,512]{1,0:T(8,128)(2,1)S(1)}, bf16[256,512]{1,0:T(8,128)(2,1)S(1)}, u32[]{:S(2)}, u32[]{:S(2)}) collective-permute-start(bf16[256,512]{1,0:T(8,128)(2,1)S(1)} %collective-permute-done.12.refs_10_), channel_id=1, source_target_pairs={{0,8},{2,10},{8,16},{10,18},{16,24},{18,26},{24,28},{26,30},{28,20... | collective-permute-start | bytes 786440 | tf_op jit(solution)/shard_map/ppermute | solution.py:1019
  44.6 7.7 %collective-permute-start.15 = (bf16[256,512]{1,0:T(8,128)(2,1)S(1)}, bf16[256,512]{1,0:T(8,128)(2,1)S(1)}, u32[]{:S(2)}, u32[]{:S(2)}) collective-permute-start(bf16[256,512]{1,0:T(8,128)(2,1)S(1)} %collective-permute-done.11.refs_13_), channel_id=1, source_target_pairs={{0,4},{2,6},{8,0},{10,2},{16,8},{18,10},{24,16},{26,18},{28,24},{3... | collective-permute-start | bytes 786440 | tf_op jit(solution)/shard_map/ppermute | solution.py:1020
  61.1 157.2 %collective-permute-start.17 = (bf16[64,1792]{1,0:T(8,128)(2,1)S(1)}, bf16[64,1792]{1,0:T(8,128)(2,1)S(1)}, u32[]{:S(2)}, u32[]{:S(2)}) collective-permute-start(bf16[64,1792]{1,0:T(8,128)(2,1)S(1)} %late_decode.1.refs_0_), channel_id=1, source_target_pairs={{0,8},{2,10},{4,12},{6,14},{8,16},{10,18},{12,20},{14,22},{16,24},... | collective-permute-start | bytes 688136 | tf_op jit(solution)/shard_map/ppermute | solution.py:1055
  62.4 155.9 %collective-permute-start.18 = (bf16[64,1792]{1,0:T(8,128)(2,1)S(1)}, bf16[64,1792]{1,0:T(8,128)(2,1)S(1)}, u32[]{:S(2)}, u32[]{:S(2)}) collective-permute-start(bf16[64,1792]{1,0:T(8,128)(2,1)S(1)} %late_decode.1.refs_0_), channel_id=1, source_target_pairs={{0,16},{2,18},{4,20},{6,22},{8,24},{10,26},{12,28},{14,30},{16,0},... | collective-permute-start | bytes 688136 | tf_op jit(solution)/shard_map/ppermute | solution.py:1055
  62.5 155.9 %collective-permute-start.19 = (bf16[64,1792]{1,0:T(8,128)(2,1)S(1)}, bf16[64,1792]{1,0:T(8,128)(2,1)S(1)}, u32[]{:S(2)}, u32[]{:S(2)}) collective-permute-start(bf16[64,1792]{1,0:T(8,128)(2,1)S(1)} %late_decode.1.refs_0_), channel_id=1, source_target_pairs={{0,24},{2,26},{4,28},{6,30},{8,0},{10,2},{12,4},{14,6},{16,8},{18,... | collective-permute-start | bytes 688136 | tf_op jit(solution)/shard_map/ppermute | solution.py:1055
  218.3 6.7 %collective-permute-start.21 = (bf16[256,1792]{1,0:T(8,128)(2,1)S(1)}, bf16[256,1792]{1,0:T(8,128)(2,1)S(1)}, u32[]{:S(2)}, u32[]{:S(2)}) collective-permute-start(bf16[256,1792]{1,0:T(8,128)(2,1)S(1)} %get-tuple-element.265), channel_id=1, source_target_pairs={{0,2},{2,0},{4,6},{6,4},{8,10},{10,8},{12,14},{14,12},{16,18},{18,... | collective-permute-start | bytes 2752520 | tf_op jit(solution)/shard_map/ppermute | solution.py:1059
  222.9 3.7 %collective-permute-start.20 = (bf16[448,128]{1,0:T(8,128)(2,1)S(1)}, bf16[448,128]{1,0:T(8,128)(2,1)S(1)}, u32[]{:S(2)}, u32[]{:S(2)}) collective-permute-start(bf16[448,128]{1,0:T(8,128)(2,1)S(1)} %get-tuple-element.264), channel_id=1, source_target_pairs={{0,2},{1,3},{2,0},{3,1},{4,6},{5,7},{6,4},{7,5},{8,10},{9,11},{10,... | collective-permute-start | bytes 344072 | tf_op jit(solution)/shard_map/ppermute | solution.py:1068
  222.9 4.3 %collective-permute-start.22 = (bf16[448,128]{1,0:T(8,128)(2,1)S(1)}, bf16[448,128]{1,0:T(8,128)(2,1)S(1)}, u32[]{:S(2)}, u32[]{:S(2)}) collective-permute-start(bf16[448,128]{1,0:T(8,128)(2,1)S(1)} %get-tuple-element.270), channel_id=1, source_target_pairs={{0,1},{1,0},{2,3},{3,2},{4,5},{5,4},{6,7},{7,6},{8,9},{9,8},{10,11... | collective-permute-start | bytes 344072 | tf_op jit(solution)/shard_map/ppermute | solution.py:1068
  224.2 6.1 %collective-permute-start.23 = (bf16[448,128]{1,0:T(8,128)(2,1)S(1)}, bf16[448,128]{1,0:T(8,128)(2,1)S(1)}, u32[]{:S(2)}, u32[]{:S(2)}) collective-permute-start(bf16[448,128]{1,0:T(8,128)(2,1)S(1)} %get-tuple-element.271), channel_id=1, source_target_pairs={{0,3},{1,2},{2,1},{3,0},{4,7},{5,6},{6,5},{7,4},{8,11},{9,10},{10,... | collective-permute-start | bytes 344072 | tf_op jit(solution)/shard_map/ppermute | solution.py:1068

commit v5 on v4

--- a/solution.py
+++ b/solution.py
@@ -261,7 +261,7 @@
         return sum(pair.astype(jnp.int32) for pair in pairs)
 
     here, later = count(range(first, end)), count(range(end, parts))
-    return (here == 2 * (end - first)) & (here + later <= 6)
+    return (here == 2 * (end - first)) & (here + later <= 8)
 
 
 def side_rows(side, heads, tok):

time: 232 us -> 237 us (1.022)
  the two profiles are of different devices: /device:TPU:21 before, /device:TPU:27 now
where the time goes in v5:
time: 237 us; the launch traced here: 240 us
  Pallas kernels  191 us (81%)
  starting transfers between devices  26.1 us (11%)
  waiting for transfers between devices  17.2 us (7%)
  local copies, waits for them, and re-layouts  4.4 us (2%)
    pallas_call x1, Pallas kernels, finish(): pl.pallas_call(functools.partial(finish_kernel, tok, heads, groups, done)...  159 us
    pallas_call x1, Pallas kernels, late_decode(): pl.pallas_call(functools.partial(late_kernel, own, steps, heads, groups,...  8.75 us
    pallas_call x2, Pallas kernels, stage(): pl.pallas_call(functools.partial(stage_kernel, tok, rows // (2 * tok), gr...  7.32 us
    ppermute x4, starting transfers between devices, split_heads(): held_k[-d] = lax.ppermute(held_k[1 - d], 'seq', up)  7.2 us
  transfers between devices with their start and end apart: 24, of which 12 were waited for; matrix products, arithmetic and copies ran while one was open for 0% of the time, Pallas kernels for 76%

profile of v5, /device:TPU:27, one launch (start us, length us, event | category | flops | bytes accessed | tf_op | source)
XLA Modules:
  0.0 239.6 jit_solution(1742364840091046132)
XLA Ops:
  0.7 0.9 copy-done.4
  1.6 0.9 copy-done.5
  2.6 0.1 prepare.1
  2.7 0.7 collective-permute-start
  3.6 1.1 collective-permute-done.theirs
  4.6 1.5 copy-done.1
  6.1 0.1 join.1
  6.3 0.4 collective-permute-start.5
  6.7 1.2 collective-permute-start.3
  8.0 0.2 collective-permute-start.4
  8.2 1.2 collective-permute-start.1
  9.4 0.2 collective-permute-start.2
  9.7 4.3 %open.1 = (bf16[2,3584,128]{2,1,0:T(8,128)(2,1)S(1)}, f32[2,3584,128]{2,1,0:T(8,128)S(1)}, f32[2,3584,128]{2,1,0:T(8,128)S(1)}) custom-call(s32[15]{0:T(128)S(1)} %stack.60.meta, s32[3]{0:T(128)S(1)} %copy-done.9, bf16[256,3584]{1,0:T(8,128)(2,1)S(1)} %copy-done.2, bf16[256,1792]{1,0:T(8,128)(2,1)S(1)} %collective-permute-done.5.q_near, ...), custom_call_target="tpu_custom_call" | custom-call | flops 1024 | bytes 1024 | tf_op jit(solution)/shard_map/open/pallas_call | solution.py:301
  14.0 0.5 collective-permute-done.3.refs_0_.refs_2_
  14.5 0.9 collective-permute-done.4.refs_2_.refs_4_
  15.4 0.3 collective-permute-start.8
  15.7 1.1 collective-permute-start.9
  16.9 3.0 %requests.1 = (f32[2,448,128]{2,1,0:T(8,128)S(1)}, f32[2,448,128]{2,1,0:T(8,128)S(1)}, bf16[2,448,128]{2,1,0:T(8,128)(2,1)S(1)}, bf16[64,256]{1,0:T(8,128)(2,1)S...) custom-call(s32[15]{0:T(128)S(1)} %stack.60.meta, bf16[64,4,3584]{2,1,0:T(4,128)(2,1)S(1)} %copy-done.3, ...), custom_call_target="tpu_custom_call" | custom-call | flops 1024 | bytes 1024 | tf_op jit(solution)/shard_map/requests/pallas_call | solution.py:574
  19.9 0.2 collective-permute-done.1.refs_1_.refs_3_
  20.1 0.9 collective-permute-done.2.refs_3_.refs_5_
  21.0 0.3 collective-permute-start.6
  21.3 1.1 collective-permute-start.7
  22.5 5.6 %stage1.1 = (f32[2,3584,128]{2,1,0:T(8,128)S(1)}, f32[2,3584,128]{2,1,0:T(8,128)S(1)}) custom-call(s32[15]{0:T(128)S(1)} %stack.60.meta, s32[3]{0:T(128)S(1)} %copy-done.9, bf16[2,3584,128]{2,1,0:T(8,128)(2,1)S(1)} %get-tuple-element.254.qs, f32[2,3584,128]{2,1,0:T(8,128)S(1)} %get-tuple-element.166.total_in, ...), custom_call_target="tpu_custom_call", output_to_operand_aliasing={{0}: (3, {}), {1}: (4, {})} | custom-call | flops 1024 | bytes 1024 | tf_op jit(solution)/shard_map/stage1/pallas_call | solution.py:362
  28.2 5.6 %collective-permute-start.12 = (bf16[256,512]{1,0:T(8,128)(2,1)S(1)}, bf16[256,512]{1,0:T(8,128)(2,1)S(1)}, u32[]{:S(2)}, u32[]{:S(2)}) collective-permute-start(bf16[256,512]{1,0:T(8,128)(2,1)S(1)} %collective-permute-done.8.refs_0_.refs_6_), channel_id=1, source_target_pairs={{0,8},{2,10},{8,16},{10,18},{16,24},{18,26},{24,28},{26,30},{28,20... | collective-permute-start | bytes 786440 | tf_op jit(solution)/shard_map/ppermute | solution.py:1019
  33.8 1.5 collective-permute-start.10
  35.3 1.7 stage3.1
  37.0 0.1 collective-permute-done.12.refs_10_
  37.1 1.9 collective-permute-done.13.refs_12_
  39.0 3.4 %collective-permute-done.10.refs_11_ = bf16[256,512]{1,0:T(8,128)(2,1)S(1)} collective-permute-done((bf16[256,512]{1,0:T(8,128)(2,1)S(1)}, bf16[256,512]{1,0:T(8,128)(2,1)S(1)}, u32[]{:S(2)}, u32[]{:S(2)}) %collective-permute-start.10) | collective-permute-done | bytes 262176 | tf_op jit(solution)/shard_map/ppermute | solution.py:1023
  42.4 1.9 collective-permute-done.11.refs_13_
  44.3 0.7 take.1
  45.0 3.8 %collective-permute-start.14 = (bf16[448,1792]{1,0:T(8,128)(2,1)S(1)}, bf16[448,1792]{1,0:T(8,128)(2,1)S(1)}, u32[]{:S(2)}, u32[]{:S(2)}) collective-permute-start(bf16[448,1792]{1,0:T(8,128)(2,1)S(1)} %take.1), channel_id=1, source_target_pairs={{0,2},{2,0},{4,6},{6,4},{8,10},{10,8},{12,14},{14,12},{16,18},{18,... | collective-permute-start | bytes 4816904 | tf_op jit(solution)/shard_map/ppermute | solution.py:1047
  48.9 1.4 collective-permute-start.15
  50.3 4.0 %early_decode.1 = (f32[2,448,128]{2,1,0:T(8,128)S(1)}, f32[2,448,128]{2,1,0:T(8,128)S(1)}) custom-call(f32[2,448,128]{2,1,0:T(8,128)S(1)} %get-tuple-element.218.total_in, f32[2,448,128]{2,1,0:T(8,128)S(1)} %get-tuple-element.219.acc_in, bf16[2,448,128]{2,1,0:T(8,128)(2,1)S(1)} %get-tuple-element.245.query, ...), custom_call_target="tpu_custom_call", output_to_operand_aliasing={{0}: (0, {}), {1}: (1, {})} | custom-call | flops 1024 | bytes 1024 | tf_op jit(solution)/shard_map/early_decode/pallas_call | solution.py:614
  54.3 2.4 %collective-permute-done.16.refs_14_ = bf16[256,512]{1,0:T(8,128)(2,1)S(1)} collective-permute-done((bf16[256,512]{1,0:T(8,128)(2,1)S(1)}, bf16[256,512]{1,0:T(8,128)(2,1)S(1)}, u32[]{:S(2)}, u32[]{:S(2)}) %collective-permute-start.16) | collective-permute-done | bytes 262176 | tf_op jit(solution)/shard_map/ppermute | solution.py:1019
  56.7 8.7 %late_decode.1.refs_0_ = bf16[64,1792]{1,0:T(8,128)(2,1)S(1)} custom-call(s32[15]{0:T(128)S(1)} %stack.60.meta, f32[2,448,128]{2,1,0:T(8,128)S(1)} %get-tuple-element.243.total, f32[2,448,128]{2,1,0:T(8,128)S(1)} %get-tuple-element.244.acc, bf16[2,448,128]{2,1,0:T(8,128)(2,1)S(1)} %get-tuple-element.245.query, bf16[64,256]{1,0:T(8,128)(2,1)S(1)} %get-tuple-element.246.newk, ...), custom_call_target="tpu_custom_call" | custom-call | flops 469762048 | bytes 57344 | tf_op jit(solution)/shard_map/late_decode/pallas_call | solution.py:680
  65.5 1.0 collective-permute-start.17
  66.4 1.4 collective-permute-start.18
  67.8 158.8 %finish.1 = (bf16[256,1792]{1,0:T(8,128)(2,1)S(1)}, bf16[256,3584]{1,0:T(8,128)(2,1)}) custom-call(s32[15]{0:T(128)S(1)} %stack.60.meta, s32[3]{0:T(128)S(1)} %copy-done.9, bf16[2,3584,128]{2,1,0:T(8,128)(2,1)S(1)} %get-tuple-element.254.qs, f32[2,3584,128]{2,1,0:T(8,128)S(1)} %get-tuple-element.255.total, f32[2,3584,128]{2,1,0:T(8,128)S(1)} %get-tuple-element.256.acc, ...), custom_call_target="tpu_custom_call" | custom-call | flops 1879048192 | bytes 1835008 | tf_op jit(solution)/shard_map/finish/pallas_call | solution.py:473
  226.7 2.1 collective-permute-start.21
  228.7 2.4 %project.1 = (f32[448,128]{1,0:T(8,128)S(1)}, bf16[448,128]{1,0:T(8,128)(2,1)S(1)}, bf16[448,128]{1,0:T(8,128)(2,1)S(1)}, bf16[448,128]{1,0:T(8,128)(2,1)S(1)}) custom-call(s32[15]{0:T(128)S(1)} %stack.60.meta, bf16[64,1792]{1,0:T(8,128)(2,1)S(1)} %late_decode.1.refs_0_, bf16[64,1792]{1,0:T(8,128)(2,1)S(1)} %collective-permute-done.17.refs_1_, ...), custom_call_target="tpu_custom_call" | custom-call | flops 822083584 | bytes 3211264 | tf_op jit(solution)/shard_map/project/pallas_call | solution.py:901
  231.3 0.3 collective-permute-start.22
  231.6 1.8 collective-permute-start.23
  233.4 1.5 settle.1
  234.9 0.7 collective-permute-done.22
  235.6 3.0 %collective-permute-done.23 = bf16[448,128]{1,0:T(8,128)(2,1)S(1)} collective-permute-done((bf16[448,128]{1,0:T(8,128)(2,1)S(1)}, bf16[448,128]{1,0:T(8,128)(2,1)S(1)}, u32[]{:S(2)}, u32[]{:S(2)}) %collective-permute-start.23) | collective-permute-done | bytes 114720 | tf_op jit(solution)/shard_map/ppermute | solution.py:1068
  238.7 0.1 copy.20
  238.8 0.8 copy.22
  (37 shorter events, 0.5 us)
Async XLA Ops:
  0.6 9.0 %copy-start.9 = (s32[3]{0:T(128)S(1)}, s32[3]{0:T(128)}, u32[]{:S(2)}) copy-start(s32[3]{0:T(128)} %lengths.7) | copy-start | bytes 40
  0.6 1.0 copy-start.4
  1.6 0.9 copy-start.5
  2.5 14.3 %copy-start.7 = (bf16[64,4,512]{2,1,0:T(4,128)(2,1)S(1)}, bf16[64,4,512]{2,1,0:T(4,128)(2,1)}, u32[]{:S(2)}) copy-start(bf16[64,4,512]{2,1,0:T(4,128)(2,1)} %refs_2_.1) | copy-start | bytes 786436
  2.7 14.2 %copy-start.6 = (bf16[64,4,512]{2,1,0:T(4,128)(2,1)S(1)}, bf16[64,4,512]{2,1,0:T(4,128)(2,1)}, u32[]{:S(2)}) copy-start(bf16[64,4,512]{2,1,0:T(4,128)(2,1)} %refs_1_.1) | copy-start | bytes 786436
  2.7 14.2 %copy-start.8 = (s32[64,32]{0,1:T(8,128)S(1)}, s32[64,32]{0,1:T(8,128)}, u32[]{:S(2)}) copy-start(s32[64,32]{0,1:T(8,128)} %param.16) | copy-start | bytes 24580
  2.7 1.9 collective-permute-start
  4.6 1.5 copy-start.1
  6.1 3.5 %copy-start.2 = (bf16[256,3584]{1,0:T(8,128)(2,1)S(1)}, bf16[256,3584]{1,0:T(8,128)(2,1)}, u32[]{:S(2)}) copy-start(bf16[256,3584]{1,0:T(8,128)(2,1)} %q.3) | copy-start | bytes 5505028
  6.1 10.7 %copy-start.3 = (bf16[64,4,3584]{2,1,0:T(4,128)(2,1)S(1)}, bf16[64,4,3584]{2,1,0:T(4,128)(2,1)}, u32[]{:S(2)}) copy-start(bf16[64,4,3584]{2,1,0:T(4,128)(2,1)} %refs_0_.1) | copy-start | bytes 5505028
  6.3 3.4 %collective-permute-start.5 = (bf16[256,1792]{1,0:T(8,128)(2,1)S(1)}, bf16[256,1792]{1,0:T(8,128)(2,1)S(1)}, u32[]{:S(2)}, u32[]{:S(2)}) collective-permute-start(bf16[256,1792]{1,0:T(8,128)(2,1)S(1)} %get-tuple-element.144), channel_id=1, source_target_pairs={{0,2},{2,0},{4,6},{6,4},{8,10},{10,8},{12,14},{14,12},{16,18},{18,... | collective-permute-start | bytes 2752520 | tf_op jit(solution)/shard_map/ppermute | solution.py:1014
  6.7 7.8 %collective-permute-start.3 = (bf16[256,512]{1,0:T(8,128)(2,1)S(1)}, bf16[256,512]{1,0:T(8,128)(2,1)S(1)}, u32[]{:S(2)}, u32[]{:S(2)}) collective-permute-start(bf16[256,512]{1,0:T(8,128)(2,1)S(1)} %get-tuple-element.143.upper.refs_0_), channel_id=1, source_target_pairs={{0,8},{2,10},{8,16},{10,18},{16,24},{18,26},{24,28},{26,30},{28,20... | collective-permute-start | bytes 786440 | tf_op jit(solution)/shard_map/ppermute | solution.py:1019
  8.0 7.4 %collective-permute-start.4 = (bf16[256,512]{1,0:T(8,128)(2,1)S(1)}, bf16[256,512]{1,0:T(8,128)(2,1)S(1)}, u32[]{:S(2)}, u32[]{:S(2)}) collective-permute-start(bf16[256,512]{1,0:T(8,128)(2,1)S(1)} %get-tuple-element.143.upper.refs_0_), channel_id=1, source_target_pairs={{0,4},{2,6},{8,0},{10,2},{16,8},{18,10},{24,16},{26,18},{28,24},{3... | collective-permute-start | bytes 786440 | tf_op jit(solution)/shard_map/ppermute | solution.py:1022
  8.2 11.9 %collective-permute-start.1 = (bf16[256,512]{1,0:T(8,128)(2,1)S(1)}, bf16[256,512]{1,0:T(8,128)(2,1)S(1)}, u32[]{:S(2)}, u32[]{:S(2)}) collective-permute-start(bf16[256,512]{1,0:T(8,128)(2,1)S(1)} %get-tuple-element.142.lower.refs_1_), channel_id=1, source_target_pairs={{0,8},{2,10},{8,16},{10,18},{16,24},{18,26},{24,28},{26,30},{28,20... | collective-permute-start | bytes 786440 | tf_op jit(solution)/shard_map/ppermute | solution.py:1023
  9.4 11.6 %collective-permute-start.2 = (bf16[256,512]{1,0:T(8,128)(2,1)S(1)}, bf16[256,512]{1,0:T(8,128)(2,1)S(1)}, u32[]{:S(2)}, u32[]{:S(2)}) collective-permute-start(bf16[256,512]{1,0:T(8,128)(2,1)S(1)} %get-tuple-element.142.lower.refs_1_), channel_id=1, source_target_pairs={{0,4},{2,6},{8,0},{10,2},{16,8},{18,10},{24,16},{26,18},{28,24},{3... | collective-permute-start | bytes 786440 | tf_op jit(solution)/shard_map/ppermute | solution.py:1020
  15.4 12.7 %collective-permute-start.8 = (bf16[256,512]{1,0:T(8,128)(2,1)S(1)}, bf16[256,512]{1,0:T(8,128)(2,1)S(1)}, u32[]{:S(2)}, u32[]{:S(2)}) collective-permute-start(bf16[256,512]{1,0:T(8,128)(2,1)S(1)} %collective-permute-done.3.refs_0_.refs_2_), channel_id=1, source_target_pairs={{0,8},{2,10},{8,16},{10,18},{16,24},{18,26},{24,28},{26,30},{28,20... | collective-permute-start | bytes 786440 | tf_op jit(solution)/shard_map/ppermute | solution.py:1019
  15.7 12.4 %collective-permute-start.9 = (bf16[256,512]{1,0:T(8,128)(2,1)S(1)}, bf16[256,512]{1,0:T(8,128)(2,1)S(1)}, u32[]{:S(2)}, u32[]{:S(2)}) collective-permute-start(bf16[256,512]{1,0:T(8,128)(2,1)S(1)} %collective-permute-done.4.refs_2_.refs_4_), channel_id=1, source_target_pairs={{0,4},{2,6},{8,0},{10,2},{16,8},{18,10},{24,16},{26,18},{28,24},{3... | collective-permute-start | bytes 786440 | tf_op jit(solution)/shard_map/ppermute | solution.py:1022
  21.0 12.7 %collective-permute-start.6 = (bf16[256,512]{1,0:T(8,128)(2,1)S(1)}, bf16[256,512]{1,0:T(8,128)(2,1)S(1)}, u32[]{:S(2)}, u32[]{:S(2)}) collective-permute-start(bf16[256,512]{1,0:T(8,128)(2,1)S(1)} %collective-permute-done.1.refs_1_.refs_3_), channel_id=1, source_target_pairs={{0,8},{2,10},{8,16},{10,18},{16,24},{18,26},{24,28},{26,30},{28,20... | collective-permute-start | bytes 786440 | tf_op jit(solution)/shard_map/ppermute | solution.py:1023
  21.3 12.4 %collective-permute-start.7 = (bf16[256,512]{1,0:T(8,128)(2,1)S(1)}, bf16[256,512]{1,0:T(8,128)(2,1)S(1)}, u32[]{:S(2)}, u32[]{:S(2)}) collective-permute-start(bf16[256,512]{1,0:T(8,128)(2,1)S(1)} %collective-permute-done.2.refs_3_.refs_5_), channel_id=1, source_target_pairs={{0,4},{2,6},{8,0},{10,2},{16,8},{18,10},{24,16},{26,18},{28,24},{3... | collective-permute-start | bytes 786440 | tf_op jit(solution)/shard_map/ppermute | solution.py:1020
  28.2 16.2 %copy-start = (bf16[3584,448]{0,1:T(8,128)(2,1)S(1)}, bf16[3584,448]{0,1:T(8,128)(2,1)}, u32[]{:S(2)}) copy-start(bf16[3584,448]{0,1:T(8,128)(2,1)} %param.17) | copy-start | bytes 9633796
  28.2 8.9 %collective-permute-start.12 = (bf16[256,512]{1,0:T(8,128)(2,1)S(1)}, bf16[256,512]{1,0:T(8,128)(2,1)S(1)}, u32[]{:S(2)}, u32[]{:S(2)}) collective-permute-start(bf16[256,512]{1,0:T(8,128)(2,1)S(1)} %collective-permute-done.8.refs_0_.refs_6_), channel_id=1, source_target_pairs={{0,8},{2,10},{8,16},{10,18},{16,24},{18,26},{24,28},{26,30},{28,20... | collective-permute-start | bytes 786440 | tf_op jit(solution)/shard_map/ppermute | solution.py:1019
  33.7 5.2 %collective-permute-start.13 = (bf16[256,512]{1,0:T(8,128)(2,1)S(1)}, bf16[256,512]{1,0:T(8,128)(2,1)S(1)}, u32[]{:S(2)}, u32[]{:S(2)}) collective-permute-start(bf16[256,512]{1,0:T(8,128)(2,1)S(1)} %collective-permute-done.9.refs_2_.refs_8_), channel_id=1, source_target_pairs={{0,4},{2,6},{8,0},{10,2},{16,8},{18,10},{24,16},{26,18},{28,24},{3... | collective-permute-start | bytes 786440 | tf_op jit(solution)/shard_map/ppermute | solution.py:1022
  33.8 8.7 %collective-permute-start.10 = (bf16[256,512]{1,0:T(8,128)(2,1)S(1)}, bf16[256,512]{1,0:T(8,128)(2,1)S(1)}, u32[]{:S(2)}, u32[]{:S(2)}) collective-permute-start(bf16[256,512]{1,0:T(8,128)(2,1)S(1)} %collective-permute-done.6.refs_1_.refs_7_), channel_id=1, source_target_pairs={{0,8},{2,10},{8,16},{10,18},{16,24},{18,26},{24,28},{26,30},{28,20... | collective-permute-start | bytes 786440 | tf_op jit(solution)/shard_map/ppermute | solution.py:1023
  35.2 9.1 %collective-permute-start.11 = (bf16[256,512]{1,0:T(8,128)(2,1)S(1)}, bf16[256,512]{1,0:T(8,128)(2,1)S(1)}, u32[]{:S(2)}, u32[]{:S(2)}) collective-permute-start(bf16[256,512]{1,0:T(8,128)(2,1)S(1)} %collective-permute-done.7.refs_3_.refs_9_), channel_id=1, source_target_pairs={{0,4},{2,6},{8,0},{10,2},{16,8},{18,10},{24,16},{26,18},{28,24},{3... | collective-permute-start | bytes 786440 | tf_op jit(solution)/shard_map/ppermute | solution.py:1020
  45.0 11.7 %collective-permute-start.14 = (bf16[448,1792]{1,0:T(8,128)(2,1)S(1)}, bf16[448,1792]{1,0:T(8,128)(2,1)S(1)}, u32[]{:S(2)}, u32[]{:S(2)}) collective-permute-start(bf16[448,1792]{1,0:T(8,128)(2,1)S(1)} %take.1), channel_id=1, source_target_pairs={{0,2},{2,0},{4,6},{6,4},{8,10},{10,8},{12,14},{14,12},{16,18},{18,... | collective-permute-start | bytes 4816904 | tf_op jit(solution)/shard_map/ppermute | solution.py:1047
  48.8 7.9 %collective-permute-start.16 = (bf16[256,512]{1,0:T(8,128)(2,1)S(1)}, bf16[256,512]{1,0:T(8,128)(2,1)S(1)}, u32[]{:S(2)}, u32[]{:S(2)}) collective-permute-start(bf16[256,512]{1,0:T(8,128)(2,1)S(1)} %collective-permute-done.12.refs_10_), channel_id=1, source_target_pairs={{0,8},{2,10},{8,16},{10,18},{16,24},{18,26},{24,28},{26,30},{28,20... | collective-permute-start | bytes 786440 | tf_op jit(solution)/shard_map/ppermute | solution.py:1019
  48.9 7.8 %collective-permute-start.15 = (bf16[256,512]{1,0:T(8,128)(2,1)S(1)}, bf16[256,512]{1,0:T(8,128)(2,1)S(1)}, u32[]{:S(2)}, u32[]{:S(2)}) collective-permute-start(bf16[256,512]{1,0:T(8,128)(2,1)S(1)} %collective-permute-done.11.refs_13_), channel_id=1, source_target_pairs={{0,4},{2,6},{8,0},{10,2},{16,8},{18,10},{24,16},{26,18},{28,24},{3... | collective-permute-start | bytes 786440 | tf_op jit(solution)/shard_map/ppermute | solution.py:1020
  65.5 161.2 %collective-permute-start.17 = (bf16[64,1792]{1,0:T(8,128)(2,1)S(1)}, bf16[64,1792]{1,0:T(8,128)(2,1)S(1)}, u32[]{:S(2)}, u32[]{:S(2)}) collective-permute-start(bf16[64,1792]{1,0:T(8,128)(2,1)S(1)} %late_decode.1.refs_0_), channel_id=1, source_target_pairs={{0,8},{2,10},{4,12},{6,14},{8,16},{10,18},{12,20},{14,22},{16,24},... | collective-permute-start | bytes 688136 | tf_op jit(solution)/shard_map/ppermute | solution.py:1055
  66.4 160.2 %collective-permute-start.18 = (bf16[64,1792]{1,0:T(8,128)(2,1)S(1)}, bf16[64,1792]{1,0:T(8,128)(2,1)S(1)}, u32[]{:S(2)}, u32[]{:S(2)}) collective-permute-start(bf16[64,1792]{1,0:T(8,128)(2,1)S(1)} %late_decode.1.refs_0_), channel_id=1, source_target_pairs={{0,16},{2,18},{4,20},{6,22},{8,24},{10,26},{12,28},{14,30},{16,0},... | collective-permute-start | bytes 688136 | tf_op jit(solution)/shard_map/ppermute | solution.py:1055
  67.8 158.8 %collective-permute-start.19 = (bf16[64,1792]{1,0:T(8,128)(2,1)S(1)}, bf16[64,1792]{1,0:T(8,128)(2,1)S(1)}, u32[]{:S(2)}, u32[]{:S(2)}) collective-permute-start(bf16[64,1792]{1,0:T(8,128)(2,1)S(1)} %late_decode.1.refs_0_), channel_id=1, source_target_pairs={{0,24},{2,26},{4,28},{6,30},{8,0},{10,2},{12,4},{14,6},{16,8},{18,... | collective-permute-start | bytes 688136 | tf_op jit(solution)/shard_map/ppermute | solution.py:1055
  226.7 6.7 %collective-permute-start.21 = (bf16[256,1792]{1,0:T(8,128)(2,1)S(1)}, bf16[256,1792]{1,0:T(8,128)(2,1)S(1)}, u32[]{:S(2)}, u32[]{:S(2)}) collective-permute-start(bf16[256,1792]{1,0:T(8,128)(2,1)S(1)} %get-tuple-element.265), channel_id=1, source_target_pairs={{0,2},{2,0},{4,6},{6,4},{8,10},{10,8},{12,14},{14,12},{16,18},{18,... | collective-permute-start | bytes 2752520 | tf_op jit(solution)/shard_map/ppermute | solution.py:1059
  231.2 3.7 %collective-permute-start.20 = (bf16[448,128]{1,0:T(8,128)(2,1)S(1)}, bf16[448,128]{1,0:T(8,128)(2,1)S(1)}, u32[]{:S(2)}, u32[]{:S(2)}) collective-permute-start(bf16[448,128]{1,0:T(8,128)(2,1)S(1)} %get-tuple-element.264), channel_id=1, source_target_pairs={{0,2},{1,3},{2,0},{3,1},{4,6},{5,7},{6,4},{7,5},{8,10},{9,11},{10,... | collective-permute-start | bytes 344072 | tf_op jit(solution)/shard_map/ppermute | solution.py:1068
  231.3 4.3 %collective-permute-start.22 = (bf16[448,128]{1,0:T(8,128)(2,1)S(1)}, bf16[448,128]{1,0:T(8,128)(2,1)S(1)}, u32[]{:S(2)}, u32[]{:S(2)}) collective-permute-start(bf16[448,128]{1,0:T(8,128)(2,1)S(1)} %get-tuple-element.270), channel_id=1, source_target_pairs={{0,1},{1,0},{2,3},{3,2},{4,5},{5,4},{6,7},{7,6},{8,9},{9,8},{10,11... | collective-permute-start | bytes 344072 | tf_op jit(solution)/shard_map/ppermute | solution.py:1068
  231.6 7.1 %collective-permute-start.23 = (bf16[448,128]{1,0:T(8,128)(2,1)S(1)}, bf16[448,128]{1,0:T(8,128)(2,1)S(1)}, u32[]{:S(2)}, u32[]{:S(2)}) collective-permute-start(bf16[448,128]{1,0:T(8,128)(2,1)S(1)} %get-tuple-element.271), channel_id=1, source_target_pairs={{0,3},{1,2},{2,1},{3,0},{4,7},{5,6},{6,5},{7,4},{8,11},{9,10},{10,... | collective-permute-start | bytes 344072 | tf_op jit(solution)/shard_map/ppermute | solution.py:1068
